TPU v7x, 32 devices: a whole 2x2x4 slice. The times are simulated.
32 devices in a mesh: dp: 8 (over y, x, core), mp: 4 (over z).
Axes of the slice: x: 2, y: 2, z: 4, core: 2. Of those that a mesh axis runs over, the one named last changes fastest.
Arguments:
- inputs: bfloat16 [64, 128, 512], P('dp'), may hold values from -6 to 6
- encoder: bfloat16 [64, 512, 512], P('dp', 'mp'), may hold values from -6 to 6
- cotangent: bfloat16 [64, 128, 512], P('dp'), may hold values from -6 to 6
- target_segments: int32 [64, 128], P('dp'), may hold values from 0 to 2, never falling along the last dimension, each value on 1 to 64 neighbouring positions
- encoder_segments: int32 [64, 512], P('dp'), may hold values from 0 to 2, never falling along the last dimension, each value on 1 to 256 neighbouring positions
- query_weight: float32 [2, 512, 512], P(None, 'dp', 'mp'), may hold values from -0.0625 to 0.0625
- query_first: float32 [2, 512, 512], P(None, 'dp', 'mp'), may hold values from -640 to 640
- query_second: float32 [2, 512, 512], P(None, 'dp', 'mp'), may hold values from 32768 to 163840
- keyval_weight: float32 [2, 2, 512, 512], P(None, None, 'dp', 'mp'), may hold values from -0.25 to 0.25
- keyval_first: float32 [2, 2, 512, 512], P(None, None, 'dp', 'mp'), may hold values from -128 to 128
- keyval_second: float32 [2, 2, 512, 512], P(None, None, 'dp', 'mp'), may hold values from 1310.72 to 6553.6
- output_weight: float32 [2, 512, 512], P(None, 'mp', 'dp'), may hold values from -0.75 to 0.75
- output_first: float32 [2, 512, 512], P(None, 'mp', 'dp'), may hold values from -24 to 24
- output_second: float32 [2, 512, 512], P(None, 'mp', 'dp'), may hold values from 52.4288 to 262.144
- inner_weight: float32 [512, 2048], P('dp', 'mp'), may hold values from -0.25 to 0.25
- inner_first: float32 [512, 2048], P('dp', 'mp'), may hold values from -40 to 40
- inner_second: float32 [512, 2048], P('dp', 'mp'), may hold values from 163.84 to 819.2
- outer_weight: float32 [2048, 512], P('mp', 'dp'), may hold values from -0.1875 to 0.1875
- outer_first: float32 [2048, 512], P('mp', 'dp'), may hold values from -32 to 32
- outer_second: float32 [2048, 512], P('mp', 'dp'), may hold values from 122.88 to 573.44
- gains: float32 [3, 512], P(None, 'dp'), may hold values from 0.5 to 1.5
- gains_first: float32 [3, 512], P(None, 'dp'), may hold values from -256 to 256
- gains_second: float32 [3, 512], P(None, 'dp'), may hold values from 5242.88 to 26214.4
- bias_table: float32 [32, 8], P('dp', 'mp'), may hold values from -6 to 6
- table_first: float32 [32, 8], P('dp', 'mp'), may hold values from -448 to 448
- table_second: float32 [32, 8], P('dp', 'mp'), may hold values from 16384 to 81920
Outputs:
- outputs: bfloat16 [64, 128, 512], P('dp')
- input_grad: bfloat16 [64, 128, 512], P('dp')
- new_query_first: float32 [2, 512, 512], P(None, 'dp', 'mp')
- new_query_second: float32 [2, 512, 512], P(None, 'dp', 'mp')
- new_query_weight: float32 [2, 512, 512], P(None, 'dp', 'mp')
- new_keyval_first: float32 [2, 2, 512, 512], P(None, None, 'dp', 'mp')
- new_keyval_second: float32 [2, 2, 512, 512], P(None, None, 'dp', 'mp')
- new_keyval_weight: float32 [2, 2, 512, 512], P(None, None, 'dp', 'mp')
- new_output_first: float32 [2, 512, 512], P(None, 'mp', 'dp')
- new_output_second: float32 [2, 512, 512], P(None, 'mp', 'dp')
- new_output_weight: float32 [2, 512, 512], P(None, 'mp', 'dp')
- new_inner_first: float32 [512, 2048], P('dp', 'mp')
- new_inner_second: float32 [512, 2048], P('dp', 'mp')
- new_inner_weight: float32 [512, 2048], P('dp', 'mp')
- new_outer_first: float32 [2048, 512], P('mp', 'dp')
- new_outer_second: float32 [2048, 512], P('mp', 'dp')
- new_outer_weight: float32 [2048, 512], P('mp', 'dp')
- new_gains_first: float32 [3, 512], P(None, 'dp')
- new_gains_second: float32 [3, 512], P(None, 'dp')
- new_gains: float32 [3, 512], P(None, 'dp')
- new_table_first: float32 [32, 8], P('dp', 'mp')
- new_table_second: float32 [32, 8], P('dp', 'mp')
- new_table: float32 [32, 8], P('dp', 'mp')
Inputs may be any that keep to these rules, and one draw needn't show every extreme that they name: `target_segments`: along each row the numbers never fall and every number from 0 to 2 occurs; target tokens of example s attend to the encoder tokens of example s of the same row. `encoder_segments`: along each row the numbers never fall and every number from 0 to 2 occurs.
All inputs are finite; a program needn't handle non-finite values.
Results may differ from a plain program's by a relative error of at most 0.02.
The roundings to bfloat16 on the way count: a program that leaves them out, or rounds other values in their place, can miss the bound.
Values may be sent and summed in bfloat16 or wider, within the bound.
No kernel may reach another device: no remote copies, remote signals or barrier semaphores. Data moves between devices by JAX's collectives and lax.ppermute only.
A program may use at most 128 MiB of HBM per device.

v0:
```python
import math

import jax
import jax.numpy as jnp
from jax import lax
from jax.sharding import PartitionSpec as P

D = 512
HEAD_DIM = 64
FF = 2048
NB = 32
HD = 512
STEP = 10


norm_eps = 1e-06
beta_first = 0.9
beta_second = 0.95
adam_eps = 1e-08
decay_weight = 0.1
rate_factor = 0.6
masked_value = -1000000000.0
bucket_edges = tuple((math.ceil(16 * 8 ** (number / 16)) for number in range(1, 16)))
step_decays = (decay_weight, decay_weight, decay_weight, decay_weight, decay_weight, 0.0, 0.0)


def bucket_onehot(length):
    places = jnp.arange(length, dtype=jnp.int32)
    distance = jnp.maximum(places[:, None] - places[None, :], 0)
    bucket = jnp.minimum(distance, 16)
    for edge_value in bucket_edges:
        bucket = bucket + (distance >= edge_value).astype(jnp.int32)
    return (bucket[:, :, None] == jnp.arange(NB, dtype=jnp.int32)[None, None, :]).astype(
        jnp.float32
    )


def root_norm(values, gain_vector):
    return (
        values
        * lax.rsqrt(jnp.mean(values * values, axis=-1, keepdims=True) + norm_eps)
        * gain_vector
    )


def split_rows(tensor, per_block):
    return tensor.reshape((tensor.shape[0] // per_block, per_block) + tensor.shape[1:])


def join_rows(tensor):
    return tensor.reshape((-1,) + tensor.shape[2:])


def soft_scores(queries, key_rows, score_bias, allowed):
    scores = (
        jnp.einsum("bqhe,bkhe->bhqk", queries, key_rows, preferred_element_type=jnp.float32)
        + score_bias
    )
    return jnp.where(allowed, scores, masked_value)


def attend_forward(queries, key_rows, values, score_bias, allowed):
    logits = soft_scores(queries, key_rows, score_bias, allowed)
    row_peak = jnp.max(logits, axis=-1, keepdims=True)
    exp_terms = jnp.exp(logits - row_peak)
    row_total = jnp.sum(exp_terms, axis=-1, keepdims=True)
    attn_probs = (exp_terms / row_total).astype(jnp.bfloat16)
    attn_mixed = jnp.einsum(
        "bhqk,bkhe->bqhe", attn_probs, values, preferred_element_type=jnp.float32
    )
    return (attn_mixed.astype(jnp.bfloat16), row_peak + jnp.log(row_total))


def attend_backward(queries, key_rows, values, score_bias, allowed, log_total, grad_mixed):
    attn_probs = jnp.exp(soft_scores(queries, key_rows, score_bias, allowed) - log_total)
    grad_probs = jnp.einsum(
        "bqhe,bkhe->bhqk", grad_mixed, values, preferred_element_type=jnp.float32
    )
    grad_values = jnp.einsum(
        "bhqk,bqhe->bkhe",
        attn_probs.astype(jnp.bfloat16),
        grad_mixed,
        preferred_element_type=jnp.float32,
    )
    grad_scores = attn_probs * (
        grad_probs - jnp.sum(grad_probs * attn_probs, axis=-1, keepdims=True)
    )
    low_scores = grad_scores.astype(jnp.bfloat16)
    grad_queries = jnp.einsum(
        "bhqk,bkhe->bqhe", low_scores, key_rows, preferred_element_type=jnp.float32
    )
    grad_keys = jnp.einsum(
        "bhqk,bqhe->bkhe", low_scores, queries, preferred_element_type=jnp.float32
    )
    return (
        grad_queries.astype(jnp.bfloat16),
        grad_keys.astype(jnp.bfloat16),
        grad_values.astype(jnp.bfloat16),
        jnp.sum(grad_scores, axis=0),
    )


def add_heads(partial_value):
    return lax.psum(partial_value, "mp")


def add_head_grads(partial_value):
    return lax.psum(partial_value, "mp")


def adam_step(weight, first, second, grad, rate, decay):
    new_first = beta_first * first + (1.0 - beta_first) * grad
    new_second = beta_second * second + (1.0 - beta_second) * grad * grad
    ratio = (
        new_first
        / (1.0 - beta_first**STEP)
        / (jnp.sqrt(new_second / (1.0 - beta_second**STEP)) + adam_eps)
    )
    return (new_first, new_second, weight - rate * (ratio + decay * weight))


def step_rates():
    return (
        rate_factor * (16 * D) ** (-0.5),
        rate_factor * D ** (-0.5),
        rate_factor * (HD // 8) ** (-0.5),
        rate_factor * D ** (-0.5),
        rate_factor * (FF // 2) ** (-0.5),
        rate_factor,
        rate_factor,
    )


def shards(
    inputs,
    encoder,
    cotangent,
    target_segments,
    encoder_segments,
    query_weight,
    query_first,
    query_second,
    keyval_weight,
    keyval_first,
    keyval_second,
    output_weight,
    output_first,
    output_second,
    inner_weight,
    inner_first,
    inner_second,
    outer_weight,
    outer_first,
    outer_second,
    gains,
    gains_first,
    gains_second,
    bias_table,
    table_first,
    table_second,
):
    seq_count, length, model_width = inputs.shape
    enc_length = encoder_segments.shape[1]
    row_count = seq_count * length
    per_block = min(seq_count, max(1, 512 // length))
    query_all, keyval_all, output_all, inner_all, outer_all, gain_all, table_all = (
        lax.all_gather(query_weight.astype(jnp.bfloat16), "dp", axis=1, tiled=True),
        lax.all_gather(keyval_weight.astype(jnp.bfloat16), "dp", axis=2, tiled=True),
        lax.all_gather(output_weight.astype(jnp.bfloat16), "dp", axis=2, tiled=True),
        lax.all_gather(inner_weight.astype(jnp.bfloat16), "dp", axis=0, tiled=True),
        lax.all_gather(outer_weight.astype(jnp.bfloat16), "dp", axis=1, tiled=True),
        lax.all_gather(gains.astype(jnp.bfloat16), "dp", axis=1, tiled=True),
        lax.all_gather(bias_table.astype(jnp.bfloat16), "dp", axis=0, tiled=True),
    )
    gain_low = gain_all.astype(jnp.float32)
    local_heads = table_all.shape[1]
    onehot = bucket_onehot(length)
    score_bias = jnp.einsum(
        "qkb,bh->hqk", onehot, table_all.astype(jnp.float32), precision=lax.Precision.HIGHEST
    )
    places = jnp.arange(length)
    causal = places[:, None] >= places[None, :]

    def heads_of(flat):
        return flat.reshape(seq_count, -1, local_heads, HEAD_DIM)

    def self_mask(segments):
        same_segment = segments[:, :, None] == segments[:, None, :]
        return (causal[None] & same_segment)[:, None]

    def cross_mask(segments, sources):
        return (segments[:, :, None] == sources[:, None, :])[:, None]

    resident = inputs.astype(jnp.float32).reshape(row_count, model_width)
    normed_one = root_norm(resident, gain_low[0]).astype(jnp.bfloat16)
    self_weights = jnp.concatenate((query_all[0][None], keyval_all[0]), axis=0)
    projected = jnp.einsum(
        "td,kdc->ktc", normed_one, self_weights, preferred_element_type=jnp.float32
    ).astype(jnp.bfloat16)
    self_q = heads_of(projected[0])
    self_k = heads_of(projected[1])
    self_v = heads_of(projected[2])

    def self_forward(queries, key_rows, values, segments):
        return attend_forward(queries, key_rows, values, score_bias, self_mask(segments))

    self_mixed, self_total = lax.map(
        lambda pieces: self_forward(*pieces),
        (
            split_rows(self_q, per_block),
            split_rows(self_k, per_block),
            split_rows(self_v, per_block),
            split_rows(target_segments, per_block),
        ),
    )
    self_flat = join_rows(self_mixed).reshape(row_count, -1)
    after_self = resident + add_heads(
        jnp.dot(self_flat, output_all[0], preferred_element_type=jnp.float32)
    )
    normed_two = root_norm(after_self, gain_low[1]).astype(jnp.bfloat16)
    cross_q = heads_of(
        jnp.dot(normed_two, query_all[1], preferred_element_type=jnp.float32).astype(jnp.bfloat16)
    )
    encoder_full = lax.all_gather(encoder, "mp", axis=1, tiled=True)
    cross_kv = jnp.einsum(
        "std,kdc->stkc", encoder_full, keyval_all[1], preferred_element_type=jnp.float32
    ).astype(jnp.bfloat16)
    cross_k = heads_of(cross_kv[:, :, 0])
    cross_v = heads_of(cross_kv[:, :, 1])

    def cross_forward(queries, key_rows, values, segments, sources):
        return attend_forward(queries, key_rows, values, 0.0, cross_mask(segments, sources))

    cross_mixed, cross_total = lax.map(
        lambda pieces: cross_forward(*pieces),
        (
            split_rows(cross_q, per_block),
            split_rows(cross_k, per_block),
            split_rows(cross_v, per_block),
            split_rows(target_segments, per_block),
            split_rows(encoder_segments, per_block),
        ),
    )
    cross_flat = join_rows(cross_mixed).reshape(row_count, -1)
    after_cross = after_self + add_heads(
        jnp.dot(cross_flat, output_all[1], preferred_element_type=jnp.float32)
    )
    normed_three = root_norm(after_cross, gain_low[2]).astype(jnp.bfloat16)
    before = jnp.dot(normed_three, inner_all, preferred_element_type=jnp.float32)
    hidden = jax.nn.gelu(before, approximate=True).astype(jnp.bfloat16)
    outputs = after_cross + add_heads(
        jnp.dot(hidden, outer_all, preferred_element_type=jnp.float32)
    )
    low_out = cotangent.reshape(row_count, model_width)
    grad_outer = jnp.einsum("tc,td->cd", hidden, low_out, preferred_element_type=jnp.float32)
    grad_hidden = jnp.einsum("td,cd->tc", low_out, outer_all, preferred_element_type=jnp.float32)
    _, gelu_pull = jax.vjp(lambda before_act: jax.nn.gelu(before_act, approximate=True), before)
    grad_before = gelu_pull(grad_hidden)[0].astype(jnp.bfloat16)
    grad_inner = jnp.einsum(
        "td,tc->dc", normed_three, grad_before, preferred_element_type=jnp.float32
    )
    grad_normed_three = add_head_grads(
        jnp.einsum("tc,dc->td", grad_before, inner_all, preferred_element_type=jnp.float32)
    )
    _, norm_pull = jax.vjp(root_norm, after_cross, gain_low[2])
    grad_cross_norm, grad_gain_three = norm_pull(grad_normed_three)
    grad_second = low_out.astype(jnp.float32) + grad_cross_norm
    low_second = grad_second.astype(jnp.bfloat16)
    grad_output_cross = jnp.einsum(
        "tc,td->cd", cross_flat, low_second, preferred_element_type=jnp.float32
    )
    grad_cross_mixed = heads_of(
        jnp.einsum(
            "td,cd->tc", low_second, output_all[1], preferred_element_type=jnp.float32
        ).astype(jnp.bfloat16)
    )

    def cross_backward(queries, key_rows, values, segments, sources, log_total, grad_mixed):
        return attend_backward(
            queries, key_rows, values, 0.0, cross_mask(segments, sources), log_total, grad_mixed
        )

    cross_grads = lax.map(
        lambda pieces: cross_backward(*pieces),
        (
            split_rows(cross_q, per_block),
            split_rows(cross_k, per_block),
            split_rows(cross_v, per_block),
            split_rows(target_segments, per_block),
            split_rows(encoder_segments, per_block),
            cross_total,
            split_rows(grad_cross_mixed, per_block),
        ),
    )
    grad_cross_q = join_rows(cross_grads[0]).reshape(row_count, -1)
    kv_grad = jnp.stack(
        (
            join_rows(cross_grads[1]).reshape(seq_count, enc_length, -1),
            join_rows(cross_grads[2]).reshape(seq_count, enc_length, -1),
        ),
        axis=2,
    )
    grad_query_cross = jnp.einsum(
        "td,tc->dc", normed_two, grad_cross_q, preferred_element_type=jnp.float32
    )
    grad_keyval_cross = jnp.einsum(
        "std,stkc->kdc", encoder_full, kv_grad, preferred_element_type=jnp.float32
    )
    grad_normed_two = add_head_grads(
        jnp.einsum("tc,dc->td", grad_cross_q, query_all[1], preferred_element_type=jnp.float32)
    )
    _, norm_pull = jax.vjp(root_norm, after_self, gain_low[1])
    grad_self_norm, grad_gain_two = norm_pull(grad_normed_two)
    grad_first = grad_second + grad_self_norm
    low_first = grad_first.astype(jnp.bfloat16)
    grad_output_self = jnp.einsum(
        "tc,td->cd", self_flat, low_first, preferred_element_type=jnp.float32
    )
    grad_self_mixed = heads_of(
        jnp.einsum(
            "td,cd->tc", low_first, output_all[0], preferred_element_type=jnp.float32
        ).astype(jnp.bfloat16)
    )

    def self_backward(queries, key_rows, values, segments, log_total, grad_mixed):
        return attend_backward(
            queries, key_rows, values, score_bias, self_mask(segments), log_total, grad_mixed
        )

    self_grads = lax.map(
        lambda pieces: self_backward(*pieces),
        (
            split_rows(self_q, per_block),
            split_rows(self_k, per_block),
            split_rows(self_v, per_block),
            split_rows(target_segments, per_block),
            self_total,
            split_rows(grad_self_mixed, per_block),
        ),
    )
    grad_bias = jnp.sum(self_grads[3], axis=0)
    grad_table = jnp.einsum("qkb,hqk->bh", onehot, grad_bias, precision=lax.Precision.HIGHEST)
    stacked = jnp.stack(
        (
            join_rows(self_grads[0]).reshape(row_count, -1),
            join_rows(self_grads[1]).reshape(row_count, -1),
            join_rows(self_grads[2]).reshape(row_count, -1),
        ),
        axis=0,
    )
    grad_self_proj = jnp.einsum(
        "td,ktc->kdc", normed_one, stacked, preferred_element_type=jnp.float32
    )
    grad_normed_one = add_head_grads(
        jnp.einsum("ktc,kdc->td", stacked, self_weights, preferred_element_type=jnp.float32)
    )
    _, norm_pull = jax.vjp(root_norm, resident, gain_low[0])
    grad_input_norm, grad_gain_one = norm_pull(grad_normed_one)
    input_grad = (grad_first + grad_input_norm).astype(jnp.bfloat16).reshape(inputs.shape)
    reduced = (
        lax.psum_scatter(
            jnp.stack((grad_self_proj[0], grad_query_cross)), "dp", scatter_dimension=1, tiled=True
        ),
        lax.psum_scatter(
            jnp.stack((grad_self_proj[1:3], grad_keyval_cross)),
            "dp",
            scatter_dimension=2,
            tiled=True,
        ),
        lax.psum_scatter(
            jnp.stack((grad_output_self, grad_output_cross)), "dp", scatter_dimension=2, tiled=True
        ),
        lax.psum_scatter(grad_inner, "dp", scatter_dimension=0, tiled=True),
        lax.psum_scatter(grad_outer, "dp", scatter_dimension=1, tiled=True),
        lax.psum_scatter(
            jnp.stack((grad_gain_one, grad_gain_two, grad_gain_three)),
            "dp",
            scatter_dimension=1,
            tiled=True,
        ),
        lax.psum_scatter(grad_table, "dp", scatter_dimension=0, tiled=True),
    )
    params = (
        query_weight,
        keyval_weight,
        output_weight,
        inner_weight,
        outer_weight,
        gains,
        bias_table,
    )
    firsts = (
        query_first,
        keyval_first,
        output_first,
        inner_first,
        outer_first,
        gains_first,
        table_first,
    )
    seconds = (
        query_second,
        keyval_second,
        output_second,
        inner_second,
        outer_second,
        gains_second,
        table_second,
    )
    updated = [
        adam_step(*param_entry)
        for param_entry in zip(params, firsts, seconds, reduced, step_rates(), step_decays)
    ]
    return (
        outputs.astype(jnp.bfloat16).reshape(inputs.shape),
        input_grad,
        updated[0][0],
        updated[0][1],
        updated[0][2],
        updated[1][0],
        updated[1][1],
        updated[1][2],
        updated[2][0],
        updated[2][1],
        updated[2][2],
        updated[3][0],
        updated[3][1],
        updated[3][2],
        updated[4][0],
        updated[4][1],
        updated[4][2],
        updated[5][0],
        updated[5][1],
        updated[5][2],
        updated[6][0],
        updated[6][1],
        updated[6][2],
    )


def solution(mesh):
    return jax.shard_map(
        shards,
        mesh=mesh,
        in_specs=(
            P("dp", None, None),
            P("dp", "mp", None),
            P("dp", None, None),
            P("dp", None),
            P("dp", None),
            P(None, "dp", "mp"),
            P(None, "dp", "mp"),
            P(None, "dp", "mp"),
            P(None, None, "dp", "mp"),
            P(None, None, "dp", "mp"),
            P(None, None, "dp", "mp"),
            P(None, "mp", "dp"),
            P(None, "mp", "dp"),
            P(None, "mp", "dp"),
            P("dp", "mp"),
            P("dp", "mp"),
            P("dp", "mp"),
            P("mp", "dp"),
            P("mp", "dp"),
            P("mp", "dp"),
            P(None, "dp"),
            P(None, "dp"),
            P(None, "dp"),
            P("dp", "mp"),
            P("dp", "mp"),
            P("dp", "mp"),
        ),
        out_specs=(
            P("dp", None, None),
            P("dp", None, None),
            P(None, "dp", "mp"),
            P(None, "dp", "mp"),
            P(None, "dp", "mp"),
            P(None, None, "dp", "mp"),
            P(None, None, "dp", "mp"),
            P(None, None, "dp", "mp"),
            P(None, "mp", "dp"),
            P(None, "mp", "dp"),
            P(None, "mp", "dp"),
            P("dp", "mp"),
            P("dp", "mp"),
            P("dp", "mp"),
            P("mp", "dp"),
            P("mp", "dp"),
            P("mp", "dp"),
            P(None, "dp"),
            P(None, "dp"),
            P(None, "dp"),
            P("dp", "mp"),
            P("dp", "mp"),
            P("dp", "mp"),
        ),
        check_vma=False,
    )
```

profile of v0, /device:TPU:0, one launch (start us, length us, event | category | flops | bytes accessed | tf_op | source)
XLA Modules:
  0.0 910.4 jit_solution(9489984189621762022)
XLA Ops:
  8.8 10.2 %all-gather.1 = bf16[8,4,2]{1,2,0:T(2,128)(2,1)S(1)} all-gather(bf16[1,4,2]{1,2,0:T(2,128)(2,1)S(1)} %convert_bitcast_fusion.1), channel_id=1, replica_groups=mesh['dp'=8,'mp'=4] {'dp'}, dimensions={0}, use_global_device_ids=true | all-gather | bytes 144 | tf_op jit(solution)/shard_map/all_gather | solution.py:173
  21.1 8.9 all-gather
  33.9 8.5 all_gather.28
  42.4 9.3 %all_gather.24 = bf16[2,512,128]{2,0,1:T(2,128)(2,1)S(1)} all-gather(bf16[2,64,128]{2,0,1:T(2,128)(2,1)S(1)} %copy.398), channel_id=1, replica_groups=mesh['dp'=8,'mp'=4] {'dp'}, dimensions={1}, use_global_device_ids=true | all-gather | bytes 294912 | tf_op jit(solution)/shard_map/all_gather | solution.py:167
  52.2 8.9 all_gather.25
  72.9 85.7 %all-reduce.13.cloned.1.call-done = f32[1024,512]{1,0:T(8,128)} async-done(((f32[1024,512]{1,0:T(8,128)}), f32[1024,512]{1,0:T(8,128)}) %all-reduce.13.cloned.1.call-update) | async-done | bytes 2097168 | tf_op jit(solution)/shard_map/psum | solution.py:104
  163.0 77.0 %all-gather.4.cloned.1.call-done = bf16[8,512,512]{2,1,0:T(8,128)(2,1)} async-done(((bf16[8,128,512]{2,1,0:T(8,128)(2,1)}), bf16[8,512,512]{2,1,0:T(8,128)(2,1)}) %all-gather.4.cloned.1.call-update) | async-done | bytes 4194320 | tf_op jit(solution)/shard_map/all_gather | solution.py:224
  243.8 6.4 while.56
  252.3 10.8 %all_gather.30 = bf16[512,512]{1,0:T(8,128)(2,1)} all-gather(bf16[64,512]{1,0:T(8,128)(2,1)S(1)} %convert_element_type.307), channel_id=1, replica_groups=mesh['dp'=8,'mp'=4] {'dp'}, dimensions={0}, use_global_device_ids=true | all-gather | bytes 589824 | tf_op jit(solution)/shard_map/all_gather | solution.py:170
  263.1 74.2 %all-reduce.15.cloned.1.call-done = f32[1024,512]{1,0:T(8,128)} async-done(((f32[1024,512]{1,0:T(8,128)}), f32[1024,512]{1,0:T(8,128)}) %all-reduce.15.cloned.1.call-update) | async-done | bytes 2097168 | tf_op jit(solution)/shard_map/psum | solution.py:104
  344.3 35.1 %reduce-scatter.9.cloned.1.call-done = f32[512,64]{0,1:T(8,128)} async-done(((f32[512,512]{0,1:T(8,128)}), f32[512,64]{0,1:T(8,128)}) %reduce-scatter.9.cloned.1.call-update) | async-done | bytes 131088 | tf_op jit(solution)/shard_map/reduce_scatter | solution.py:374
  381.3 9.8 %all_gather.31 = bf16[512,512]{0,1:T(8,128)(2,1)S(1)} all-gather(bf16[512,64]{0,1:T(8,128)(2,1)S(1)} %get-tuple-element.718), channel_id=1, replica_groups=mesh['dp'=8,'mp'=4] {'dp'}, dimensions={1}, use_global_device_ids=true | all-gather | bytes 589824 | tf_op jit(solution)/shard_map/all_gather | solution.py:171
  391.1 3.9 fusion.98
  398.2 12.3 %all-reduce.19.cloned.1.call-start = ((), (), s32[]{:S(2)}) async-start(), calls=%async_computation.7 | async-start | bytes 4194304 | tf_op jit(solution)/shard_map/psum | solution.py:108
  410.5 74.4 %all-reduce.17.cloned.1.call-done = f32[1024,512]{1,0:T(8,128)} async-done(((f32[1024,512]{1,0:T(8,128)}), f32[1024,512]{1,0:T(8,128)}) %all-reduce.17.cloned.1.call-update) | async-done | bytes 2097168 | tf_op jit(solution)/shard_map/psum | solution.py:108
  495.6 15.7 %while.57 = (s32[]{:T(128)}, bf16[2,4,128,2,64]{2,1,0,4,3:T(4,128)(2,1)}, bf16[2,4,512,2,64]{2,4,3,1,0:T(8,128)(2,1)}, bf16[2,4,512,2,64]{2,4,3,1,0:T(8,128)(2,1...) while((s32[]{:T(128)}, ...), condition=%wide.region_18.19_spmd, body=%wide.region_16.18_spmd.sunk | while | flops 340589568 | bytes 43964784 | solution.py:283
  521.3 4.2 fusion.118
  525.6 75.7 %all-reduce.19.cloned.1.call-done = f32[1024,512]{1,0:T(8,128)} async-done(((f32[1024,512]{1,0:T(8,128)}), f32[1024,512]{1,0:T(8,128)}) %all-reduce.19.cloned.1.call-update) | async-done | bytes 2097168 | tf_op jit(solution)/shard_map/psum | solution.py:108
  609.3 10.6 %while.59 = (s32[]{:T(128)}, bf16[2,4,128,2,64]{2,4,3,1,0:T(8,128)(2,1)}, bf16[2,4,128,2,64]{2,4,3,1,0:T(8,128)(2,1)}, bf16[2,4,128,2,64]{2,4,3,1,0:T(8,128)(2,1...) while((s32[]{:T(128)}, ...), condition=%wide.region_24.25_spmd.clone, body=%wide.region_21.24_spmd.clone.sunk | while | flops 85507072 | bytes 6225041 | solution.py:330
  634.9 3.9 fusion.171
  649.8 14.0 %all-reduce.3 = f32[32,2]{0,1:T(2,128)S(1)} all-reduce(f32[32,2]{0,1:T(2,128)} %fusion.124), channel_id=8, replica_groups=mesh['dp'=8,'mp'=4] {'dp'}, use_global_device_ids=true, to_apply=%region_37.38.clone | all-reduce | flops 64 | bytes 512
  665.1 40.2 %all-reduce.21.cloned.1.call-done = (f32[2,512,128]{2,0,1:T(2,128)}, f32[2,2,512,128]{3,1,0,2:T(2,128)}, f32[2,128,512]{1,0,2:T(2,128)}) async-done(((f32[2,512,128]{2,0,1:T(2,128)}, f32[2,2,512,128]{3,1,0,2:T(2,128)}, f32[2,128,512]{1,0,2:T(2,128)}), (f32[2,512,128]{2,0,1:T(2,128)}, f32[2,2,512,128]{3,1,0,2:T(2,128)}, f32[2,128,512]{1,0,2:T(2,128)})) %all-reduce.21.cloned.1.call-update) | async-done | bytes 2097168
  712.8 149.6 %all-reduce.23.cloned.1.call-done = (f32[1024,512]{1,0:T(8,128)}, f32[1024,512]{1,0:T(8,128)}) async-done(((f32[1024,512]{1,0:T(8,128)}, f32[1024,512]{1,0:T(8,128)}), (f32[1024,512]{1,0:T(8,128)}, f32[1024,512]{1,0:T(8,128)})) %all-reduce.23.cloned.1.call-update) | async-done | bytes 4194320 | tf_op jit(solution)/shard_map/psum | solution.py:104
  872.1 29.8 %reduce-scatter.11.cloned.1.call-done = f32[64,3]{1,0:T(8,128)} async-done(((f32[512,3]{1,0:T(8,128)}), f32[64,3]{1,0:T(8,128)}) %reduce-scatter.11.cloned.1.call-update) | async-done | bytes 784
  (411 shorter events, 150.4 us)
Async XLA Ops:
  7.2 151.4 %all-reduce.13.cloned.1.call-start = ((), (), s32[]{:S(2)}) async-start(), calls=%async_computation.3 | async-start | bytes 4194304 | tf_op jit(solution)/shard_map/psum | solution.py:104
  30.7 129.9 %copy-start.68 = (f32[1,512]{1,0:T(1,128)}, f32[1,512]{1,0:T(1,128)S(1)}, u32[]{:S(2)}) copy-start(f32[1,512]{1,0:T(1,128)S(1)} %get-tuple-element.720) | copy-start | bytes 6148
  42.4 208.0 %copy-start.22 = (bf16[2,128,512]{1,2,0:T(8,128)(2,1)}, bf16[2,128,512]{1,2,0:T(8,128)(2,1)S(1)}, u32[]{:S(2)}) copy-start(bf16[2,128,512]{1,2,0:T(8,128)(2,1)S(1)} %all_gather.28) | copy-start | bytes 786436
  52.0 108.6 %copy-start.35 = (bf16[1,512,128]{2,0,1:T(2,128)(2,1)}, bf16[1,512,128]{2,0,1:T(2,128)(2,1)S(1)}, u32[]{:S(2)}) copy-start(bf16[1,512,128]{2,0,1:T(2,128)(2,1)S(1)} %get-tuple-element.716) | copy-start | bytes 393220
  71.6 168.4 %all-gather.4.cloned.1.call-start = ((), (), s32[]{:S(2)}) async-start(), calls=%async_computation.4 | async-start | bytes 5242880 | tf_op jit(solution)/shard_map/all_gather | solution.py:224
  72.4 265.0 %all-reduce.15.cloned.1.call-start = ((), (), s32[]{:S(2)}) async-start(), calls=%async_computation.5 | async-start | bytes 4194304 | tf_op jit(solution)/shard_map/psum | solution.py:104
  160.5 79.5 %copy-start.72 = (f32[1024]{0:T(1024)}, f32[1024]{0:T(1024)S(1)}, u32[]{:S(2)}) copy-start(f32[1024]{0:T(1024)S(1)} %get-tuple-element.697) | copy-start | bytes 12292
  160.6 79.4 %copy-start.57 = (f32[1024]{0:T(1024)}, f32[1024]{0:T(1024)S(1)}, u32[]{:S(2)}) copy-start(f32[1024]{0:T(1024)S(1)} %fusion.161) | copy-start | bytes 12292
  252.2 127.1 %reduce-scatter.9.cloned.1.call-start = ((), (), s32[]{:S(2)}) async-start(), calls=%async_computation.9 | async-start | bytes 1179648 | tf_op jit(solution)/shard_map/reduce_scatter | solution.py:374
  344.2 140.6 %all-reduce.17.cloned.1.call-start = ((), (), s32[]{:S(2)}) async-start(), calls=%async_computation.6 | async-start | bytes 4194304 | tf_op jit(solution)/shard_map/psum | solution.py:108
  398.2 203.1 %all-reduce.19.cloned.1.call-start = ((), (), s32[]{:S(2)}) async-start(), calls=%async_computation.7 | async-start | bytes 4194304 | tf_op jit(solution)/shard_map/psum | solution.py:108
  515.4 128.1 %reduce-scatter.7.cloned.1.call-start = ((), (), s32[]{:S(2)}) async-start(), calls=%async_computation.8 | async-start | bytes 1179648 | tf_op jit(solution)/shard_map/reduce_scatter | solution.py:373
  517.3 188.0 %all-reduce.21.cloned.1.call-start = ((), (), s32[]{:S(2)}) async-start(), calls=%async_computation.11 | async-start | bytes 4194304
  525.6 78.7 %copy-start.73 = (f32[1024]{0:T(1024)S(1)}, f32[1024]{0:T(1024)}, u32[]{:S(2)}) copy-start(f32[1024]{0:T(1024)} %copy-done.72) | copy-start | bytes 12292
  634.9 227.6 %all-reduce.23.cloned.1.call-start = ((), (), s32[]{:S(2)}) async-start(), calls=%async_computation.12 | async-start | bytes 8388608 | tf_op jit(solution)/shard_map/psum | solution.py:104
  640.9 67.1 %copy-start.51 = (f32[2,128,64]{1,2,0:T(8,128)S(1)}, f32[2,128,64]{1,2,0:T(8,128)}, u32[]{:S(2)}) copy-start(f32[2,128,64]{1,2,0:T(8,128)} %param.45) | copy-start | bytes 196612
  640.9 68.6 %copy-start.52 = (f32[2,64,128]{2,1,0:T(8,128)S(1)}, f32[2,64,128]{2,1,0:T(8,128)}, u32[]{:S(2)}) copy-start(f32[2,64,128]{2,1,0:T(8,128)} %param.39) | copy-start | bytes 196612
  640.9 70.2 %copy-start.43 = (f32[2,2,64,128]{3,2,1,0:T(8,128)S(1)}, f32[2,2,64,128]{3,2,1,0:T(8,128)}, u32[]{:S(2)}) copy-start(f32[2,2,64,128]{3,2,1,0:T(8,128)} %param.42) | copy-start | bytes 393220
  640.9 261.0 %reduce-scatter.11.cloned.1.call-start = ((), (), s32[]{:S(2)}) async-start(), calls=%async_computation.10 | async-start | bytes 294912
  643.4 219.0 %copy-start.8 = (bf16[8,128,512]{2,1,0:T(8,128)(2,1)S(1)}, bf16[8,128,512]{2,1,0:T(8,128)(2,1)}, u32[]{:S(2)}) copy-start(bf16[8,128,512]{2,1,0:T(8,128)(2,1)} %param.34) | copy-start | bytes 3145732
  643.4 219.0 %copy-start.64 = (f32[1024]{0:T(1024)S(1)}, f32[1024]{0:T(1024)}, u32[]{:S(2)}) copy-start(f32[1024]{0:T(1024)} %copy-done.63) | copy-start | bytes 12292
  643.4 219.0 %copy-start.77 = (f32[1,512]{1,0:T(1,128)S(1)}, f32[1,512]{1,0:T(1,128)}, u32[]{:S(2)}) copy-start(f32[1,512]{1,0:T(1,128)} %copy-done.76) | copy-start | bytes 6148
  647.1 64.0 %copy-start.53 = (f32[2,2,64,128]{3,2,1,0:T(8,128)S(1)}, f32[2,2,64,128]{3,2,1,0:T(8,128)}, u32[]{:S(2)}) copy-start(f32[2,2,64,128]{3,2,1,0:T(8,128)} %param.44) | copy-start | bytes 393220
  711.1 153.9 %copy-start.71 = (f32[8,128]{1,0:T(8,128)S(1)}, f32[8,128]{1,0:T(8,128)}, u32[]{:S(2)}) copy-start(f32[8,128]{1,0:T(8,128)} %copy-done.70) | copy-start | bytes 12292
  (84 other events, 405.0 us)
Sparse Core Ops, SparseCore 0:
  71.7 86.8 all-reduce.12
  160.3 79.7 all-gather.3
  252.3 85.0 all-reduce.14
  344.3 34.9 reduce-scatter.8
  398.3 86.5 all-reduce.16
  515.5 85.7 all-reduce.18
  604.4 35.0 reduce-scatter.6
  643.5 61.8 all-reduce.20
  707.8 154.6 all-reduce.22
  869.3 32.5 reduce-scatter.10
where the time goes:
time: 918 us; the launch traced here: 910 us
  waiting for transfers between devices  643 us (70%)
  blocking collectives  80.3 us (9%)
  matrix products  63.2 us (7%)
  local copies, waits for them, and re-layouts  50.4 us (5%)
  other arithmetic  43.5 us (5%)
  between operations  16.9 us (2%)
  starting transfers between devices  12.9 us (1%)
    psum x3, waiting for transfers between devices, add_heads(): return lax.psum(partial_value, 'mp')  310 us
    psum x2, waiting for transfers between devices, add_head_grads(): return lax.psum(partial_value, 'mp')  150 us
    all_gather x1, waiting for transfers between devices, shards(): encoder_full = lax.all_gather(encoder, 'mp', axis=1, tiled=True)  77 us
    unnamed x12, waiting for transfers between devices  70.9 us
    reduce_scatter x1, waiting for transfers between devices, shards(): lax.psum_scatter(grad_outer, 'dp', scatter_dimension=1, tiled=True)  35.1 us
  transfers between devices with their start and end apart: 10, of which 9 were waited for; matrix products, arithmetic and copies ran while one was open for 8% of the time, Pallas kernels for 0%

commit v1 on v0

v1 whole, which is shorter than its diff:
```python
import functools
import math

import jax
import jax.numpy as jnp
from jax import lax
from jax.experimental import pallas as pl
from jax.experimental.pallas import tpu as pltpu
from jax.sharding import PartitionSpec as P

D = 512
HEADS = 8
HEAD_DIM = 64
FF = 2048
NB = 32
HD = 512
STEP = 10
PAIRS = HEADS // 2
PAIR = 2 * HEAD_DIM
HIDDEN = FF // PAIRS
EXTRA = 16
VMEM_BYTES = 56 * 1024 * 1024

norm_eps = 1e-06
beta_first = 0.9
beta_second = 0.95
adam_eps = 1e-08
decay_weight = 0.1
rate_factor = 0.6
masked_value = -1000000000.0
bucket_edges = tuple((math.ceil(16 * 8 ** (number / 16)) for number in range(1, 16)))
step_decays = (decay_weight, decay_weight, decay_weight, decay_weight, decay_weight, 0.0, 0.0)
gelu_slope = math.sqrt(2.0 / math.pi)
gelu_cubic = 0.044715

f32 = jnp.float32
bf16 = jnp.bfloat16
ALL = ("dp", "mp")
VM = pltpu.VMEM


def dot_nn(a, b):
    return lax.dot_general(a, b, (((1,), (0,)), ((), ())), preferred_element_type=f32)


def dot_nt(a, b):
    return lax.dot_general(a, b, (((1,), (1,)), ((), ())), preferred_element_type=f32)


def dot_tn(a, b):
    return lax.dot_general(a, b, (((0,), (0,)), ((), ())), preferred_element_type=f32)


def root_scale(values):
    return lax.rsqrt(jnp.mean(values * values, axis=-1, keepdims=True) + norm_eps)


def root_back(values, gain, grad):
    scale = root_scale(values)
    grad_gain = jnp.sum(grad * values * scale, axis=0, keepdims=True)
    weighted = grad * gain
    along = jnp.sum(weighted * values, axis=-1, keepdims=True)
    inverse = 1.0 / values.shape[-1]
    return scale * weighted - values * (scale * scale * scale * along * inverse), grad_gain


def stack_heads(pair):
    lane = lax.broadcasted_iota(jnp.int32, pair.shape, 1)
    zero = jnp.zeros_like(pair)
    return jnp.concatenate(
        (jnp.where(lane < HEAD_DIM, pair, zero), jnp.where(lane >= HEAD_DIM, pair, zero)), axis=0
    )


def unstack_heads(stacked):
    half = stacked.shape[0] // 2
    top, bottom = stacked[:half], stacked[half:]
    lane = lax.broadcasted_iota(jnp.int32, top.shape, 1)
    return jnp.where(lane < HEAD_DIM, top, bottom)


def column_of(row):
    return jnp.transpose(jnp.broadcast_to(row, (128, row.shape[1])))


def doubled(mask_value):
    return jnp.concatenate((mask_value, mask_value), axis=1)


def attend(query, key, value, bias, allowed):
    scores = dot_nt(key, stack_heads(query))
    if bias is not None:
        scores = scores + bias
    scores = jnp.where(allowed, scores, masked_value)
    peak = jnp.max(scores, axis=0, keepdims=True)
    terms = jnp.exp(scores - peak)
    total = jnp.sum(terms, axis=0, keepdims=True)
    probs = (terms * (1.0 / total)).astype(bf16)
    mixed = unstack_heads(dot_tn(probs, value))
    return mixed.astype(bf16), peak + jnp.log(total)


def attend_back(query, key, value, bias, allowed, log_total, grad_mixed):
    query_stack, grad_stack = stack_heads(query), stack_heads(grad_mixed)
    scores = dot_nt(key, query_stack)
    if bias is not None:
        scores = scores + bias
    scores = jnp.where(allowed, scores, masked_value)
    probs = jnp.exp(scores - log_total)
    grad_probs = dot_nt(value, grad_stack)
    grad_value = dot_nn(probs.astype(bf16), grad_stack)
    along = jnp.sum(grad_probs * probs, axis=0, keepdims=True)
    grad_scores = probs * (grad_probs - along)
    low_scores = grad_scores.astype(bf16)
    grad_key = dot_nn(low_scores, query_stack)
    grad_query = unstack_heads(dot_tn(low_scores, key))
    return (
        grad_query.astype(bf16),
        grad_key.astype(bf16),
        grad_value.astype(bf16),
        grad_scores,
    )


def weight_copies(slots, weights, tab, sems):
    copies = []
    for number, slot in enumerate(slots):
        rows = weights.shape[1] // len(slots)
        start = pl.multiple_of(tab[number] * rows, rows)
        copies.append(
            pltpu.make_async_copy(
                slot.at[:, pl.ds(0, rows), :], weights.at[:, pl.ds(start, rows), :], sems.at[number]
            )
        )
    return copies


def extra_copies(slots, extras, rows, sems):
    return [
        pltpu.make_async_copy(slot.at[:, pl.ds(rows, EXTRA), :], extras.at[number], sems.at[number])
        for number, slot in enumerate(slots)
    ]


def permute_rows(source, target, tab, n_slots):
    rows = source.shape[0] // n_slots
    for number in range(n_slots):
        start = pl.multiple_of(tab[number] * rows, rows)
        target[number * rows : (number + 1) * rows, :] = source[pl.ds(start, rows), :]


def slot_part(outs, number):
    for out in outs:
        if number < out.shape[0]:
            return out, number
        number -= out.shape[0]
    raise ValueError


def write_slots(outs, n_slots, pair, grad):
    rows = grad.shape[0] // n_slots
    low = grad.astype(bf16)
    for number in range(n_slots):
        out, place = slot_part(outs, number)
        out[place, pair, 0:rows, :] = low[number * rows : (number + 1) * rows]


def toeplitz(row, length):
    return pltpu.roll(jnp.broadcast_to(row, (length, row.shape[1])), 0, 1, stride=1, stride_axis=0)


def bias_of(tab, falls, pair, length):
    head = tab[16 + pair] * 2
    return jnp.concatenate(
        [toeplitz(falls[pl.ds(head + side, 1), :], length) for side in range(2)], axis=1
    )


def fold_diagonals(grad):
    length = grad.shape[1]
    folded = grad[0:8]
    for start in range(8, grad.shape[0], 8):
        folded = folded + pltpu.roll(grad[start : start + 8], length - start, 1)
    row = lax.broadcasted_iota(jnp.int32, folded.shape, 0)
    for bit in (1, 2, 4):
        folded = jnp.where(row & bit != 0, pltpu.roll(folded, length - bit, 1), folded)
    return jnp.sum(folded, axis=0, keepdims=True)


def self_masks(tab, targets, row, length):
    segments = targets[pl.ds(tab[24] + row, 1), :].astype(f32)
    column = column_of(segments)
    keys = lax.broadcasted_iota(jnp.int32, (length, length), 0)
    queries = lax.broadcasted_iota(jnp.int32, (length, length), 1)
    return doubled(
        jnp.where((column == segments) & (queries >= keys), 1.0, 0.0)
    ) > 0.5


def cross_masks(tab, targets, sources, row, n_pieces, piece_tab):
    segments = targets[pl.ds(tab[24] + row, 1), :].astype(f32)
    width = sources.shape[1] // n_pieces
    chosen = lax.broadcasted_iota(jnp.int32, (sources.shape[0], width), 0) == tab[24] + row
    parts = []
    for i in range(n_pieces):
        start = pl.multiple_of(tab[piece_tab + i] * width, 128)
        slab = sources[:, pl.ds(start, width)].astype(f32)
        parts.append(jnp.sum(jnp.where(chosen, slab, 0.0), axis=0, keepdims=True))
    column = column_of(jnp.concatenate(parts, axis=1) if n_pieces > 1 else parts[0])
    return doubled(jnp.where(column == segments, 1.0, 0.0)) > 0.5


def self_forward_kernel(n_slots, rows_held, tab, targets, onehot, x_all, *refs):
    slots, refs = refs[:n_slots], refs[n_slots:]
    after, normed, query, key, value, mixed, totals, gains, falls = refs[:9]
    weights, extras, x_rows, sems, extra_sems, x_sem = refs[9:]
    length = x_all.shape[1]
    fetch_x = pltpu.make_async_copy(x_all.at[pl.ds(tab[24], rows_held)], x_rows, x_sem)
    fetch_extra = extra_copies(slots, extras, D // n_slots, extra_sems)
    fetch = weight_copies(slots, weights, tab, sems)
    for copy in [fetch_x] + fetch_extra + fetch:
        copy.start()
    for copy in fetch_extra:
        copy.wait()
    tile = jnp.zeros((EXTRA, D), f32)
    for number in range(n_slots):
        for pair in range(PAIRS):
            tile = tile + extras[number, pair].astype(f32)
    gains[...] = tile[0:8]
    falls[...] = dot_nn(tile[8:16, 0:128].astype(bf16), onehot[...])
    fetch_x.wait()
    resident = x_rows[...].reshape(rows_held * length, D).astype(f32)
    low = (resident * root_scale(resident) * tile[0:1]).astype(bf16)
    normed[...] = low
    for copy in fetch:
        copy.wait()
    for pair in range(PAIRS):
        projected = dot_nn(low, weights[pair, :, 0 : 3 * PAIR]).astype(bf16)
        query[pair] = projected[:, 0:PAIR]
        key[pair] = projected[:, PAIR : 2 * PAIR]
        value[pair] = projected[:, 2 * PAIR :]
    allowed = [self_masks(tab, targets, row, length) for row in range(rows_held)]
    total = resident
    for pair in range(PAIRS):
        bias = bias_of(tab, falls, pair, length)
        for row in range(rows_held):
            span = slice(row * length, (row + 1) * length)
            mix, log_total = attend(
                query[pair, span], key[pair, span], value[pair, span], bias, allowed[row]
            )
            mixed[pair, span] = mix
            totals[pair, row : row + 1, :] = log_total
        total = total + dot_nt(mixed[pair], weights[pair, :, 3 * PAIR :])
    after[...] = total


def encoder_copies(pieces, encoder, tab, rows_held, sems):
    width = encoder.shape[1] // len(pieces)
    copies = []
    for number, piece in enumerate(pieces):
        start = tab[24] if piece.shape[0] > rows_held else 0
        copies.append(
            pltpu.make_async_copy(
                piece.at[pl.ds(start, rows_held)],
                encoder.at[:, pl.ds(number * width, width), :],
                sems.at[number],
            )
        )
    return copies


def cross_forward_kernel(n_slots, n_pieces, rows_held, tab, targets, sources, gains, before, *refs):
    slots, pieces, refs = refs[:n_slots], refs[n_slots : n_slots + n_pieces], refs[n_slots + n_pieces :]
    after, normed, query, key, value, mixed, totals, encoder = refs[:8]
    weights, sems, piece_sems = refs[8:]
    length = before.shape[0] // rows_held
    source_length = sources.shape[1]
    fetch_pieces = encoder_copies(pieces, encoder, tab, rows_held, piece_sems)
    fetch = weight_copies(slots, weights, tab, sems)
    for copy in fetch_pieces + fetch:
        copy.start()
    resident = before[...]
    low = (resident * root_scale(resident) * gains[1:2]).astype(bf16)
    normed[...] = low
    allowed = [
        cross_masks(tab, targets, sources, row, n_pieces, 16 if n_pieces > 1 else 25)
        for row in range(rows_held)
    ]
    for copy in fetch_pieces + fetch:
        copy.wait()
    source = encoder[...].reshape(rows_held * source_length, D)
    total = resident
    for pair in range(PAIRS):
        query[pair] = dot_nn(low, weights[pair, :, 0:PAIR]).astype(bf16)
        projected = dot_nn(source, weights[pair, :, PAIR : 3 * PAIR]).astype(bf16)
        key[pair] = projected[:, 0:PAIR]
        value[pair] = projected[:, PAIR:]
        for row in range(rows_held):
            span = slice(row * length, (row + 1) * length)
            wide = slice(row * source_length, (row + 1) * source_length)
            mix, log_total = attend(
                query[pair, span], key[pair, wide], value[pair, wide], None, allowed[row]
            )
            mixed[pair, span] = mix
            totals[pair, row : row + 1, :] = log_total
        total = total + dot_nt(mixed[pair], weights[pair, :, 3 * PAIR :])
    after[...] = total


def feed_kernel(n_slots, n_outs, rows_held, tab, gains, before, c_all, *refs):
    slots, refs = refs[:n_slots], refs[n_slots:]
    low_out, grad_before, grad_gain = refs[:3]
    outs, refs = refs[3 : 3 + n_outs], refs[3 + n_outs :]
    weights, c_rows, turned, normed_turned, c_turned, sems, c_sem = refs
    fetch_c = pltpu.make_async_copy(c_all.at[pl.ds(tab[24], rows_held)], c_rows, c_sem)
    fetch = weight_copies(slots, weights, tab, sems)
    fetch_c.start()
    for copy in fetch:
        copy.start()
    resident = before[...]
    gain = gains[2:3]
    low = (resident * root_scale(resident) * gain).astype(bf16)
    turned[...] = jnp.transpose(low)
    permute_rows(turned, normed_turned, tab, n_slots)
    fetch_c.wait()
    cotangent = c_rows[...].reshape(resident.shape)
    turned[...] = jnp.transpose(cotangent)
    permute_rows(turned, c_turned, tab, n_slots)
    for copy in fetch:
        copy.wait()
    total = resident
    grad_normed = jnp.zeros_like(resident)
    for pair in range(PAIRS):
        inner, outer = weights[pair, :, 0:HIDDEN], weights[pair, :, HIDDEN:]
        u = dot_nn(low, inner)
        squared = u * u
        bent = jnp.tanh(gelu_slope * (u + gelu_cubic * u * squared))
        hidden = (0.5 * u * (1.0 + bent)).astype(bf16)
        slope = 0.5 * (1.0 + bent) + 0.5 * u * (1.0 - bent * bent) * gelu_slope * (
            1.0 + 3.0 * gelu_cubic * squared
        )
        total = total + dot_nt(hidden, outer)
        grad_u = (dot_nn(cotangent, outer) * slope).astype(bf16)
        grad_normed = grad_normed + dot_nt(grad_u, inner)
        write_slots(
            outs,
            n_slots,
            pair,
            jnp.concatenate(
                (dot_nn(normed_turned[...], grad_u), dot_nn(c_turned[...], hidden)), axis=1
            ),
        )
    low_out[...] = total.astype(bf16)
    through, gain_part = root_back(resident, gain, grad_normed)
    grad_before[...] = cotangent.astype(f32) + through
    grad_gain[...] = gain_part


def cross_back_kernel(
    n_slots, n_pieces, n_outs, rows_held, tab, targets, sources, gains, grad_after, before, *refs
):
    normed, query, key, value, mixed, totals, encoder = refs[:7]
    slots, refs = refs[7 : 7 + n_slots], refs[7 + n_slots :]
    grad_before, grad_gain = refs[:2]
    outs, refs = refs[2 : 2 + n_outs], refs[2 + n_outs :]
    weights, turned, low_turned, normed_turned, wide_turned, encoder_turned, d_key, d_value, sems = refs
    length = before.shape[0] // rows_held
    source_length = sources.shape[1]
    fetch = weight_copies(slots, weights, tab, sems)
    for copy in fetch:
        copy.start()
    grad_in = grad_after[...]
    low = grad_in.astype(bf16)
    turned[...] = jnp.transpose(low)
    permute_rows(turned, low_turned, tab, n_slots)
    turned[...] = jnp.transpose(normed[...])
    permute_rows(turned, normed_turned, tab, n_slots)
    wide_turned[...] = jnp.transpose(encoder[...].reshape(rows_held * source_length, D))
    permute_rows(wide_turned, encoder_turned, tab, n_slots)
    allowed = [
        cross_masks(tab, targets, sources, row, n_pieces, 16 if n_pieces > 1 else 25)
        for row in range(rows_held)
    ]
    for copy in fetch:
        copy.wait()
    grad_normed = jnp.zeros_like(grad_in)
    for pair in range(PAIRS):
        grad_mixed = dot_nn(low, weights[pair, :, 3 * PAIR :]).astype(bf16)
        d_queries = []
        for row in range(rows_held):
            span = slice(row * length, (row + 1) * length)
            wide = slice(row * source_length, (row + 1) * source_length)
            d_query, d_key[wide], d_value[wide], _ = attend_back(
                query[pair, span],
                key[pair, wide],
                value[pair, wide],
                None,
                allowed[row],
                totals[pair, row : row + 1, :],
                grad_mixed[span],
            )
            d_queries.append(d_query)
        d_query = jnp.concatenate(d_queries, axis=0) if rows_held > 1 else d_queries[0]
        grad_normed = grad_normed + dot_nt(d_query, weights[pair, :, 0:PAIR])
        write_slots(
            outs,
            n_slots,
            pair,
            jnp.concatenate(
                (
                    dot_nn(normed_turned[...], d_query),
                    dot_nn(encoder_turned[...], d_key[...]),
                    dot_nn(encoder_turned[...], d_value[...]),
                    dot_nn(low_turned[...], mixed[pair]),
                ),
                axis=1,
            ),
        )
    through, gain_part = root_back(before[...], gains[1:2], grad_normed)
    grad_before[...] = grad_in + through
    grad_gain[...] = gain_part


def self_back_kernel(
    n_slots, n_outs, rows_held, tab, targets, onehot, gains, falls, gain_two, gain_three, grad_after, x_all, *refs
):
    normed, query, key, value, mixed, totals = refs[:6]
    slots, refs = refs[6 : 6 + n_slots], refs[6 + n_slots :]
    low_grad = refs[0]
    outs, refs = refs[1 : 1 + n_outs], refs[1 + n_outs :]
    weights, x_rows, turned, low_turned, normed_turned, bias_rows, sems, x_sem = refs
    length = x_all.shape[1]
    fetch_x = pltpu.make_async_copy(x_all.at[pl.ds(tab[24], rows_held)], x_rows, x_sem)
    fetch = weight_copies(slots, weights, tab, sems)
    for copy in fetch + [fetch_x]:
        copy.start()
    grad_in = grad_after[...]
    low = grad_in.astype(bf16)
    turned[...] = jnp.transpose(low)
    permute_rows(turned, low_turned, tab, n_slots)
    turned[...] = jnp.transpose(normed[...])
    permute_rows(turned, normed_turned, tab, n_slots)
    allowed = [self_masks(tab, targets, row, length) for row in range(rows_held)]
    for copy in fetch:
        copy.wait()
    grad_normed = jnp.zeros_like(grad_in)
    for pair in range(PAIRS):
        bias = bias_of(tab, falls, pair, length)
        grad_mixed = dot_nn(low, weights[pair, :, 3 * PAIR :]).astype(bf16)
        parts = []
        grad_bias = jnp.zeros((length, 2 * length), f32)
        for row in range(rows_held):
            span = slice(row * length, (row + 1) * length)
            d_query, d_key, d_value, grad_scores = attend_back(
                query[pair, span],
                key[pair, span],
                value[pair, span],
                bias,
                allowed[row],
                totals[pair, row : row + 1, :],
                grad_mixed[span],
            )
            parts.append(jnp.concatenate((d_query, d_key, d_value), axis=1))
            grad_bias = grad_bias + grad_scores
        for side in range(2):
            diagonal = fold_diagonals(grad_bias[:, side * length : (side + 1) * length])
            bias_rows[pl.ds(tab[16 + pair] * 2 + side, 1), :] = diagonal
        joined = jnp.concatenate(parts, axis=0) if rows_held > 1 else parts[0]
        grad_normed = grad_normed + dot_nt(joined, weights[pair, :, 0 : 3 * PAIR])
        write_slots(
            outs,
            n_slots,
            pair,
            jnp.concatenate(
                (dot_nn(normed_turned[...], joined), dot_nn(low_turned[...], mixed[pair])), axis=1
            ),
        )
    fetch_x.wait()
    resident = x_rows[...].reshape(grad_in.shape).astype(f32)
    through, gain_one = root_back(resident, gains[0:1], grad_normed)
    low_grad[...] = (grad_in + through).astype(bf16)
    table = lax.dot_general(
        bias_rows[...],
        onehot[...].astype(f32),
        (((1,), (1,)), ((), ())),
        precision=lax.Precision.HIGHEST,
        preferred_element_type=f32,
    )
    blank = jnp.zeros((5, D), f32)
    table = jnp.concatenate((table, jnp.zeros((8, D - 128), f32)), axis=1)
    tile = jnp.concatenate((gain_one, gain_two[...], gain_three[...], blank, table), axis=0).astype(bf16)
    rows = D // n_slots
    for number in range(n_slots):
        out, place = slot_part(outs, number)
        for pair in range(PAIRS):
            out[place, pair, rows : rows + EXTRA, :] = tile


def pack_kernel(query, keyval, output, inner, outer, tile, own_self, own_cross, own_feed):
    rows = query.shape[1]
    for number, own in enumerate((own_self, own_cross)):
        parts = (query[number], keyval[number, 0], keyval[number, 1], output[number])
        own[0:rows, :] = jnp.concatenate(parts, axis=1).astype(bf16)
    own_self[rows : rows + EXTRA, :] = tile[...].astype(bf16)
    own_feed[...] = jnp.concatenate((inner[...], outer[...]), axis=1).astype(bf16)


def spread_kernel(rows_held, tab, *refs):
    pieces, out = refs[:-1], refs[-1]
    for number, piece in enumerate(pieces):
        out[pl.ds(tab[16 + number] * rows_held, rows_held)] = piece[...]


def shape(dims, dtype):
    return jax.ShapeDtypeStruct(dims, dtype)


def dma_sems(count):
    return pltpu.SemaphoreType.DMA((count,))


def call(kernel, operands, outs, scratch, flops=0):
    spaces = {"smem": pltpu.SMEM, "vmem": pltpu.VMEM, "any": pl.ANY}
    arrays = [array for array, _ in operands]
    moved = sum(a.size * a.dtype.itemsize for a in arrays) + sum(
        math.prod(o.shape) * o.dtype.itemsize for o in outs
    )
    return pl.pallas_call(
        kernel,
        out_shape=tuple(outs),
        in_specs=[pl.BlockSpec(memory_space=spaces[place]) for _, place in operands],
        out_specs=tuple(pl.BlockSpec(memory_space=pltpu.VMEM) for _ in outs),
        scratch_shapes=scratch,
        compiler_params=pltpu.CompilerParams(vmem_limit_bytes=VMEM_BYTES),
        cost_estimate=pl.CostEstimate(flops=flops, bytes_accessed=moved, transcendentals=0),
    )(*arrays)


def bucket_onehot(length):
    distance = jnp.arange(length, dtype=jnp.int32)
    bucket = jnp.minimum(distance, 16)
    for edge_value in bucket_edges:
        bucket = bucket + (distance >= edge_value).astype(jnp.int32)
    return (jnp.arange(128, dtype=jnp.int32)[:, None] == bucket[None, :]).astype(bf16)


def adam_step(weight, first, second, grad, rate, decay):
    new_first = beta_first * first + (1.0 - beta_first) * grad
    new_second = beta_second * second + (1.0 - beta_second) * grad * grad
    ratio = (
        new_first
        / (1.0 - beta_first**STEP)
        / (jnp.sqrt(new_second / (1.0 - beta_second**STEP)) + adam_eps)
    )
    return (new_first, new_second, weight - rate * (ratio + decay * weight))


def step_rates():
    return (
        rate_factor * (16 * D) ** (-0.5),
        rate_factor * D ** (-0.5),
        rate_factor * (HD // 8) ** (-0.5),
        rate_factor * D ** (-0.5),
        rate_factor * (FF // 2) ** (-0.5),
        rate_factor,
        rate_factor,
    )


class TreePlan:
    n_slots = 8
    out_slots = (4, 4)

    def __init__(self, n_dp, n_mp):
        self.n_dp, self.n_mp = n_dp, n_mp

    def pairs(self, target):
        n_mp = self.n_mp
        return [
            (d * n_mp + m, t * n_mp + s)
            for d in range(self.n_dp)
            for m in range(n_mp)
            for t, s in (target(d, m),)
        ]

    def hop_z(self, array, number):
        return lax.ppermute(array, ALL, self.pairs(lambda d, m: (d, m ^ number)))

    def hop_core(self, array):
        return lax.ppermute(array, ALL, self.pairs(lambda d, m: (d ^ 1, m)))

    def hop_first(self, array):
        return lax.ppermute(array, ALL, self.pairs(lambda d, m: (d ^ (4 if d & 1 else 2), m)))

    def hop_second(self, array):
        return lax.ppermute(array, ALL, self.pairs(lambda d, m: (d ^ (2 if d & 1 else 4), m)))

    def table(self, place_dp, place_mp, rows_held):
        core = place_dp & 1
        first, second = 2 + 2 * core, 4 - 2 * core
        own = [place_dp ^ (a * first) ^ (b * second) for b in range(2) for a in range(2)]
        peer = [place_dp ^ 1 ^ (a * second) ^ (b * first) for b in range(2) for a in range(2)]
        return own + peer, [place_mp ^ j for j in range(4)]

    def gather(self, own):
        base = jnp.stack([own] + [self.hop_z(own, number) for number in (1, 2, 3)])
        near, far = self.hop_first(base), self.hop_second(base)
        both = self.hop_second(near)
        slots = [base, near, far, both]
        return slots + [self.hop_core(slot) for slot in slots]

    def reduce(self, parts):
        own, peer = parts
        half = self.hop_core(peer).astype(f32) + own.astype(f32)
        kept = half[0:2] + self.hop_second(half[2:4].astype(bf16)).astype(f32)
        kept = kept[0] + self.hop_first(kept[1].astype(bf16)).astype(f32)
        low = kept.astype(bf16)
        total = kept[0]
        for number in (1, 2, 3):
            total = total + self.hop_z(low[number], number).astype(f32)
        return total, total[D // self.n_dp :]

    def encoder_pieces(self, encoder, place_mp, rows_held):
        sent = [
            self.hop_z(
                lax.dynamic_slice_in_dim(encoder, (place_mp ^ number) * rows_held, rows_held, 0), number
            )
            for number in (1, 2, 3)
        ]
        return [encoder] + sent

    def spread(self, tab, piece, rows_held):
        pieces = [piece] + [self.hop_z(piece, number) for number in (1, 2, 3)]
        out = shape((rows_held * self.n_mp,) + piece.shape[1:], piece.dtype)
        (result,) = call(
            functools.partial(spread_kernel, rows_held),
            [(tab, "smem")] + [(array, "vmem") for array in pieces],
            [out],
            [],
        )
        return result


class PlainPlan:
    n_slots = 1
    out_slots = (1,)

    def __init__(self, n_dp, n_mp):
        self.n_dp, self.n_mp = n_dp, n_mp

    def table(self, place_dp, place_mp, rows_held):
        return [0], [0, 1, 2, 3]

    def gather(self, own):
        rows = D // self.n_dp
        kinds = 4 if own.shape[1] * self.n_mp == 4 * HD else 2
        full = lax.all_gather(own[:rows], ("mp", "dp"), axis=0, tiled=True)
        full = full.reshape(self.n_mp, D, kinds, -1).transpose(2, 1, 0, 3)
        full = full.reshape(kinds, D, PAIRS, -1).transpose(2, 1, 0, 3).reshape(PAIRS, D, -1)
        return [full]

    def reduce(self, parts):
        grads = parts[0][0]
        kinds = 4 if grads.shape[2] == 4 * PAIR else 2
        full = grads[:, :D].reshape(PAIRS, D, kinds, -1).transpose(2, 1, 0, 3)
        full = full.reshape(kinds, D, self.n_mp, -1).transpose(2, 1, 0, 3)
        total = lax.psum_scatter(
            full.reshape(self.n_mp * D, -1), ("mp", "dp"), scatter_dimension=0, tiled=True
        ).astype(f32)
        return total, lax.psum(grads[0, D:].astype(f32), ALL) if grads.shape[1] > D else None

    def encoder_pieces(self, encoder, place_mp, rows_held):
        return [lax.all_to_all(encoder, "mp", split_axis=0, concat_axis=1, tiled=True)]

    def spread(self, tab, piece, rows_held):
        return lax.all_gather(piece, "mp", axis=0, tiled=True)


def shards(
    plan,
    inputs,
    encoder,
    cotangent,
    target_segments,
    encoder_segments,
    query_weight,
    query_first,
    query_second,
    keyval_weight,
    keyval_first,
    keyval_second,
    output_weight,
    output_first,
    output_second,
    inner_weight,
    inner_first,
    inner_second,
    outer_weight,
    outer_first,
    outer_second,
    gains,
    gains_first,
    gains_second,
    bias_table,
    table_first,
    table_second,
):
    n_slots, out_slots = plan.n_slots, plan.out_slots
    n_outs = len(out_slots)
    seq_count, length, _ = inputs.shape
    source_length = encoder_segments.shape[1]
    rows_held = seq_count // plan.n_mp
    tokens, sources = rows_held * length, rows_held * source_length
    place_dp, place_mp = lax.axis_index("dp"), lax.axis_index("mp")
    slot_table, pair_table = plan.table(place_dp, place_mp, rows_held)
    entries = slot_table + [0] * (16 - len(slot_table)) + pair_table + [0] * 4
    entries = entries + [place_mp * rows_held] + [0] * 7
    tab = jnp.stack([jnp.asarray(entry, jnp.int32) for entry in entries])
    onehot = bucket_onehot(length)

    width = gains.shape[1]
    lanes = jnp.arange(D, dtype=jnp.int32)
    gain_tile = jnp.where(
        ((lanes // width == place_dp) & (place_mp == 0))[None], jnp.tile(gains, (1, plan.n_dp)), 0.0
    )
    gain_tile = jnp.concatenate((gain_tile, jnp.zeros((5, D), f32)))
    bands, heads = bias_table.shape
    spread_table = jnp.tile(bias_table.T, (plan.n_mp, D // bands))
    head_number = jnp.arange(HEADS, dtype=jnp.int32)[:, None]
    table_tile = jnp.where(
        (head_number // heads == place_mp) & (lanes[None] // bands == place_dp), spread_table, 0.0
    )
    tile = jnp.concatenate((gain_tile, table_tile))
    columns = query_weight.shape[2]
    rows = D // plan.n_dp

    output_turned = output_weight.transpose(0, 2, 1)
    outer_turned = outer_weight.T
    if plan.n_slots == 8:
        own_self, own_cross, own_feed = call(
            pack_kernel,
            [
                (query_weight, "vmem"),
                (keyval_weight, "vmem"),
                (output_turned, "vmem"),
                (inner_weight, "vmem"),
                (outer_turned, "vmem"),
                (tile, "vmem"),
            ],
            [
                shape((rows + EXTRA, D), bf16),
                shape((rows, D), bf16),
                shape((rows, 2 * HIDDEN), bf16),
            ],
            [],
        )
        self_slots = plan.gather(own_self)
    else:
        own_self, own_cross = (
            jnp.concatenate(
                (query_weight[i], keyval_weight[i, 0], keyval_weight[i, 1], output_turned[i]), axis=1
            ).astype(bf16)
            for i in range(2)
        )
        own_feed = jnp.concatenate((inner_weight, outer_turned), axis=1).astype(bf16)
        (self_weights,) = plan.gather(own_self)
        small = lax.psum(tile.astype(bf16).astype(f32), ALL).astype(bf16)[None]
        small = jnp.concatenate((small, jnp.zeros((PAIRS - 1, EXTRA, D), bf16)))
        self_slots = [jnp.concatenate((self_weights, small), axis=1)]
    pieces = plan.encoder_pieces(encoder, place_mp, rows_held)
    cross_slots = plan.gather(own_cross)
    feed_slots = plan.gather(own_feed)
    n_pieces = len(pieces)

    def anys(arrays):
        return [(array, "any") for array in arrays]

    def vmems(arrays):
        return [(array, "vmem") for array in arrays]

    flat = (tokens, D)
    paired = (PAIRS, tokens, PAIR)
    wide = (PAIRS, sources, PAIR)
    stats = shape((PAIRS, rows_held, 2 * length), f32)
    attn_weights = VM((PAIRS, D, 4 * PAIR), bf16)

    after_self, normed_one, q_one, k_one, v_one, mix_one, sum_one, gain_rows, falls = call(
        functools.partial(self_forward_kernel, n_slots, rows_held),
        [(tab, "smem")] + vmems((target_segments, onehot)) + anys([inputs] + list(self_slots)),
        [shape(flat, f32), shape(flat, bf16)]
        + [shape(paired, bf16)] * 4
        + [stats, shape((8, D), f32), shape((8, length), f32)],
        [
            attn_weights,
            VM((n_slots, PAIRS, EXTRA, D), bf16),
            VM((rows_held, length, D), bf16),
            dma_sems(n_slots),
            dma_sems(n_slots),
            pltpu.SemaphoreType.DMA,
        ],
        flops=2 * tokens * D * 2048,
    )
    after_cross, normed_two, q_two, k_two, v_two, mix_two, sum_two, source_rows = call(
        functools.partial(cross_forward_kernel, n_slots, n_pieces, rows_held),
        [(tab, "smem")]
        + vmems((target_segments, encoder_segments, gain_rows, after_self))
        + anys(list(cross_slots) + list(pieces)),
        [
            shape(flat, f32),
            shape(flat, bf16),
            shape(paired, bf16),
            shape(wide, bf16),
            shape(wide, bf16),
            shape(paired, bf16),
            stats,
            shape((rows_held, source_length, D), bf16),
        ],
        [attn_weights, dma_sems(n_slots), dma_sems(n_pieces)],
        flops=2 * tokens * D * 2048 + 2 * sources * D * 1024,
    )

    def grad_outs(extra, width_out):
        return [
            shape((count, PAIRS, D // n_slots + extra, width_out), bf16) for count in out_slots
        ]

    feed_result = call(
        functools.partial(feed_kernel, n_slots, n_outs, rows_held),
        [(tab, "smem")] + vmems((gain_rows, after_cross)) + anys([cotangent] + list(feed_slots)),
        [shape(flat, bf16), shape(flat, f32), shape((1, D), f32)] + grad_outs(0, 2 * HIDDEN),
        [
            VM((PAIRS, D, 2 * HIDDEN), bf16),
            VM((rows_held, length, D), bf16),
            VM((D, tokens), bf16),
            VM((D, tokens), bf16),
            VM((D, tokens), bf16),
            dma_sems(n_slots),
            pltpu.SemaphoreType.DMA,
        ],
        flops=12 * tokens * D * FF,
    )
    low_out, grad_second, gain_three = feed_result[:3]
    grad_feed, _ = plan.reduce(feed_result[3:])
    outputs = plan.spread(tab, low_out.reshape(rows_held, length, D), rows_held)
    cross_result = call(
        functools.partial(cross_back_kernel, n_slots, n_pieces, n_outs, rows_held),
        [(tab, "smem")]
        + vmems(
            (
                target_segments,
                encoder_segments,
                gain_rows,
                grad_second,
                after_self,
                normed_two,
                q_two,
                k_two,
                v_two,
                mix_two,
                sum_two,
                source_rows,
            )
        )
        + anys(cross_slots),
        [shape(flat, f32), shape((1, D), f32)] + grad_outs(0, 4 * PAIR),
        [
            attn_weights,
            VM((D, tokens), bf16),
            VM((D, tokens), bf16),
            VM((D, tokens), bf16),
            VM((D, sources), bf16),
            VM((D, sources), bf16),
            VM((sources, PAIR), bf16),
            VM((sources, PAIR), bf16),
            dma_sems(n_slots),
        ],
        flops=4 * tokens * D * 2048 + 4 * sources * D * 1024,
    )
    grad_first, gain_two = cross_result[:2]
    grad_cross, _ = plan.reduce(cross_result[2:])
    self_result = call(
        functools.partial(self_back_kernel, n_slots, n_outs, rows_held),
        [(tab, "smem")]
        + vmems((target_segments, onehot, gain_rows, falls, gain_two, gain_three, grad_first))
        + anys([inputs])
        + vmems((normed_one, q_one, k_one, v_one, mix_one, sum_one))
        + anys(self_slots),
        [shape(flat, bf16)] + grad_outs(EXTRA, 4 * PAIR),
        [
            attn_weights,
            VM((rows_held, length, D), bf16),
            VM((D, tokens), bf16),
            VM((D, tokens), bf16),
            VM((D, tokens), bf16),
            VM((8, length), f32),
            dma_sems(n_slots),
            pltpu.SemaphoreType.DMA,
        ],
        flops=4 * tokens * D * 2048,
    )
    grad_self, tile = plan.reduce(self_result[1:])
    input_grad = plan.spread(tab, self_result[0].reshape(rows_held, length, D), rows_held)

    def kind(grads, number):
        return grads[:rows, number * columns : (number + 1) * columns]

    hidden = inner_weight.shape[1]
    grads = (
        jnp.stack((kind(grad_self, 0), kind(grad_cross, 0))),
        jnp.stack(
            (
                jnp.stack((kind(grad_self, 1), kind(grad_self, 2))),
                jnp.stack((kind(grad_cross, 1), kind(grad_cross, 2))),
            )
        ),
        jnp.stack((kind(grad_self, 3).T, kind(grad_cross, 3).T)),
        grad_feed[:, :hidden],
        grad_feed[:, hidden:].T,
        lax.dynamic_slice_in_dim(tile[0:3], place_dp * width, width, 1),
        lax.dynamic_slice(tile, (8 + place_mp * heads, place_dp * bands), (heads, bands)).T,
    )
    params = (
        query_weight,
        keyval_weight,
        output_weight,
        inner_weight,
        outer_weight,
        gains,
        bias_table,
    )
    firsts = (
        query_first,
        keyval_first,
        output_first,
        inner_first,
        outer_first,
        gains_first,
        table_first,
    )
    seconds = (
        query_second,
        keyval_second,
        output_second,
        inner_second,
        outer_second,
        gains_second,
        table_second,
    )
    updated = [
        adam_step(*param_entry)
        for param_entry in zip(params, firsts, seconds, grads, step_rates(), step_decays)
    ]
    return (outputs, input_grad) + tuple(array for triple in updated for array in triple)


def solution(mesh):
    n_dp, n_mp = mesh.shape["dp"], mesh.shape["mp"]
    plan = (TreePlan if (n_dp, n_mp) == (8, 4) else PlainPlan)(n_dp, n_mp)
    by_query, by_keyval = P(None, "dp", "mp"), P(None, None, "dp", "mp")
    by_output, by_inner, by_outer = P(None, "mp", "dp"), P("dp", "mp"), P("mp", "dp")
    weights = (by_query,) * 3 + (by_keyval,) * 3 + (by_output,) * 3 + (by_inner,) * 3
    weights = weights + (by_outer,) * 3 + (P(None, "dp"),) * 3 + (P("dp", "mp"),) * 3
    tokens = P("dp", None, None)
    return jax.shard_map(
        functools.partial(shards, plan),
        mesh=mesh,
        in_specs=(tokens, P("dp", "mp", None), tokens, P("dp", None), P("dp", None)) + weights,
        out_specs=(tokens, tokens) + weights,
        check_vma=False,
    )
```

time: 918 us -> 260 us (0.28)
  waiting for transfers between devices: 643 us -> 94.9 us
  blocking collectives: 80.3 us -> 0 us
  starting transfers between devices: 12.9 us -> 82 us
  matrix products: 63.2 us -> 0 us
  Pallas kernels: 0 us -> 58.2 us
  local copies, waits for them, and re-layouts: 50.4 us -> 9.49 us
  other arithmetic: 43.5 us -> 13.3 us
  between operations: 16.9 us -> 1.59 us
    psum x5 -> x0, waiting for transfers between devices: 460 us -> none  [the longest x3 310 us: add_heads(): return lax.psum(partial_value, 'mp')]
    ppermute x0 -> x57, waiting for transfers between devices: none -> 94.9 us  [the longest x27 58.9 us: hop_z(): return lax.ppermute(array, ALL, self.pairs(lambda d, m: (d, m ^ number)))]
    ppermute x0 -> x57, starting transfers between devices: none -> 82 us  [the longest x27 62 us: hop_z(): return lax.ppermute(array, ALL, self.pairs(lambda d, m: (d, m ^ number)))]
    all_gather x1 -> x0, waiting for transfers between devices: 77 us -> none  [shards(): encoder_full = lax.all_gather(encoder, 'mp', axis=1, tiled=True)]
    unnamed x12 -> x0, waiting for transfers between devices: 70.9 us -> none
    all_gather x7 -> x0, blocking collectives: 66.3 us -> none  [the longest x1 10.8 us: shards(): lax.all_gather(inner_weight.astype(jnp.bfloat16), 'dp', axis=0, tiled=True)]
    dot_general x50 -> x0, matrix products: 63.2 us -> none  [the longest x1 4.23 us: shards(): jnp.einsum('std,stkc->kdc', encoder_full, kv_grad, preferred_element_type...]
    pallas_call x0 -> x8, Pallas kernels: none -> 58.2 us  [call(): pl.pallas_call(kernel, out_shape=tuple(outs), in_specs=[pl.BlockSpec(memo...]
  transfers between devices with their start and end apart: 10 -> 57, of which waited for: 9 -> 17; matrix products, arithmetic and copies ran while one was open for 8% -> 5% of each run, Pallas kernels for 0% -> 12%
where the time goes in v1:
time: 260 us
  waiting for transfers between devices  94.9 us (36%)
  starting transfers between devices  82 us (32%)
  Pallas kernels  58.2 us (22%)
  other arithmetic  13.3 us (5%)
  local copies, waits for them, and re-layouts  9.49 us (4%)
    ppermute x27, starting transfers between devices, hop_z(): return lax.ppermute(array, ALL, self.pairs(lambda d, m: (d, m ^ number)))  62 us
    ppermute x27, waiting for transfers between devices, hop_z(): return lax.ppermute(array, ALL, self.pairs(lambda d, m: (d, m ^ number)))  58.9 us
    pallas_call x8, Pallas kernels, call(): pl.pallas_call(kernel, out_shape=tuple(outs), in_specs=[pl.BlockSpec(memo...  58.2 us
    ppermute x6, waiting for transfers between devices, hop_first(): lax.ppermute(array, ALL, self.pairs(lambda d, m: (d ^ (4 if d & 1 else 2)...  22.3 us
    ppermute x9, waiting for transfers between devices, hop_second(): lax.ppermute(array, ALL, self.pairs(lambda d, m: (d ^ (2 if d & 1 else 4)...  13.7 us
    ppermute x9, starting transfers between devices, hop_second(): lax.ppermute(array, ALL, self.pairs(lambda d, m: (d ^ (2 if d & 1 else 4)...  11 us
    ppermute x6, starting transfers between devices, hop_first(): lax.ppermute(array, ALL, self.pairs(lambda d, m: (d ^ (4 if d & 1 else 2)...  6.15 us
  transfers between devices with their start and end apart: 57, of which 17 were waited for; matrix products, arithmetic and copies ran while one was open for 5% of the time, Pallas kernels for 12%

profile of v1, /device:TPU:0, one launch (start us, length us, event | category | flops | bytes accessed | tf_op | source)
XLA Modules:
  0.0 259.5 jit_solution(1076846846445768991)
XLA Ops:
  5.2 3.1 %collective-permute-start.10 = (bf16[64,512]{1,0:T(8,128)(2,1)}, bf16[64,512]{1,0:T(8,128)(2,1)S(1)}, u32[]{:S(2)}, u32[]{:S(2)}) collective-permute-start(bf16[64,512]{1,0:T(8,128)(2,1)} %get-tuple-element.58), channel_id=1, source_target_pairs={{0,1},{1,0},{2,3},{3,2},{4,5},{5,4},{6,7},{7,6},{8,9},{9,8},{10,11... | collective-permute-start | bytes 196616 | tf_op jit(solution)/shard_map/ppermute | solution.py:587
  13.4 4.0 %collective-permute-start.2 = (bf16[80,512]{1,0:T(8,128)(2,1)}, bf16[80,512]{1,0:T(8,128)(2,1)S(1)}, u32[]{:S(2)}, u32[]{:S(2)}) collective-permute-start(bf16[80,512]{1,0:T(8,128)(2,1)} %get-tuple-element.55), channel_id=1, source_target_pairs={{0,3},{1,2},{2,1},{3,0},{4,7},{5,6},{6,5},{7,4},{8,11},{9,10},{10,... | collective-permute-start | bytes 245768 | tf_op jit(solution)/shard_map/ppermute | solution.py:587
  17.7 8.7 %collective-permute-done.12 = bf16[64,512]{1,0:T(8,128)(2,1)S(1)} collective-permute-done((bf16[64,512]{1,0:T(8,128)(2,1)}, bf16[64,512]{1,0:T(8,128)(2,1)S(1)}, u32[]{:S(2)}, u32[]{:S(2)}) %collective-permute-start.12) | collective-permute-done | bytes 65568 | tf_op jit(solution)/shard_map/ppermute | solution.py:587
  26.5 2.8 %collective-permute-start.24 = (bf16[64,1024]{1,0:T(8,128)(2,1)}, bf16[64,1024]{1,0:T(8,128)(2,1)S(1)}, u32[]{:S(2)}, u32[]{:S(2)}) collective-permute-start(bf16[64,1024]{1,0:T(8,128)(2,1)} %get-tuple-element.60), channel_id=1, source_target_pairs={{0,2},{1,3},{2,0},{3,1},{4,6},{5,7},{6,4},{7,5},{8,10},{9,11},{10,... | collective-permute-start | bytes 393224 | tf_op jit(solution)/shard_map/ppermute | solution.py:587
  35.4 15.0 %collective-permute-done.24 = bf16[64,1024]{1,0:T(8,128)(2,1)S(1)} collective-permute-done((bf16[64,1024]{1,0:T(8,128)(2,1)}, bf16[64,1024]{1,0:T(8,128)(2,1)S(1)}, u32[]{:S(2)}, u32[]{:S(2)}) %collective-permute-start.24) | collective-permute-done | bytes 131104 | tf_op jit(solution)/shard_map/ppermute | solution.py:587
  62.4 11.4 %collective-permute-done.3.refs_1_.refs_7_ = bf16[4,80,512]{2,1,0:T(8,128)(2,1)S(1)} collective-permute-done((bf16[4,80,512]{2,1,0:T(8,128)(2,1)S(1)}, bf16[4,80,512]{2,1,0:T(8,128)(2,1)S(1)}, u32[]{:S(2)}, u32[]{:S(2)}) %collective-permute-start.3) | collective-permute-done | bytes 327712 | tf_op jit(solution)/shard_map/ppermute | solution.py:593
  77.8 3.6 %collective-permute-done.5.refs_3_.refs_9_ = bf16[4,80,512]{2,1,0:T(8,128)(2,1)S(1)} collective-permute-done((bf16[4,80,512]{2,1,0:T(8,128)(2,1)S(1)}, bf16[4,80,512]{2,1,0:T(8,128)(2,1)S(1)}, u32[]{:S(2)}, u32[]{:S(2)}) %collective-permute-start.5) | collective-permute-done | bytes 327712 | tf_op jit(solution)/shard_map/ppermute | solution.py:596
  82.2 5.0 %collective-permute-done.27.refs_2_ = bf16[4,64,1024]{2,1,0:T(8,128)(2,1)} collective-permute-done((bf16[4,64,1024]{2,1,0:T(8,128)(2,1)S(1)}, bf16[4,64,1024]{2,1,0:T(8,128)(2,1)}, u32[]{:S(2)}, u32[]{:S(2)}) %collective-permute-start.27) | collective-permute-done | bytes 524320 | tf_op jit(solution)/shard_map/ppermute | solution.py:596
  87.8 5.0 %collective-permute-done.28.refs_3_ = bf16[4,64,1024]{2,1,0:T(8,128)(2,1)} collective-permute-done((bf16[4,64,1024]{2,1,0:T(8,128)(2,1)}, bf16[4,64,1024]{2,1,0:T(8,128)(2,1)}, u32[]{:S(2)}, u32[]{:S(2)}) %collective-permute-start.28) | collective-permute-done | bytes 524320 | tf_op jit(solution)/shard_map/ppermute | solution.py:596
  94.1 6.4 %shard_map.426 = (f32[256,512]{1,0:T(8,128)}, bf16[256,512]{1,0:T(8,128)(2,1)}, bf16[4,256,128]{2,1,0:T(8,128)(2,1)}, bf16[4,256,128]{2,1,0:T(8,128)(2,1)}, bf16...) custom-call(s32[32]{0:T(128)} %stack.145.tab, ...), custom_call_target="tpu_custom_call" | custom-call | flops 536870912 | bytes 5570688 | tf_op jit(solution)/shard_map/pallas_call | solution.py:528
  101.3 11.3 %shard_map.427 = (f32[256,512]{1,0:T(8,128)}, bf16[256,512]{1,0:T(8,128)(2,1)}, bf16[4,256,128]{2,1,0:T(8,128)(2,1)}, bf16[4,1024,128]{2,1,0:T(8,128)(2,1)}, bf1...) custom-call(s32[32]{0:T(128)} %stack.145.tab, ...), custom_call_target="tpu_custom_call" | custom-call | flops 1610612736 | bytes 8958080 | tf_op jit(solution)/shard_map/pallas_call | solution.py:528
  114.0 10.2 %shard_map.428 = (bf16[256,512]{1,0:T(8,128)(2,1)}, f32[256,512]{1,0:T(8,128)}, f32[1,512]{1,0:T(1,128)}, bf16[4,4,64,1024]{3,2,1,0:T(8,128)(2,1)}, bf16[4,4,64,1024]{3,2,1,0:T(8,128)(2,1)}) custom-call(s32[32]{0:T(128)} %stack.145.tab, f32[8,512]{1,0:T(8,128)} %get-tuple-element.56.gains, f32[256,512]{1,0:T(8,128)} %get-tuple-element.59.before, ...), custom_call_target="tpu_custom_call" | custom-call | flops 3221225472 | bytes 10766464 | tf_op jit(solution)/shard_map/pallas_call | solution.py:528
  124.3 13.9 %shard_map.430 = (f32[256,512]{1,0:T(8,128)}, f32[1,512]{1,0:T(1,128)}, bf16[4,4,64,512]{3,2,1,0:T(8,128)(2,1)}, bf16[4,4,64,512]{3,2,1,0:T(8,128)(2,1)}) custom-call(s32[32]{0:T(128)} %stack.145.tab, s32[8,128]{1,0:T(8,128)} %targets.7, s32[8,512]{1,0:T(8,128)} %sources.3, f32[8,512]{1,0:T(8,128)} %get-tuple-element.56.gains, ...), custom_call_target="tpu_custom_call" | custom-call | flops 3221225472 | bytes 9746560 | tf_op jit(solution)/shard_map/pallas_call | solution.py:528
  138.3 10.0 %shard_map.431 = (bf16[256,512]{1,0:T(8,128)(2,1)}, bf16[4,4,80,512]{3,2,1,0:T(8,128)(2,1)}, bf16[4,4,80,512]{3,2,1,0:T(8,128)(2,1)}) custom-call(s32[32]{0:T(128)} %stack.145.tab, s32[8,128]{1,0:T(8,128)} %targets.7, bf16[128,128]{1,0:T(8,128)(2,1)} %fusion.20.onehot, f32[8,512]{1,0:T(8,128)} %get-tuple-element.56.gains, f32[8,128]{1,0:T(8,128)} %get-tuple-element.62.falls, ...), custom_call_target="tpu_custom_call" | custom-call | flops 1073741824 | bytes 8458368 | tf_op jit(solution)/shard_map/pallas_call | solution.py:528
  150.2 7.6 %collective-permute-start.36 = (bf16[2,128,512]{2,1,0:T(8,128)(2,1)S(1)}, bf16[2,128,512]{2,1,0:T(8,128)(2,1)S(1)}, u32[]{:S(2)}, u32[]{:S(2)}) collective-permute-start(bf16[2,128,512]{2,1,0:T(8,128)(2,1)S(1)} %bitcast.140), channel_id=1, source_target_pairs={{0,1},{1,0},{2,3},{3,2},{4,5},{5,4},{6,7},{7,6},{8,9},{9,8},{10,11... | collective-permute-start | bytes 786440 | tf_op jit(solution)/shard_map/ppermute | solution.py:587
  163.2 5.4 %collective-permute-done.36.refs_1_ = bf16[2,128,512]{2,1,0:T(8,128)(2,1)S(1)} collective-permute-done((bf16[2,128,512]{2,1,0:T(8,128)(2,1)S(1)}, bf16[2,128,512]{2,1,0:T(8,128)(2,1)S(1)}, u32[]{:S(2)}, u32[]{:S(2)}) %collective-permute-start.36) | collective-permute-done | bytes 262176 | tf_op jit(solution)/shard_map/ppermute | solution.py:587
  168.7 10.5 %collective-permute-done.37.refs_2_ = bf16[2,128,512]{2,1,0:T(8,128)(2,1)S(1)} collective-permute-done((bf16[2,128,512]{2,1,0:T(8,128)(2,1)S(1)}, bf16[2,128,512]{2,1,0:T(8,128)(2,1)S(1)}, u32[]{:S(2)}, u32[]{:S(2)}) %collective-permute-start.37) | collective-permute-done | bytes 262176 | tf_op jit(solution)/shard_map/ppermute | solution.py:587
  183.4 14.3 %collective-permute-start.48 = (bf16[64,512]{1,0:T(8,128)(2,1)}, bf16[64,512]{1,0:T(8,128)(2,1)S(1)}, u32[]{:S(2)}, u32[]{:S(2)}) collective-permute-start(bf16[64,512]{1,0:T(8,128)(2,1)} %get-tuple-element.123), channel_id=1, source_target_pairs={{0,1},{1,0},{2,3},{3,2},{4,5},{5,4},{6,7},{7,6},{8,9},{9,8},{10,11... | collective-permute-start | bytes 196616 | tf_op jit(solution)/shard_map/ppermute | solution.py:587
  197.8 3.9 %collective-permute-done.34.refs_2_ = bf16[2,128,512]{2,1,0:T(8,128)(2,1)S(1)} collective-permute-done((bf16[2,128,512]{2,1,0:T(8,128)(2,1)S(1)}, bf16[2,128,512]{2,1,0:T(8,128)(2,1)S(1)}, u32[]{:S(2)}, u32[]{:S(2)}) %collective-permute-start.34) | collective-permute-done | bytes 262176 | tf_op jit(solution)/shard_map/ppermute | solution.py:587
  216.5 3.7 %collective-permute-done.41 = bf16[4,80,512]{2,1,0:T(8,128)(2,1)S(1)} collective-permute-done((bf16[4,80,512]{2,1,0:T(8,128)(2,1)S(1)}, bf16[4,80,512]{2,1,0:T(8,128)(2,1)S(1)}, u32[]{:S(2)}, u32[]{:S(2)}) %collective-permute-start.41) | collective-permute-done | bytes 327712 | tf_op jit(solution)/shard_map/ppermute | solution.py:593
  220.4 6.8 %collective-permute-start.42 = (bf16[80,512]{1,0:T(8,128)(2,1)S(1)}, bf16[80,512]{1,0:T(8,128)(2,1)S(1)}, u32[]{:S(2)}, u32[]{:S(2)}) collective-permute-start(bf16[80,512]{1,0:T(8,128)(2,1)S(1)} %get-tuple-element.120), channel_id=1, source_target_pairs={{0,1},{1,0},{2,3},{3,2},{4,5},{5,4},{6,7},{7,6},{8,9},{9,8},{10,11... | collective-permute-start | bytes 245768 | tf_op jit(solution)/shard_map/ppermute | solution.py:587
  229.7 4.3 %collective-permute-done.43 = bf16[80,512]{1,0:T(8,128)(2,1)S(1)} collective-permute-done((bf16[80,512]{1,0:T(8,128)(2,1)S(1)}, bf16[80,512]{1,0:T(8,128)(2,1)S(1)}, u32[]{:S(2)}, u32[]{:S(2)}) %collective-permute-start.43) | collective-permute-done | bytes 81952 | tf_op jit(solution)/shard_map/ppermute | solution.py:587
  237.9 7.3 %collective-permute-done.53 = bf16[4,64,1024]{2,1,0:T(8,128)(2,1)S(1)} collective-permute-done((bf16[4,64,1024]{2,1,0:T(8,128)(2,1)S(1)}, bf16[4,64,1024]{2,1,0:T(8,128)(2,1)S(1)}, u32[]{:S(2)}, u32[]{:S(2)}) %collective-permute-start.53) | collective-permute-done | bytes 524320 | tf_op jit(solution)/shard_map/ppermute | solution.py:593
  250.9 6.9 %collective-permute-done.55 = bf16[64,1024]{1,0:T(8,128)(2,1)S(1)} collective-permute-done((bf16[64,1024]{1,0:T(8,128)(2,1)S(1)}, bf16[64,1024]{1,0:T(8,128)(2,1)S(1)}, u32[]{:S(2)}, u32[]{:S(2)}) %collective-permute-start.55) | collective-permute-done | bytes 131104 | tf_op jit(solution)/shard_map/ppermute | solution.py:587
  (270 shorter events, 76.7 us)
Async XLA Ops:
  10.9 42.5 %collective-permute-start.20 = (bf16[2,128,512]{2,1,0:T(8,128)(2,1)S(1)}, bf16[2,128,512]{2,1,0:T(8,128)(2,1)S(1)}, u32[]{:S(2)}, u32[]{:S(2)}) collective-permute-start(bf16[2,128,512]{2,1,0:T(8,128)(2,1)S(1)} %get-tuple-element.116), channel_id=1, source_target_pairs={{0,1},{1,0},{2,3},{3,2},{4,5},{5,4},{6,7},{7,6},{8,9},{9,8},{10,11... | collective-permute-start | bytes 786440 | tf_op jit(solution)/shard_map/ppermute | solution.py:587
  13.0 16.3 %collective-permute-start.1 = (bf16[80,512]{1,0:T(8,128)(2,1)}, bf16[80,512]{1,0:T(8,128)(2,1)S(1)}, u32[]{:S(2)}, u32[]{:S(2)}) collective-permute-start(bf16[80,512]{1,0:T(8,128)(2,1)} %get-tuple-element.55), channel_id=1, source_target_pairs={{0,2},{1,3},{2,0},{3,1},{4,6},{5,7},{6,4},{7,5},{8,10},{9,11},{10,... | collective-permute-start | bytes 245768 | tf_op jit(solution)/shard_map/ppermute | solution.py:587
  13.4 16.0 %collective-permute-start.2 = (bf16[80,512]{1,0:T(8,128)(2,1)}, bf16[80,512]{1,0:T(8,128)(2,1)S(1)}, u32[]{:S(2)}, u32[]{:S(2)}) collective-permute-start(bf16[80,512]{1,0:T(8,128)(2,1)} %get-tuple-element.55), channel_id=1, source_target_pairs={{0,3},{1,2},{2,1},{3,0},{4,7},{5,6},{6,5},{7,4},{8,11},{9,10},{10,... | collective-permute-start | bytes 245768 | tf_op jit(solution)/shard_map/ppermute | solution.py:587
  26.5 23.9 %collective-permute-start.24 = (bf16[64,1024]{1,0:T(8,128)(2,1)}, bf16[64,1024]{1,0:T(8,128)(2,1)S(1)}, u32[]{:S(2)}, u32[]{:S(2)}) collective-permute-start(bf16[64,1024]{1,0:T(8,128)(2,1)} %get-tuple-element.60), channel_id=1, source_target_pairs={{0,2},{1,3},{2,0},{3,1},{4,6},{5,7},{6,4},{7,5},{8,10},{9,11},{10,... | collective-permute-start | bytes 393224 | tf_op jit(solution)/shard_map/ppermute | solution.py:587
  29.3 26.7 %collective-permute-start.21 = (bf16[2,128,512]{2,1,0:T(8,128)(2,1)S(1)}, bf16[2,128,512]{2,1,0:T(8,128)(2,1)S(1)}, u32[]{:S(2)}, u32[]{:S(2)}) collective-permute-start(bf16[2,128,512]{2,1,0:T(8,128)(2,1)S(1)} %get-tuple-element.115), channel_id=1, source_target_pairs={{0,2},{1,3},{2,0},{3,1},{4,6},{5,7},{6,4},{7,5},{8,10},{9,11},{10,... | collective-permute-start | bytes 786440 | tf_op jit(solution)/shard_map/ppermute | solution.py:587
  29.4 22.5 %collective-permute-start.25 = (bf16[64,1024]{1,0:T(8,128)(2,1)}, bf16[64,1024]{1,0:T(8,128)(2,1)S(1)}, u32[]{:S(2)}, u32[]{:S(2)}) collective-permute-start(bf16[64,1024]{1,0:T(8,128)(2,1)} %get-tuple-element.60), channel_id=1, source_target_pairs={{0,3},{1,2},{2,1},{3,0},{4,7},{5,6},{6,5},{7,4},{8,11},{9,10},{10,... | collective-permute-start | bytes 393224 | tf_op jit(solution)/shard_map/ppermute | solution.py:587
  33.6 24.0 %collective-permute-start.22 = (bf16[2,128,512]{2,1,0:T(8,128)(2,1)S(1)}, bf16[2,128,512]{2,1,0:T(8,128)(2,1)S(1)}, u32[]{:S(2)}, u32[]{:S(2)}) collective-permute-start(bf16[2,128,512]{2,1,0:T(8,128)(2,1)S(1)} %get-tuple-element.114), channel_id=1, source_target_pairs={{0,3},{1,2},{2,1},{3,0},{4,7},{5,6},{6,5},{7,4},{8,11},{9,10},{10,... | collective-permute-start | bytes 786440 | tf_op jit(solution)/shard_map/ppermute | solution.py:587
  56.0 20.4 %collective-permute-start.26 = (bf16[4,64,1024]{2,1,0:T(8,128)(2,1)S(1)}, bf16[4,64,1024]{2,1,0:T(8,128)(2,1)}, u32[]{:S(2)}, u32[]{:S(2)}) collective-permute-start(bf16[4,64,1024]{2,1,0:T(8,128)(2,1)S(1)} %pad_maximum_fusion.refs_0_), channel_id=1, source_target_pairs={{0,8},{1,9},{2,10},{3,11},{4,20},{5,21},{6,22},{7,23},{8,0},{9,1},... | collective-permute-start | bytes 1572872 | tf_op jit(solution)/shard_map/ppermute | solution.py:593
  57.6 16.2 %collective-permute-start.3 = (bf16[4,80,512]{2,1,0:T(8,128)(2,1)S(1)}, bf16[4,80,512]{2,1,0:T(8,128)(2,1)S(1)}, u32[]{:S(2)}, u32[]{:S(2)}) collective-permute-start(bf16[4,80,512]{2,1,0:T(8,128)(2,1)S(1)} %pad_maximum_fusion.1.refs_0_.refs_6_), channel_id=1, source_target_pairs={{0,8},{1,9},{2,10},{3,11},{4,20},{5,21},{6,22},{7,23},{8,0},{9,1},... | collective-permute-start | bytes 983048 | tf_op jit(solution)/shard_map/ppermute | solution.py:593
  76.4 16.4 %collective-permute-start.28 = (bf16[4,64,1024]{2,1,0:T(8,128)(2,1)}, bf16[4,64,1024]{2,1,0:T(8,128)(2,1)}, u32[]{:S(2)}, u32[]{:S(2)}) collective-permute-start(bf16[4,64,1024]{2,1,0:T(8,128)(2,1)} %collective-permute-done.26.refs_1_), channel_id=1, source_target_pairs={{0,16},{1,17},{2,18},{3,19},{4,12},{5,13},{6,14},{7,15},{8,24},{9,... | collective-permute-start | bytes 1572872 | tf_op jit(solution)/shard_map/ppermute | solution.py:596
  87.2 25.4 %collective-permute-start.29 = (bf16[4,64,1024]{2,1,0:T(8,128)(2,1)S(1)}, bf16[4,64,1024]{2,1,0:T(8,128)(2,1)S(1)}, u32[]{:S(2)}, u32[]{:S(2)}) collective-permute-start(bf16[4,64,1024]{2,1,0:T(8,128)(2,1)S(1)} %pad_maximum_fusion.refs_0_), channel_id=1, source_target_pairs={{0,4},{1,5},{2,6},{3,7},{4,0},{5,1},{6,2},{7,3},{8,12},{9,13},{10,... | collective-permute-start | bytes 1572872 | tf_op jit(solution)/shard_map/ppermute | solution.py:590
  87.2 25.4 %collective-permute-start.30 = (bf16[4,64,1024]{2,1,0:T(8,128)(2,1)}, bf16[4,64,1024]{2,1,0:T(8,128)(2,1)S(1)}, u32[]{:S(2)}, u32[]{:S(2)}) collective-permute-start(bf16[4,64,1024]{2,1,0:T(8,128)(2,1)} %collective-permute-done.26.refs_1_), channel_id=1, source_target_pairs={{0,4},{1,5},{2,6},{3,7},{4,0},{5,1},{6,2},{7,3},{8,12},{9,13},{10,... | collective-permute-start | bytes 1572872 | tf_op jit(solution)/shard_map/ppermute | solution.py:590
  87.7 24.9 %collective-permute-start.31 = (bf16[4,64,1024]{2,1,0:T(8,128)(2,1)}, bf16[4,64,1024]{2,1,0:T(8,128)(2,1)S(1)}, u32[]{:S(2)}, u32[]{:S(2)}) collective-permute-start(bf16[4,64,1024]{2,1,0:T(8,128)(2,1)} %collective-permute-done.27.refs_2_), channel_id=1, source_target_pairs={{0,4},{1,5},{2,6},{3,7},{4,0},{5,1},{6,2},{7,3},{8,12},{9,13},{10,... | collective-permute-start | bytes 1572872 | tf_op jit(solution)/shard_map/ppermute | solution.py:590
  92.8 19.9 %collective-permute-start.32 = (bf16[4,64,1024]{2,1,0:T(8,128)(2,1)}, bf16[4,64,1024]{2,1,0:T(8,128)(2,1)S(1)}, u32[]{:S(2)}, u32[]{:S(2)}) collective-permute-start(bf16[4,64,1024]{2,1,0:T(8,128)(2,1)} %collective-permute-done.28.refs_3_), channel_id=1, source_target_pairs={{0,4},{1,5},{2,6},{3,7},{4,0},{5,1},{6,2},{7,3},{8,12},{9,13},{10,... | collective-permute-start | bytes 1572872 | tf_op jit(solution)/shard_map/ppermute | solution.py:590
  150.2 18.4 %collective-permute-start.36 = (bf16[2,128,512]{2,1,0:T(8,128)(2,1)S(1)}, bf16[2,128,512]{2,1,0:T(8,128)(2,1)S(1)}, u32[]{:S(2)}, u32[]{:S(2)}) collective-permute-start(bf16[2,128,512]{2,1,0:T(8,128)(2,1)S(1)} %bitcast.140), channel_id=1, source_target_pairs={{0,1},{1,0},{2,3},{3,2},{4,5},{5,4},{6,7},{7,6},{8,9},{9,8},{10,11... | collective-permute-start | bytes 786440 | tf_op jit(solution)/shard_map/ppermute | solution.py:587
  157.8 21.4 %collective-permute-start.37 = (bf16[2,128,512]{2,1,0:T(8,128)(2,1)S(1)}, bf16[2,128,512]{2,1,0:T(8,128)(2,1)S(1)}, u32[]{:S(2)}, u32[]{:S(2)}) collective-permute-start(bf16[2,128,512]{2,1,0:T(8,128)(2,1)S(1)} %bitcast.141), channel_id=1, source_target_pairs={{0,2},{1,3},{2,0},{3,1},{4,6},{5,7},{6,4},{7,5},{8,10},{9,11},{10,... | collective-permute-start | bytes 786440 | tf_op jit(solution)/shard_map/ppermute | solution.py:587
  158.4 23.7 %collective-permute-start.38 = (bf16[2,128,512]{2,1,0:T(8,128)(2,1)S(1)}, bf16[2,128,512]{2,1,0:T(8,128)(2,1)S(1)}, u32[]{:S(2)}, u32[]{:S(2)}) collective-permute-start(bf16[2,128,512]{2,1,0:T(8,128)(2,1)S(1)} %bitcast.142), channel_id=1, source_target_pairs={{0,3},{1,2},{2,1},{3,0},{4,7},{5,6},{6,5},{7,4},{8,11},{9,10},{10,... | collective-permute-start | bytes 786440 | tf_op jit(solution)/shard_map/ppermute | solution.py:587
  160.1 52.7 %collective-permute-start.51 = (bf16[4,4,64,1024]{3,2,1,0:T(8,128)(2,1)}, bf16[4,4,64,1024]{3,2,1,0:T(8,128)(2,1)}, u32[]{:S(2)}, u32[]{:S(2)}) collective-permute-start(bf16[4,4,64,1024]{3,2,1,0:T(8,128)(2,1)} %get-tuple-element.85), channel_id=1, source_target_pairs={{0,4},{1,5},{2,6},{3,7},{4,0},{5,1},{6,2},{7,3},{8,12},{9,13},{10,... | collective-permute-start | bytes 6291464 | tf_op jit(solution)/shard_map/ppermute | solution.py:590
  160.4 18.8 %collective-permute-start.47 = (bf16[4,64,512]{2,1,0:T(8,128)(2,1)S(1)}, bf16[4,64,512]{2,1,0:T(8,128)(2,1)S(1)}, u32[]{:S(2)}, u32[]{:S(2)}) collective-permute-start(bf16[4,64,512]{2,1,0:T(8,128)(2,1)S(1)} %fusion.5), channel_id=1, source_target_pairs={{0,8},{1,9},{2,10},{3,11},{4,20},{5,21},{6,22},{7,23},{8,0},{9,1},... | collective-permute-start | bytes 786440 | tf_op jit(solution)/shard_map/ppermute | solution.py:593
  179.2 22.5 %collective-permute-start.34 = (bf16[2,128,512]{2,1,0:T(8,128)(2,1)S(1)}, bf16[2,128,512]{2,1,0:T(8,128)(2,1)S(1)}, u32[]{:S(2)}, u32[]{:S(2)}) collective-permute-start(bf16[2,128,512]{2,1,0:T(8,128)(2,1)S(1)} %bitcast.137), channel_id=1, source_target_pairs={{0,2},{1,3},{2,0},{3,1},{4,6},{5,7},{6,4},{7,5},{8,10},{9,11},{10,... | collective-permute-start | bytes 786440 | tf_op jit(solution)/shard_map/ppermute | solution.py:587
  179.9 21.8 %collective-permute-start.35 = (bf16[2,128,512]{2,1,0:T(8,128)(2,1)S(1)}, bf16[2,128,512]{2,1,0:T(8,128)(2,1)S(1)}, u32[]{:S(2)}, u32[]{:S(2)}) collective-permute-start(bf16[2,128,512]{2,1,0:T(8,128)(2,1)S(1)} %bitcast.138), channel_id=1, source_target_pairs={{0,3},{1,2},{2,1},{3,0},{4,7},{5,6},{6,5},{7,4},{8,11},{9,10},{10,... | collective-permute-start | bytes 786440 | tf_op jit(solution)/shard_map/ppermute | solution.py:587
  182.2 28.1 %collective-permute-start.40 = (bf16[2,4,80,512]{3,2,1,0:T(8,128)(2,1)}, bf16[2,4,80,512]{3,2,1,0:T(8,128)(2,1)}, u32[]{:S(2)}, u32[]{:S(2)}) collective-permute-start(bf16[2,4,80,512]{3,2,1,0:T(8,128)(2,1)} %slice.257), channel_id=1, source_target_pairs={{0,16},{1,17},{2,18},{3,19},{4,12},{5,13},{6,14},{7,15},{8,24},{9,... | collective-permute-start | bytes 1966088 | tf_op jit(solution)/shard_map/ppermute | solution.py:596
  183.4 25.8 %collective-permute-start.48 = (bf16[64,512]{1,0:T(8,128)(2,1)}, bf16[64,512]{1,0:T(8,128)(2,1)S(1)}, u32[]{:S(2)}, u32[]{:S(2)}) collective-permute-start(bf16[64,512]{1,0:T(8,128)(2,1)} %get-tuple-element.123), channel_id=1, source_target_pairs={{0,1},{1,0},{2,3},{3,2},{4,5},{5,4},{6,7},{7,6},{8,9},{9,8},{10,11... | collective-permute-start | bytes 196616 | tf_op jit(solution)/shard_map/ppermute | solution.py:587
  215.6 19.9 %collective-permute-start.52 = (bf16[2,4,64,1024]{3,2,1,0:T(8,128)(2,1)S(1)}, bf16[2,4,64,1024]{3,2,1,0:T(8,128)(2,1)S(1)}, u32[]{:S(2)}, u32[]{:S(2)}) collective-permute-start(bf16[2,4,64,1024]{3,2,1,0:T(8,128)(2,1)S(1)} %slice.256), channel_id=1, source_target_pairs={{0,16},{1,17},{2,18},{3,19},{4,12},{5,13},{6,14},{7,15},{8,24},{9,... | collective-permute-start | bytes 3145736 | tf_op jit(solution)/shard_map/ppermute | solution.py:596
  (92 other events, 1086.5 us)

commit v2 on v1

v2 whole, which is shorter than its diff:
```python
import functools
import math

import jax
import jax.numpy as jnp
import numpy as np
from jax import lax
from jax.experimental import pallas as pl
from jax.experimental.pallas import tpu as pltpu
from jax.sharding import PartitionSpec as P

D = 512
HEADS = 8
HEAD_DIM = 64
FF = 2048
NB = 32
HD = 512
STEP = 10
PAIRS = HEADS // 2
PAIR = 2 * HEAD_DIM
HIDDEN = FF // PAIRS
EXTRA = 16
GROUPS = tuple((i, i + 1) for i in range(0, PAIRS, 2))
VMEM_BYTES = 56 * 1024 * 1024

norm_eps = 1e-06
beta_first = 0.9
beta_second = 0.95
adam_eps = 1e-08
decay_weight = 0.1
rate_factor = 0.6
masked_value = -1000000000.0
bucket_edges = tuple((math.ceil(16 * 8 ** (number / 16)) for number in range(1, 16)))
step_decays = (decay_weight, decay_weight, decay_weight, decay_weight, decay_weight, 0.0, 0.0)
gelu_slope = math.sqrt(2.0 / math.pi)
gelu_cubic = 0.044715

f32 = jnp.float32
bf16 = jnp.bfloat16
ALL = ("dp", "mp")
VM = pltpu.VMEM


def dot_nn(a, b):
    return lax.dot_general(a, b, (((1,), (0,)), ((), ())), preferred_element_type=f32)


def dot_nt(a, b):
    return lax.dot_general(a, b, (((1,), (1,)), ((), ())), preferred_element_type=f32)


def dot_tn(a, b):
    return lax.dot_general(a, b, (((0,), (0,)), ((), ())), preferred_element_type=f32)


def root_scale(values):
    return lax.rsqrt(jnp.mean(values * values, axis=-1, keepdims=True) + norm_eps)


def root_back(values, gain, grad):
    scale = root_scale(values)
    grad_gain = jnp.sum(grad * values * scale, axis=0, keepdims=True)
    weighted = grad * gain
    along = jnp.sum(weighted * values, axis=-1, keepdims=True)
    inverse = 1.0 / values.shape[-1]
    return scale * weighted - values * (scale * scale * scale * along * inverse), grad_gain


def stack_heads(pair):
    lane = lax.broadcasted_iota(jnp.int32, pair.shape, 1)
    zero = jnp.zeros_like(pair)
    return jnp.concatenate(
        (jnp.where(lane < HEAD_DIM, pair, zero), jnp.where(lane >= HEAD_DIM, pair, zero)), axis=0
    )


def unstack_heads(stacked):
    half = stacked.shape[0] // 2
    top, bottom = stacked[:half], stacked[half:]
    lane = lax.broadcasted_iota(jnp.int32, top.shape, 1)
    return jnp.where(lane < HEAD_DIM, top, bottom)


def column_of(row):
    return jnp.transpose(jnp.broadcast_to(row, (128, row.shape[1])))


def doubled(mask_value):
    return jnp.concatenate((mask_value, mask_value), axis=1)


def masked_scores(units):
    scores = [dot_nt(key, query) for query, key, _, _ in units]
    scores = [s if unit[2] is None else s + unit[2] for s, unit in zip(scores, units)]
    return [jnp.where(unit[3], s, masked_value) for s, unit in zip(scores, units)]


def attend(units):
    scores = masked_scores([(stack_heads(u[0]), u[1], u[3], u[4]) for u in units])
    peaks = [jnp.max(s, axis=0, keepdims=True) for s in scores]
    terms = [jnp.exp(s - peak) for s, peak in zip(scores, peaks)]
    sums = [jnp.sum(t, axis=0, keepdims=True) for t in terms]
    probs = [(t * (1.0 / total)).astype(bf16) for t, total in zip(terms, sums)]
    mixes = [dot_tn(p, u[2]) for p, u in zip(probs, units)]
    mixes = [unstack_heads(m).astype(bf16) for m in mixes]
    return mixes, [peak + jnp.log(total) for peak, total in zip(peaks, sums)]


def attend_back(units):
    queries = [stack_heads(u[0]) for u in units]
    grads = [stack_heads(u[6]) for u in units]
    scores = masked_scores([(q, u[1], u[3], u[4]) for q, u in zip(queries, units)])
    grad_probs = [dot_nt(u[2], g) for u, g in zip(units, grads)]
    probs = [jnp.exp(s - u[5]) for s, u in zip(scores, units)]
    grad_values = [dot_nn(p.astype(bf16), g).astype(bf16) for p, g in zip(probs, grads)]
    along = [jnp.sum(g * p, axis=0, keepdims=True) for g, p in zip(grad_probs, probs)]
    grad_scores = [p * (g - t) for p, g, t in zip(probs, grad_probs, along)]
    low = [g.astype(bf16) for g in grad_scores]
    grad_keys = [dot_nn(x, q).astype(bf16) for x, q in zip(low, queries)]
    grad_queries = [unstack_heads(dot_tn(x, u[1])).astype(bf16) for x, u in zip(low, units)]
    return grad_queries, grad_keys, grad_values, grad_scores


def weight_copies(slots, weights, tab, sems, first=0):
    copies = []
    for pair in range(PAIRS):
        row = []
        for number, slot in enumerate(slots):
            rows = weights.shape[1] // len(slots)
            start = pl.multiple_of(tab[number] * rows, rows)
            row.append(
                pltpu.make_async_copy(
                    slot.at[pair, pl.ds(0, rows), pl.ds(first, weights.shape[2])],
                    weights.at[pair, pl.ds(start, rows), :],
                    sems.at[number, pair],
                )
            )
        copies.append(row)
    for row in copies:
        for copy in row:
            copy.start()
    return copies


def wait_for(copies):
    for copy in copies:
        copy.wait()


def extra_copies(slots, extras, rows, sems):
    return [
        pltpu.make_async_copy(slot.at[:, pl.ds(rows, EXTRA), pl.ds(0, D)], extras.at[number], sems.at[number])
        for number, slot in enumerate(slots)
    ]


def permute_rows(source, target, tab, n_slots):
    rows = source.shape[0] // n_slots
    for number in range(n_slots):
        start = pl.multiple_of(tab[number] * rows, rows)
        target[number * rows : (number + 1) * rows, :] = source[pl.ds(start, rows), :]


class SlotWriter:
    def __init__(self, outs, held, sems):
        self.outs, self.held, self.sems = outs, held, sems
        self.copies = []

    def send(self, pair, first, rows, sem):
        begin = 0
        for place, out in enumerate(self.outs):
            copy = pltpu.make_async_copy(
                self.held.at[pl.ds(begin, out.shape[0]), pair, pl.ds(first, rows), :],
                out.at[:, pair, pl.ds(first, rows), :],
                self.sems.at[place, sem],
            )
            copy.start()
            self.copies.append(copy)
            begin += out.shape[0]

    def write(self, pair, grads):
        n_slots = self.held.shape[0]
        first = 0
        for grad in grads:
            rows, width = grad.shape[0] // n_slots, grad.shape[1]
            low = grad.astype(bf16)
            for number in range(n_slots):
                part = low[number * rows : (number + 1) * rows]
                self.held[number, pair, 0:rows, first : first + width] = part
            first += width
        self.send(pair, 0, rows, pair)

    def finish(self):
        wait_for(self.copies)


def toeplitz(row, length):
    return pltpu.roll(jnp.broadcast_to(row, (length, row.shape[1])), 0, 1, stride=1, stride_axis=0)


def bias_of(tab, falls, pair, length):
    head = tab[16 + pair] * 2
    return jnp.concatenate(
        [toeplitz(falls[pl.ds(head + side, 1), :], length) for side in range(2)], axis=1
    )


def fold_diagonals(grad):
    length = grad.shape[1]
    folded = grad[0:8]
    for start in range(8, grad.shape[0], 8):
        folded = folded + pltpu.roll(grad[start : start + 8], length - start, 1)
    row = lax.broadcasted_iota(jnp.int32, folded.shape, 0)
    for bit in (1, 2, 4):
        folded = jnp.where(row & bit != 0, pltpu.roll(folded, length - bit, 1), folded)
    return jnp.sum(folded, axis=0, keepdims=True)


def self_masks(tab, targets, row, length):
    segments = targets[pl.ds(tab[24] + row, 1), :].astype(f32)
    column = column_of(segments)
    keys = lax.broadcasted_iota(jnp.int32, (length, length), 0)
    queries = lax.broadcasted_iota(jnp.int32, (length, length), 1)
    return doubled(
        jnp.where((column == segments) & (queries >= keys), 1.0, 0.0)
    ) > 0.5


def cross_masks(tab, targets, sources, row, n_pieces, piece_tab):
    segments = targets[pl.ds(tab[24] + row, 1), :].astype(f32)
    width = sources.shape[1] // n_pieces
    chosen = lax.broadcasted_iota(jnp.int32, (sources.shape[0], width), 0) == tab[24] + row
    parts = []
    for i in range(n_pieces):
        start = pl.multiple_of(tab[piece_tab + i] * width, 128)
        slab = sources[:, pl.ds(start, width)].astype(f32)
        parts.append(jnp.sum(jnp.where(chosen, slab, 0.0), axis=0, keepdims=True))
    column = column_of(jnp.concatenate(parts, axis=1) if n_pieces > 1 else parts[0])
    return doubled(jnp.where(column == segments, 1.0, 0.0)) > 0.5


def self_forward_kernel(n_slots, n_after, rows_held, tab, targets, onehot, x_all, *refs):
    slots, refs = refs[:n_slots], refs[n_slots + n_after :]
    after, normed, query, key, value, mixed, totals, gains, falls = refs[:9]
    weights, extras, x_rows, sems, extra_sems, x_sem = refs[9:]
    length = x_all.shape[1]
    fetch_x = pltpu.make_async_copy(x_all.at[pl.ds(tab[24], rows_held)], x_rows, x_sem)
    fetch_extra = extra_copies(slots, extras, D // n_slots, extra_sems)
    for copy in [fetch_x] + fetch_extra:
        copy.start()
    fetch = weight_copies(slots, weights, tab, sems)
    wait_for(fetch_extra)
    tile = jnp.zeros((EXTRA, D), f32)
    for number in range(n_slots):
        for pair in range(PAIRS):
            tile = tile + extras[number, pair].astype(f32)
    gains[...] = tile[0:8]
    falls[...] = dot_nn(tile[8:16, 0:128].astype(bf16), onehot[...])
    fetch_x.wait()
    resident = x_rows[...].reshape(rows_held * length, D).astype(f32)
    low = (resident * root_scale(resident) * tile[0:1]).astype(bf16)
    normed[...] = low
    allowed = [self_masks(tab, targets, row, length) for row in range(rows_held)]
    total = resident
    for group in GROUPS:
        for pair in group:
            wait_for(fetch[pair])
            projected = dot_nn(low, weights[pair, :, 0 : 3 * PAIR]).astype(bf16)
            query[pair] = projected[:, 0:PAIR]
            key[pair] = projected[:, PAIR : 2 * PAIR]
            value[pair] = projected[:, 2 * PAIR :]
        places = [(pair, row, slice(row * length, (row + 1) * length)) for pair in group for row in range(rows_held)]
        biases = {pair: bias_of(tab, falls, pair, length) for pair in group}
        mixes, logs = attend(
            [
                (query[pair, span], key[pair, span], value[pair, span], biases[pair], allowed[row])
                for pair, row, span in places
            ]
        )
        for (pair, row, span), mix, log_total in zip(places, mixes, logs):
            mixed[pair, span] = mix
            totals[pair, row : row + 1, :] = log_total
        for pair in group:
            total = total + dot_nt(mixed[pair], weights[pair, :, 3 * PAIR :])
    after[...] = total


def encoder_copies(pieces, encoder, tab, rows_held, sems):
    width = encoder.shape[1] // len(pieces)
    copies = []
    for number, piece in enumerate(pieces):
        start = tab[24] if piece.shape[0] > rows_held else 0
        copies.append(
            pltpu.make_async_copy(
                piece.at[pl.ds(start, rows_held)],
                encoder.at[:, pl.ds(number * width, width), :],
                sems.at[number],
            )
        )
    return copies


def cross_forward_kernel(n_slots, n_pieces, rows_held, tab, targets, sources, gains, before, *refs):
    slots, pieces, refs = refs[:n_slots], refs[n_slots : n_slots + n_pieces], refs[n_slots + n_pieces :]
    after, normed, query, key, value, mixed, totals, encoder = refs[:8]
    weights, sems, piece_sems = refs[8:]
    length = before.shape[0] // rows_held
    source_length = sources.shape[1]
    fetch_pieces = encoder_copies(pieces, encoder, tab, rows_held, piece_sems)
    for copy in fetch_pieces:
        copy.start()
    fetch = weight_copies(slots, weights, tab, sems, 4 * PAIR)
    resident = before[...]
    low = (resident * root_scale(resident) * gains[1:2]).astype(bf16)
    normed[...] = low
    allowed = [
        cross_masks(tab, targets, sources, row, n_pieces, 16 if n_pieces > 1 else 28)
        for row in range(rows_held)
    ]
    wait_for(fetch_pieces)
    source = encoder[...].reshape(rows_held * source_length, D)
    total = resident
    for group in GROUPS:
        for pair in group:
            wait_for(fetch[pair])
            query[pair] = dot_nn(low, weights[pair, :, 0:PAIR]).astype(bf16)
            projected = dot_nn(source, weights[pair, :, PAIR : 3 * PAIR]).astype(bf16)
            key[pair] = projected[:, 0:PAIR]
            value[pair] = projected[:, PAIR:]
        places = [(pair, row) for pair in group for row in range(rows_held)]
        spans = [slice(row * length, (row + 1) * length) for row in range(rows_held)]
        wides = [slice(row * source_length, (row + 1) * source_length) for row in range(rows_held)]
        mixes, logs = attend(
            [
                (query[pair, spans[row]], key[pair, wides[row]], value[pair, wides[row]], None, allowed[row])
                for pair, row in places
            ]
        )
        for (pair, row), mix, log_total in zip(places, mixes, logs):
            mixed[pair, spans[row]] = mix
            totals[pair, row : row + 1, :] = log_total
        for pair in group:
            total = total + dot_nt(mixed[pair], weights[pair, :, 3 * PAIR :])
    after[...] = total


def feed_kernel(n_slots, n_outs, rows_held, tab, gains, before, c_all, *refs):
    slots, refs = refs[:n_slots], refs[n_slots:]
    low_out, grad_before, grad_gain = refs[:3]
    outs, refs = refs[3 : 3 + n_outs], refs[3 + n_outs :]
    weights, c_rows, turned, normed_turned, again, c_turned, held, sems, c_sem, out_sems = refs
    fetch_c = pltpu.make_async_copy(c_all.at[pl.ds(tab[24], rows_held)], c_rows, c_sem)
    fetch = weight_copies(slots, weights, tab, sems)
    fetch_c.start()
    resident = before[...]
    gain = gains[2:3]
    low = (resident * root_scale(resident) * gain).astype(bf16)
    turned[...] = jnp.transpose(low)
    permute_rows(turned, normed_turned, tab, n_slots)
    fetch_c.wait()
    cotangent = c_rows[...].reshape(resident.shape)
    again[...] = jnp.transpose(cotangent)
    permute_rows(again, c_turned, tab, n_slots)
    writer = SlotWriter(outs, held, out_sems)
    total = resident
    grad_normed = jnp.zeros_like(resident)
    for pair in range(PAIRS):
        wait_for(fetch[pair])
        inner, outer = weights[pair, :, 0:HIDDEN], weights[pair, :, HIDDEN:]
        u = dot_nn(low, inner)
        squared = u * u
        bent = jnp.tanh(gelu_slope * (u + gelu_cubic * u * squared))
        hidden = (0.5 * u * (1.0 + bent)).astype(bf16)
        slope = 0.5 * (1.0 + bent) + 0.5 * u * (1.0 - bent * bent) * gelu_slope * (
            1.0 + 3.0 * gelu_cubic * squared
        )
        total = total + dot_nt(hidden, outer)
        grad_u = (dot_nn(cotangent, outer) * slope).astype(bf16)
        grad_normed = grad_normed + dot_nt(grad_u, inner)
        writer.write(pair, (dot_nn(normed_turned[...], grad_u), dot_nn(c_turned[...], hidden)))
    low_out[...] = total.astype(bf16)
    through, gain_part = root_back(resident, gain, grad_normed)
    grad_before[...] = cotangent.astype(f32) + through
    grad_gain[...] = gain_part
    writer.finish()


def cross_back_kernel(
    n_slots, n_pieces, rows_held, tab, targets, sources, gains, grad_after, before, *refs
):
    query, key, value, totals = refs[:4]
    slots, refs = refs[4 : 4 + n_slots], refs[4 + n_slots :]
    grad_before, grad_gain, d_query, d_key, d_value, weights, sems = refs
    length = before.shape[0] // rows_held
    source_length = sources.shape[1]
    fetch = weight_copies(slots, weights, tab, sems, 4 * PAIR)
    grad_in = grad_after[...]
    low = grad_in.astype(bf16)
    allowed = [
        cross_masks(tab, targets, sources, row, n_pieces, 16 if n_pieces > 1 else 28)
        for row in range(rows_held)
    ]
    spans = [slice(row * length, (row + 1) * length) for row in range(rows_held)]
    wides = [slice(row * source_length, (row + 1) * source_length) for row in range(rows_held)]
    grad_normed = jnp.zeros_like(grad_in)
    for group in GROUPS:
        wait_for([copy for pair in group for copy in fetch[pair]])
        grad_mixed = {pair: dot_nn(low, weights[pair, :, 3 * PAIR :]).astype(bf16) for pair in group}
        places = [(pair, row) for pair in group for row in range(rows_held)]
        results = attend_back(
            [
                (
                    query[pair, spans[row]],
                    key[pair, wides[row]],
                    value[pair, wides[row]],
                    None,
                    allowed[row],
                    totals[pair, row : row + 1, :],
                    grad_mixed[pair][spans[row]],
                )
                for pair, row in places
            ]
        )
        for (pair, row), one, two, three, _ in zip(places, *results):
            d_query[pair, spans[row]] = one
            d_key[pair, wides[row]] = two
            d_value[pair, wides[row]] = three
        for pair in group:
            grad_normed = grad_normed + dot_nt(d_query[pair], weights[pair, :, 0:PAIR])
    through, gain_part = root_back(before[...], gains[1:2], grad_normed)
    grad_before[...] = grad_in + through
    grad_gain[...] = gain_part


def cross_weights_kernel(
    n_slots, n_outs, n_after, tab, grad_after, normed, mixed, encoder, d_query, d_key, d_value, *refs
):
    refs = refs[n_after:]
    outs, refs = refs[:n_outs], refs[n_outs:]
    turned, low_turned, again, normed_turned, wide_turned, encoder_turned, held, out_sems = refs
    writer = SlotWriter(outs, held, out_sems)
    turned[...] = jnp.transpose(grad_after[...].astype(bf16))
    permute_rows(turned, low_turned, tab, n_slots)
    again[...] = jnp.transpose(normed[...])
    permute_rows(again, normed_turned, tab, n_slots)
    wide_turned[...] = jnp.transpose(encoder[...].reshape(wide_turned.shape[1], D))
    permute_rows(wide_turned, encoder_turned, tab, n_slots)
    for pair in range(PAIRS):
        writer.write(
            pair,
            (
                dot_nn(normed_turned[...], d_query[pair]),
                dot_nn(encoder_turned[...], d_key[pair]),
                dot_nn(encoder_turned[...], d_value[pair]),
                dot_nn(low_turned[...], mixed[pair]),
            ),
        )
    writer.finish()


def self_back_kernel(
    n_slots, n_outs, n_after, rows_held, tab, targets, onehot, gains, falls, gain_two, gain_three, grad_after, low_out, x_all, *refs
):
    normed, query, key, value, mixed, totals = refs[:6]
    slots, refs = refs[6 : 6 + n_slots], refs[6 + n_slots + n_after :]
    low_grad = refs[0]
    outs, refs = refs[1 : 1 + n_outs], refs[1 + n_outs :]
    weights, x_rows, turned, low_turned, again, normed_turned, bias_rows, held, sems, x_sem, out_sems = refs
    writer = SlotWriter(outs, held, out_sems)
    length = x_all.shape[1]
    fetch_x = pltpu.make_async_copy(x_all.at[pl.ds(tab[24], rows_held)], x_rows, x_sem)
    fetch = weight_copies(slots, weights, tab, sems)
    fetch_x.start()
    grad_in = grad_after[...]
    low = grad_in.astype(bf16)
    turned[...] = jnp.transpose(low)
    permute_rows(turned, low_turned, tab, n_slots)
    again[...] = jnp.transpose(normed[...])
    permute_rows(again, normed_turned, tab, n_slots)
    allowed = [self_masks(tab, targets, row, length) for row in range(rows_held)]
    grad_normed = jnp.zeros_like(grad_in)
    spans = [slice(row * length, (row + 1) * length) for row in range(rows_held)]
    for group in GROUPS:
        wait_for([copy for pair in group for copy in fetch[pair]])
        grad_mixed = {pair: dot_nn(low, weights[pair, :, 3 * PAIR :]).astype(bf16) for pair in group}
        biases = {pair: bias_of(tab, falls, pair, length) for pair in group}
        places = [(pair, row) for pair in group for row in range(rows_held)]
        results = attend_back(
            [
                (
                    query[pair, spans[row]],
                    key[pair, spans[row]],
                    value[pair, spans[row]],
                    biases[pair],
                    allowed[row],
                    totals[pair, row : row + 1, :],
                    grad_mixed[pair][spans[row]],
                )
                for pair, row in places
            ]
        )
        parts = {place: result for place, *result in zip(places, *results)}
        for pair in group:
            joined = [jnp.concatenate(parts[pair, row][:3], axis=1) for row in range(rows_held)]
            joined = jnp.concatenate(joined, axis=0) if rows_held > 1 else joined[0]
            grad_normed = grad_normed + dot_nt(joined, weights[pair, :, 0 : 3 * PAIR])
            writer.write(
                pair, (dot_nn(normed_turned[...], joined), dot_nn(low_turned[...], mixed[pair]))
            )
            grad_bias = sum(parts[pair, row][3] for row in range(rows_held))
            for side in range(2):
                diagonal = fold_diagonals(grad_bias[:, side * length : (side + 1) * length])
                bias_rows[pl.ds(tab[16 + pair] * 2 + side, 1), :] = diagonal
    fetch_x.wait()
    resident = x_rows[...].reshape(grad_in.shape).astype(f32)
    through, gain_one = root_back(resident, gains[0:1], grad_normed)
    low_grad[0:rows_held] = low_out[...].reshape(x_rows.shape)
    low_grad[rows_held:] = (grad_in + through).astype(bf16).reshape(x_rows.shape)
    table = lax.dot_general(
        bias_rows[...],
        onehot[...].astype(f32),
        (((1,), (1,)), ((), ())),
        precision=lax.Precision.HIGHEST,
        preferred_element_type=f32,
    )
    blank = jnp.zeros((5, D), f32)
    table = jnp.concatenate((table, jnp.zeros((8, D - 128), f32)), axis=1)
    tile = jnp.concatenate((gain_one, gain_two[...], gain_three[...], blank, table), axis=0).astype(bf16)
    rows = D // n_slots
    for pair in range(PAIRS):
        for number in range(n_slots):
            held[number, pair, rows : rows + EXTRA, :] = tile
        writer.send(pair, rows, EXTRA, PAIRS + pair)
    writer.finish()


def pack_attention_kernel(n_dp, tab, query, keyval, output, gains, table, own):
    rows, width = query.shape[1], gains.shape[1]
    place_dp, place_mp = tab[25], tab[26]
    parts = []
    for number in range(2):
        parts += [query[number], keyval[number, 0], keyval[number, 1], output[number]]
    own[0:rows, :] = jnp.concatenate(parts, axis=1).astype(bf16)
    wide = jnp.concatenate([gains[...]] * n_dp, axis=1)
    lane = lax.broadcasted_iota(jnp.int32, wide.shape, 1)
    wide = jnp.where((lane // width == place_dp) & (place_mp == 0), wide, 0.0)
    heads, bands = table.shape
    lane = lax.broadcasted_iota(jnp.int32, (bands, D), 1)
    band = lax.broadcasted_iota(jnp.int32, (bands, D), 0)
    at_band = jnp.where(lane == place_dp * bands + band, 1.0, 0.0).astype(bf16)
    head = lax.broadcasted_iota(jnp.int32, (HEADS, heads), 0)
    column = lax.broadcasted_iota(jnp.int32, (HEADS, heads), 1)
    at_head = jnp.where(head == place_mp * heads + column, 1.0, 0.0).astype(bf16)
    placed = dot_nn(at_head, dot_nn(table[...].astype(bf16), at_band).astype(bf16))
    blank = jnp.zeros((HEADS - wide.shape[0], D), f32)
    tile = jnp.concatenate((wide, blank, placed), axis=0).astype(bf16)
    own[rows : rows + EXTRA, 0:D] = tile
    own[rows : rows + EXTRA, D:] = jnp.zeros_like(tile)


def pack_feed_kernel(inner, outer, *refs):
    refs[-1][...] = jnp.concatenate((inner[...], outer[...]), axis=1).astype(bf16)


def split_encoder_kernel(rows_held, tab, encoder, *refs):
    outs, sems = refs[:-1], refs[-1]
    copies = [
        pltpu.make_async_copy(
            encoder.at[pl.ds(tab[17 + number] * rows_held, rows_held)], out, sems.at[number]
        )
        for number, out in enumerate(outs)
    ]
    for copy in copies:
        copy.start()
    for copy in copies:
        copy.wait()


def stack_kernel(count, *refs):
    out = refs[-1]
    for number in range(count):
        out[number] = refs[number][...]


def stack_through_kernel(count, *refs):
    stack_kernel(count, *refs[:-1])


def spread_kernel(rows_held, tab, *refs):
    pieces, outs = refs[:4], refs[-2:]
    for number, piece in enumerate(pieces):
        for side, out in enumerate(outs):
            here = piece[side * rows_held : (side + 1) * rows_held]
            out[pl.ds(tab[16 + number] * rows_held, rows_held)] = here


def shape(dims, dtype):
    return jax.ShapeDtypeStruct(dims, dtype)


def dma_sems(*counts):
    return pltpu.SemaphoreType.DMA(counts)


def anys(arrays):
    return [(array, "any") for array in arrays]


def vmems(arrays):
    return [(array, "vmem") for array in arrays]


def call(kernel, operands, outs, scratch, micros=1, aliases=None, any_outs=()):
    spaces = {"smem": pltpu.SMEM, "vmem": pltpu.VMEM, "any": pl.ANY}
    arrays = [array for array, _ in operands]
    moved = sum(a.size * a.dtype.itemsize for a in arrays) + sum(
        math.prod(o.shape) * o.dtype.itemsize for o in outs
    )
    return pl.pallas_call(
        kernel,
        out_shape=tuple(outs),
        in_specs=[pl.BlockSpec(memory_space=spaces[place]) for _, place in operands],
        out_specs=tuple(
            pl.BlockSpec(memory_space=pl.ANY if i in any_outs or i in (aliases or {}).values() else pltpu.VMEM)
            for i in range(len(outs))
        ),
        input_output_aliases=aliases or {},
        scratch_shapes=scratch,
        compiler_params=pltpu.CompilerParams(vmem_limit_bytes=VMEM_BYTES),
        cost_estimate=pl.CostEstimate(flops=int(micros * 1.15e9), bytes_accessed=moved if micros else 0, transcendentals=0),
    )(*arrays)


def bucket_onehot(length):
    distance = np.arange(length)
    bucket = np.minimum(distance, 16)
    for edge_value in bucket_edges:
        bucket = bucket + (distance >= edge_value)
    return jnp.asarray(np.arange(128)[:, None] == bucket[None, :], bf16)


def adam_step(weight, first, second, grad, rate, decay):
    new_first = beta_first * first + (1.0 - beta_first) * grad
    new_second = beta_second * second + (1.0 - beta_second) * grad * grad
    ratio = (
        new_first
        / (1.0 - beta_first**STEP)
        / (jnp.sqrt(new_second / (1.0 - beta_second**STEP)) + adam_eps)
    )
    return (new_first, new_second, weight - rate * (ratio + decay * weight))


def step_rates():
    return (
        rate_factor * (16 * D) ** (-0.5),
        rate_factor * D ** (-0.5),
        rate_factor * (HD // 8) ** (-0.5),
        rate_factor * D ** (-0.5),
        rate_factor * (FF // 2) ** (-0.5),
        rate_factor,
        rate_factor,
    )


def gate_kernel(*refs):
    pass


def gate(array, after):
    (same,) = call(
        gate_kernel, anys([array] + list(after)), [shape(array.shape, array.dtype)], [], aliases={0: 0}
    )
    return same


def fold(arrived, kept, after=()):
    if after:
        kept = gate(kept, after)
    half = arrived.shape[0] // 2
    parts = [(arrived[i : i + half], kept[i : i + half]) for i in (half, 0)]
    if half == 1:
        parts = [(x[0], y[0]) for x, y in parts]
    return [(x.astype(f32) + y.astype(f32)).astype(bf16) for x, y in parts]


class TreePlan:
    n_slots = 8
    out_slots = (4, 4)
    order = (0, 2, 1, 3)

    def __init__(self, n_dp, n_mp):
        self.n_dp, self.n_mp = n_dp, n_mp

    def pairs(self, target):
        n_mp = self.n_mp
        return [
            (d * n_mp + m, t * n_mp + s)
            for d in range(self.n_dp)
            for m in range(n_mp)
            for t, s in (target(d, m),)
        ]

    def hop_z(self, array, number):
        return lax.ppermute(array, ALL, self.pairs(lambda d, m: (d, m ^ number)))

    def hop_core(self, array):
        return lax.ppermute(array, ALL, self.pairs(lambda d, m: (d ^ 1, m)))

    def hop_first(self, array):
        return lax.ppermute(array, ALL, self.pairs(lambda d, m: (d ^ (4 if d & 1 else 2), m)))

    def hop_second(self, array):
        return lax.ppermute(array, ALL, self.pairs(lambda d, m: (d ^ (2 if d & 1 else 4), m)))

    def table(self, place_dp, place_mp, rows_held):
        core = place_dp & 1
        first, second = 2 + 2 * core, 4 - 2 * core
        own = [place_dp ^ (a * first) ^ (b * second) for b in range(2) for a in range(2)]
        peer = [place_dp ^ 1 ^ (a * second) ^ (b * first) for b in range(2) for a in range(2)]
        return own + peer, [place_mp ^ j for j in self.order]

    def along_z(self, own, after=()):
        across, near = self.hop_z(own, 2), self.hop_z(own, 1)
        if after:
            across = gate(across, after)
        return [own, across, near, self.hop_z(across, 1)]

    def stack(self, pieces, after=()):
        (base,) = call(
            functools.partial(stack_kernel, len(pieces)),
            vmems(pieces) + anys(after),
            [shape((len(pieces),) + pieces[0].shape, bf16)],
            [],
        )
        return base

    def stack_through(self, pieces, through):
        return call(
            functools.partial(stack_through_kernel, len(pieces)),
            vmems(pieces) + anys([through]),
            [shape((len(pieces),) + pieces[0].shape, bf16), shape(through.shape, bf16)],
            [],
            aliases={len(pieces): 1},
        )

    def in_plane(self, base, near, far):
        slots = [base, near, far, self.hop_second(near)]
        return slots + [self.hop_core(slot) for slot in slots]

    def attention_shard(self, tab, query, keyval, output, gains, table):
        rows, columns = query.shape[1:]
        (own,) = call(
            functools.partial(pack_attention_kernel, self.n_dp),
            [(tab, "smem")] + vmems((query, keyval, output, gains, table)),
            [shape((rows + EXTRA, 8 * columns), bf16)],
            [],
        )
        return own

    def feed_shard(self, inner, outer, after):
        (own,) = call(
            pack_feed_kernel,
            vmems((inner, outer)) + anys(after),
            [shape((inner.shape[0], 2 * inner.shape[1]), bf16)],
            [],
        )
        return own

    def weights(self, tab, query, keyval, output, inner, outer, gains, table, encoder, rows_held):
        attention = self.along_z(self.attention_shard(tab, query, keyval, output, gains, table))
        parts = call(
            functools.partial(split_encoder_kernel, rows_held),
            [(tab, "smem")] + anys([encoder]),
            [shape((rows_held,) + encoder.shape[1:], bf16)] * 3,
            [dma_sems(3)],
        )
        own_feed = self.feed_shard(inner, outer, [attention[1], parts[0]])
        feed = self.along_z(own_feed)
        base = self.stack(attention, [own_feed])
        near, far = self.hop_first(base), self.hop_second(base)
        feed_base, near = self.stack_through(feed, near)
        attention = self.in_plane(base, near, far)
        sources = [encoder] + [self.hop_z(part, j) for part, j in zip(parts, self.order[1:])]
        feed = self.in_plane(feed_base, self.hop_first(feed_base), self.hop_second(feed_base))
        return attention, feed, sources, feed_base

    def reduce_core(self, parts, after=()):
        own, peer = parts
        return fold(self.hop_core(peer), own, after)

    def reduce_second(self, pair, after=()):
        return fold(self.hop_second(pair[0]), pair[1], after)

    def reduce_first(self, pair, after=()):
        return fold(self.hop_first(pair[0]), pair[1], after)

    def reduce_near(self, pair, after=()):
        return fold(self.hop_z(pair[0], 1), pair[1], after)

    def reduce_across(self, pair, after=()):
        sent, kept = pair
        if after:
            kept = gate(kept, after)
        total = self.hop_z(sent, 2).astype(f32) + kept.astype(f32)
        return total, total[D // self.n_dp :]

    def finish(self, tab, rows_out, feed, cross, own):
        feed = self.reduce_first(feed, [cross[0]])
        own = self.reduce_second(own, [feed[0]])
        cross = self.reduce_core(cross, [own[0]])
        pieces = self.along_z(rows_out, [cross[0]])
        feed = self.reduce_near(feed, [cross[0]])
        own = self.reduce_first(own, [feed[0]])
        cross = self.reduce_second(cross, [own[0]])
        feed = self.reduce_across(feed, [cross[0]])
        own = self.reduce_near(own, [cross[0]])
        cross = self.reduce_first(cross, [own[0]])
        cross = self.reduce_near(cross)
        rows = self.spread(tab, pieces, [cross[0]])
        return rows, [feed, self.reduce_across(cross), self.reduce_across(own, [cross[0]])]

    def spread(self, tab, pieces, after):
        piece = pieces[0]
        half = piece.shape[0] // 2
        out = shape((half * self.n_mp,) + piece.shape[1:], piece.dtype)
        return call(
            functools.partial(spread_kernel, half),
            [(tab, "smem")] + vmems(pieces) + anys(after),
            [out, out],
            [],
        )


class PlainPlan:
    n_slots = 1
    out_slots = (1,)

    def __init__(self, n_dp, n_mp):
        self.n_dp, self.n_mp = n_dp, n_mp

    def table(self, place_dp, place_mp, rows_held):
        return [0], [0, 1, 2, 3]

    def gather(self, own, kinds):
        full = lax.all_gather(own, ("mp", "dp"), axis=0, tiled=True)
        full = full.reshape(self.n_mp, D, kinds, -1).transpose(2, 1, 0, 3)
        return full.reshape(kinds, D, PAIRS, -1).transpose(2, 1, 0, 3).reshape(PAIRS, D, -1)

    def weights(self, tab, query, keyval, output, inner, outer, gains, table, encoder, rows_held):
        place_dp, place_mp = lax.axis_index("dp"), lax.axis_index("mp")
        parts = []
        for i in range(2):
            parts += [query[i], keyval[i, 0], keyval[i, 1], output[i]]
        attention = self.gather(jnp.concatenate(parts, axis=1).astype(bf16), 8)
        feed = self.gather(jnp.concatenate((inner, outer), axis=1).astype(bf16), 2)
        width = gains.shape[1]
        tile = jnp.zeros((EXTRA, D), f32)
        spot = jnp.where(place_mp == 0, gains, 0.0)
        tile = lax.dynamic_update_slice(tile, spot, (0, place_dp * width))
        heads, bands = table.shape
        tile = lax.dynamic_update_slice(tile, table, (8 + place_mp * heads, place_dp * bands))
        tile = lax.psum(tile.astype(bf16).astype(f32), ALL).astype(bf16)
        tile = jnp.concatenate((tile, jnp.zeros_like(tile)), axis=1)[None]
        tile = jnp.concatenate((tile, jnp.zeros((PAIRS - 1,) + tile.shape[1:], bf16)))
        sources = lax.all_to_all(encoder, "mp", split_axis=0, concat_axis=1, tiled=True)
        return [jnp.concatenate((attention, tile), axis=1)], [feed], [sources], feed

    def reduce_core(self, parts):
        return parts

    def reduce(self, grads):
        kinds = 4 if grads.shape[2] == 4 * PAIR else 2
        full = grads[:, :D].reshape(PAIRS, D, kinds, -1).transpose(2, 1, 0, 3)
        full = full.reshape(kinds, D, self.n_mp, -1).transpose(2, 1, 0, 3)
        total = lax.psum_scatter(
            full.reshape(self.n_mp * D, -1), ("mp", "dp"), scatter_dimension=0, tiled=True
        ).astype(f32)
        return total, lax.psum(grads[0, D:].astype(f32), ALL) if grads.shape[1] > D else None

    def finish(self, tab, rows_out, feed, cross, own):
        half = rows_out.shape[0] // 2
        rows = [
            lax.all_gather(rows_out[i : i + half], "mp", axis=0, tiled=True) for i in (0, half)
        ]
        return rows, [self.reduce(parts[0][0]) for parts in (feed, cross, own)]

    def reduce_second(self, parts):
        return parts


def shards(
    plan,
    inputs,
    encoder,
    cotangent,
    target_segments,
    encoder_segments,
    query_weight,
    query_first,
    query_second,
    keyval_weight,
    keyval_first,
    keyval_second,
    output_weight,
    output_first,
    output_second,
    inner_weight,
    inner_first,
    inner_second,
    outer_weight,
    outer_first,
    outer_second,
    gains,
    gains_first,
    gains_second,
    bias_table,
    table_first,
    table_second,
):
    n_slots, out_slots = plan.n_slots, plan.out_slots
    n_outs = len(out_slots)
    seq_count, length, _ = inputs.shape
    source_length = encoder_segments.shape[1]
    rows_held = seq_count // plan.n_mp
    tokens, sources = rows_held * length, rows_held * source_length
    place_dp, place_mp = lax.axis_index("dp"), lax.axis_index("mp")
    slot_table, pair_table = plan.table(place_dp, place_mp, rows_held)
    entries = slot_table + [0] * (16 - len(slot_table)) + pair_table + [0] * 4
    entries = entries + [place_mp * rows_held, place_dp, place_mp] + [0] * 5
    tab = jnp.stack([jnp.asarray(entry, jnp.int32) for entry in entries])
    onehot = bucket_onehot(length)
    attn_slots, feed_slots, pieces, feed_base = plan.weights(
        tab,
        query_weight,
        keyval_weight,
        output_weight.transpose(0, 2, 1),
        inner_weight,
        outer_weight.T,
        gains,
        bias_table.T,
        encoder,
        rows_held,
    )
    n_pieces = len(pieces)
    rows, columns = query_weight.shape[1:]
    width = gains.shape[1]
    bands, heads = bias_table.shape

    flat = (tokens, D)
    paired = (PAIRS, tokens, PAIR)
    wide = (PAIRS, sources, PAIR)
    stats = shape((PAIRS, rows_held, 2 * length), f32)
    attn_weights = VM((PAIRS, D, 4 * PAIR), bf16)

    after_self, normed_one, q_one, k_one, v_one, mix_one, sum_one, gain_rows, falls = call(
        functools.partial(self_forward_kernel, n_slots, 1, rows_held),
        [(tab, "smem")] + vmems((target_segments, onehot)) + anys([inputs] + attn_slots + [feed_base]),
        [shape(flat, f32), shape(flat, bf16)]
        + [shape(paired, bf16)] * 4
        + [stats, shape((8, D), f32), shape((8, length), f32)],
        [
            attn_weights,
            VM((n_slots, PAIRS, EXTRA, D), bf16),
            VM((rows_held, length, D), bf16),
            dma_sems(n_slots, PAIRS),
            dma_sems(n_slots),
            pltpu.SemaphoreType.DMA,
        ],
        micros=6,
    )
    after_cross, normed_two, q_two, k_two, v_two, mix_two, sum_two, source_rows = call(
        functools.partial(cross_forward_kernel, n_slots, n_pieces, rows_held),
        [(tab, "smem")]
        + vmems((target_segments, encoder_segments, gain_rows, after_self))
        + anys(attn_slots + pieces),
        [
            shape(flat, f32),
            shape(flat, bf16),
            shape(paired, bf16),
            shape(wide, bf16),
            shape(wide, bf16),
            shape(paired, bf16),
            stats,
            shape((rows_held, source_length, D), bf16),
        ],
        [attn_weights, dma_sems(n_slots, PAIRS), dma_sems(n_pieces)],
        micros=11,
    )

    def grad_outs(extra, width_out):
        return [
            shape((count, PAIRS, D // n_slots + extra, width_out), bf16) for count in out_slots
        ]

    feed_result = call(
        functools.partial(feed_kernel, n_slots, n_outs, rows_held),
        [(tab, "smem")] + vmems((gain_rows, after_cross)) + anys([cotangent] + feed_slots),
        [shape(flat, bf16), shape(flat, f32), shape((1, D), f32)] + grad_outs(0, 2 * HIDDEN),
        [
            VM((PAIRS, D, 2 * HIDDEN), bf16),
            VM((rows_held, length, D), bf16),
            VM((D, tokens), bf16),
            VM((D, tokens), bf16),
            VM((D, tokens), bf16),
            VM((D, tokens), bf16),
            VM((n_slots, PAIRS, D // n_slots, 2 * HIDDEN), bf16),
            dma_sems(n_slots, PAIRS),
            pltpu.SemaphoreType.DMA,
            dma_sems(n_outs, PAIRS),
        ],
        any_outs=range(3, 3 + n_outs),
        micros=10,
    )
    low_out, grad_second, gain_three = feed_result[:3]
    core_feed = plan.reduce_core(feed_result[3:])
    grad_first, gain_two, dq_two, dk_two, dv_two = call(
        functools.partial(cross_back_kernel, n_slots, n_pieces, rows_held),
        [(tab, "smem")]
        + vmems((target_segments, encoder_segments, gain_rows, grad_second, after_self))
        + vmems((q_two, k_two, v_two, sum_two))
        + anys(attn_slots),
        [shape(flat, f32), shape((1, D), f32), shape(paired, bf16), shape(wide, bf16), shape(wide, bf16)],
        [attn_weights, dma_sems(n_slots, PAIRS)],
        micros=10,
    )
    self_result = call(
        functools.partial(self_back_kernel, n_slots, n_outs, 1, rows_held),
        [(tab, "smem")]
        + vmems((target_segments, onehot, gain_rows, falls, gain_two, gain_three, grad_first, low_out))
        + anys([inputs])
        + vmems((normed_one, q_one, k_one, v_one, mix_one, sum_one))
        + anys(attn_slots + [core_feed[0]]),
        [shape((2 * rows_held, length, D), bf16)] + grad_outs(EXTRA, 4 * PAIR),
        [
            attn_weights,
            VM((rows_held, length, D), bf16),
            VM((D, tokens), bf16),
            VM((D, tokens), bf16),
            VM((D, tokens), bf16),
            VM((D, tokens), bf16),
            VM((8, length), f32),
            VM((n_slots, PAIRS, D // n_slots + EXTRA, 4 * PAIR), bf16),
            dma_sems(n_slots, PAIRS),
            pltpu.SemaphoreType.DMA,
            dma_sems(n_outs, 2 * PAIRS),
        ],
        any_outs=range(1, 1 + n_outs),
        micros=10,
    )
    second_feed = plan.reduce_second(core_feed)
    core_self = plan.reduce_core(self_result[1:])
    cross_grads = call(
        functools.partial(cross_weights_kernel, n_slots, n_outs, 2),
        [(tab, "smem")]
        + vmems((grad_second, normed_two, mix_two, source_rows, dq_two, dk_two, dv_two))
        + anys([second_feed[0], core_self[0]]),
        grad_outs(0, 4 * PAIR),
        [
            VM((D, tokens), bf16),
            VM((D, tokens), bf16),
            VM((D, tokens), bf16),
            VM((D, tokens), bf16),
            VM((D, sources), bf16),
            VM((D, sources), bf16),
            VM((n_slots, PAIRS, D // n_slots, 4 * PAIR), bf16),
            dma_sems(n_outs, PAIRS),
        ],
        any_outs=range(n_outs),
        micros=7,
    )
    (outputs, input_grad), ((grad_feed, _), (grad_cross, _), (grad_self, tile)) = plan.finish(
        tab, self_result[0], second_feed, cross_grads, core_self
    )

    def kind(grads, number):
        return grads[:rows, number * columns : (number + 1) * columns]

    hidden = inner_weight.shape[1]
    grads = (
        jnp.stack((kind(grad_self, 0), kind(grad_cross, 0))),
        jnp.stack(
            (
                jnp.stack((kind(grad_self, 1), kind(grad_self, 2))),
                jnp.stack((kind(grad_cross, 1), kind(grad_cross, 2))),
            )
        ),
        jnp.stack((kind(grad_self, 3).T, kind(grad_cross, 3).T)),
        grad_feed[:, :hidden],
        grad_feed[:, hidden:].T,
        lax.dynamic_slice_in_dim(tile[0:3], place_dp * width, width, 1),
        lax.dynamic_slice(tile, (8 + place_mp * heads, place_dp * bands), (heads, bands)).T,
    )
    params = (
        query_weight,
        keyval_weight,
        output_weight,
        inner_weight,
        outer_weight,
        gains,
        bias_table,
    )
    firsts = (
        query_first,
        keyval_first,
        output_first,
        inner_first,
        outer_first,
        gains_first,
        table_first,
    )
    seconds = (
        query_second,
        keyval_second,
        output_second,
        inner_second,
        outer_second,
        gains_second,
        table_second,
    )
    updated = [
        adam_step(*param_entry)
        for param_entry in zip(params, firsts, seconds, grads, step_rates(), step_decays)
    ]
    return (outputs, input_grad) + tuple(array for triple in updated for array in triple)


def solution(mesh):
    n_dp, n_mp = mesh.shape["dp"], mesh.shape["mp"]
    plan = (TreePlan if (n_dp, n_mp) == (8, 4) else PlainPlan)(n_dp, n_mp)
    by_query, by_keyval = P(None, "dp", "mp"), P(None, None, "dp", "mp")
    by_output, by_inner, by_outer = P(None, "mp", "dp"), P("dp", "mp"), P("mp", "dp")
    weights = (by_query,) * 3 + (by_keyval,) * 3 + (by_output,) * 3 + (by_inner,) * 3
    weights = weights + (by_outer,) * 3 + (P(None, "dp"),) * 3 + (P("dp", "mp"),) * 3
    tokens = P("dp", None, None)
    return jax.shard_map(
        functools.partial(shards, plan),
        mesh=mesh,
        in_specs=(tokens, P("dp", "mp", None), tokens, P("dp", None), P("dp", None)) + weights,
        out_specs=(tokens, tokens) + weights,
        check_vma=False,
    )
```

time: 260 us -> 211 us (0.81)
  starting transfers between devices: 82 us -> 38.9 us
  waiting for transfers between devices: 94.9 us -> 71.1 us
  other arithmetic: 13.3 us -> 25 us
  Pallas kernels: 58.2 us -> 63.6 us
    ppermute x27 -> x18, starting transfers between devices: 62 us -> 24.5 us  [hop_z(): return lax.ppermute(array, ALL, self.pairs(lambda d, m: (d, m ^ number)))]
    convert_element_type x4 -> x12, other arithmetic: 1.02 us -> 17.9 us  [fold(): return [(x.astype(f32) + y.astype(f32)).astype(bf16) for x, y in parts]]
    ppermute x6 -> x5, waiting for transfers between devices: 22.3 us -> 6.43 us  [hop_first(): lax.ppermute(array, ALL, self.pairs(lambda d, m: (d ^ (4 if d & 1 else 2)...]
    ppermute x27 -> x18, waiting for transfers between devices: 58.9 us -> 45.5 us  [hop_z(): return lax.ppermute(array, ALL, self.pairs(lambda d, m: (d, m ^ number)))]
    ppermute x9 -> x7, waiting for transfers between devices: 13.7 us -> 19.1 us  [hop_second(): lax.ppermute(array, ALL, self.pairs(lambda d, m: (d ^ (2 if d & 1 else 4)...]
    pallas_call x8 -> x23, Pallas kernels: 58.2 us -> 63.6 us  [call(): pl.pallas_call(kernel, out_shape=tuple(outs), in_specs=[pl.BlockSpec(memo...]
    ppermute x9 -> x7, starting transfers between devices: 11 us -> 6.04 us  [hop_second(): lax.ppermute(array, ALL, self.pairs(lambda d, m: (d ^ (2 if d & 1 else 4)...]
    unnamed x116 -> x132, local copies, waits for them, and re-layouts: 4.77 us -> 9.27 us
  transfers between devices with their start and end apart: 57 -> 41, of which waited for: 17 -> 15; matrix products, arithmetic and copies ran while one was open for 5% -> 10% of each run, Pallas kernels for 12% -> 23%
where the time goes in v2:
time: 211 us; the launch traced here: 210 us
  waiting for transfers between devices  71.1 us (34%)
  Pallas kernels  63.6 us (30%)
  starting transfers between devices  38.9 us (18%)
  other arithmetic  25 us (12%)
  local copies, waits for them, and re-layouts  9.93 us (5%)
    pallas_call x23, Pallas kernels, call(): pl.pallas_call(kernel, out_shape=tuple(outs), in_specs=[pl.BlockSpec(memo...  63.6 us
    ppermute x18, waiting for transfers between devices, hop_z(): return lax.ppermute(array, ALL, self.pairs(lambda d, m: (d, m ^ number)))  45.5 us
    ppermute x18, starting transfers between devices, hop_z(): return lax.ppermute(array, ALL, self.pairs(lambda d, m: (d, m ^ number)))  24.5 us
    ppermute x7, waiting for transfers between devices, hop_second(): lax.ppermute(array, ALL, self.pairs(lambda d, m: (d ^ (2 if d & 1 else 4)...  19.1 us
    convert_element_type x12, other arithmetic, fold(): return [(x.astype(f32) + y.astype(f32)).astype(bf16) for x, y in parts]  17.9 us
    unnamed x132, local copies, waits for them, and re-layouts  9.27 us
    ppermute x5, starting transfers between devices, hop_first(): lax.ppermute(array, ALL, self.pairs(lambda d, m: (d ^ (4 if d & 1 else 2)...  6.44 us
    ppermute x5, waiting for transfers between devices, hop_first(): lax.ppermute(array, ALL, self.pairs(lambda d, m: (d ^ (4 if d & 1 else 2)...  6.43 us
  transfers between devices with their start and end apart: 41, of which 15 were waited for; matrix products, arithmetic and copies ran while one was open for 10% of the time, Pallas kernels for 23%

profile of v2, /device:TPU:0, one launch (start us, length us, event | category | flops | bytes accessed | tf_op | source)
XLA Modules:
  0.0 209.8 jit_solution(840054553671302064)
XLA Ops:
  3.2 4.0 %collective-permute-start = (bf16[80,1024]{1,0:T(8,128)(2,1)}, bf16[80,1024]{1,0:T(8,128)(2,1)S(1)}, u32[]{:S(2)}, u32[]{:S(2)}) collective-permute-start(bf16[80,1024]{1,0:T(8,128)(2,1)} %shard_map.434.refs_0_), channel_id=1, source_target_pairs={{0,2},{1,3},{2,0},{3,1},{4,6},{5,7},{6,4},{7,5},{8,10},{9,11},{10,... | collective-permute-start | bytes 491528 | tf_op jit(solution)/shard_map/ppermute | solution.py:704
  8.8 6.4 %collective-permute-done.refs_0_.refs_1_ = bf16[80,1024]{1,0:T(8,128)(2,1)S(1)} collective-permute-done((bf16[80,1024]{1,0:T(8,128)(2,1)}, bf16[80,1024]{1,0:T(8,128)(2,1)S(1)}, u32[]{:S(2)}, u32[]{:S(2)}) %collective-permute-start) | collective-permute-done | bytes 163872 | tf_op jit(solution)/shard_map/ppermute | solution.py:704
  16.0 2.7 %shard_map.435 = (bf16[2,128,512]{2,1,0:T(8,128)(2,1)}, bf16[2,128,512]{2,1,0:T(8,128)(2,1)}, bf16[2,128,512]{2,1,0:T(8,128)(2,1)}) custom-call(s32[32]{0:T(128)} %stack.102.tab, bf16[8,128,512]{2,1,0:T(8,128)(2,1)} %refs_8_.1), custom_call_target="tpu_custom_call" | custom-call | flops 1150000000 | bytes 1835136 | tf_op jit(solution)/shard_map/pallas_call | solution.py:619
  25.3 3.3 %collective-permute-start.3 = (bf16[64,1024]{1,0:T(8,128)(2,1)S(1)}, bf16[64,1024]{1,0:T(8,128)(2,1)S(1)}, u32[]{:S(2)}, u32[]{:S(2)}) collective-permute-start(bf16[64,1024]{1,0:T(8,128)(2,1)S(1)} %copy-done.62), channel_id=1, source_target_pairs={{0,2},{1,3},{2,0},{3,1},{4,6},{5,7},{6,4},{7,5},{8,10},{9,11},{10,... | collective-permute-start | bytes 393224 | tf_op jit(solution)/shard_map/ppermute | solution.py:704
  29.7 4.9 %collective-permute-done.3.refs_1_ = bf16[64,1024]{1,0:T(8,128)(2,1)S(1)} collective-permute-done((bf16[64,1024]{1,0:T(8,128)(2,1)S(1)}, bf16[64,1024]{1,0:T(8,128)(2,1)S(1)}, u32[]{:S(2)}, u32[]{:S(2)}) %collective-permute-start.3) | collective-permute-done | bytes 131104 | tf_op jit(solution)/shard_map/ppermute | solution.py:704
  35.9 4.0 %collective-permute-done.5.refs_3_ = bf16[64,1024]{1,0:T(8,128)(2,1)S(1)} collective-permute-done((bf16[64,1024]{1,0:T(8,128)(2,1)S(1)}, bf16[64,1024]{1,0:T(8,128)(2,1)S(1)}, u32[]{:S(2)}, u32[]{:S(2)}) %collective-permute-start.5) | collective-permute-done | bytes 131104 | tf_op jit(solution)/shard_map/ppermute | solution.py:704
  45.4 8.8 %collective-permute-done.8.refs_3_.refs_7_.refs_9_ = bf16[4,80,1024]{2,1,0:T(8,128)(2,1)S(1)} collective-permute-done((bf16[4,80,1024]{2,1,0:T(8,128)(2,1)}, bf16[4,80,1024]{2,1,0:T(8,128)(2,1)S(1)}, u32[]{:S(2)}, u32[]{:S(2)}) %collective-permute-start.8) | collective-permute-done | bytes 655392 | tf_op jit(solution)/shard_map/ppermute | solution.py:713
  57.1 6.4 %collective-permute-done.16.refs_1_ = bf16[4,64,1024]{2,1,0:T(8,128)(2,1)S(1)} collective-permute-done((bf16[4,64,1024]{2,1,0:T(8,128)(2,1)}, bf16[4,64,1024]{2,1,0:T(8,128)(2,1)S(1)}, u32[]{:S(2)}, u32[]{:S(2)}) %collective-permute-start.16) | collective-permute-done | bytes 524320 | tf_op jit(solution)/shard_map/ppermute | solution.py:710
  63.8 2.6 %collective-permute-start.15 = (bf16[2,128,512]{2,1,0:T(8,128)(2,1)S(1)}, bf16[2,128,512]{2,1,0:T(8,128)(2,1)S(1)}, u32[]{:S(2)}, u32[]{:S(2)}) collective-permute-start(bf16[2,128,512]{2,1,0:T(8,128)(2,1)S(1)} %copy-done.53), channel_id=1, source_target_pairs={{0,3},{1,2},{2,1},{3,0},{4,7},{5,6},{6,5},{7,4},{8,11},{9,10},{10,... | collective-permute-start | bytes 786440 | tf_op jit(solution)/shard_map/ppermute | solution.py:704
  68.5 5.8 %shard_map.439 = (f32[256,512]{1,0:T(8,128)}, bf16[256,512]{1,0:T(8,128)(2,1)}, bf16[4,256,128]{2,1,0:T(8,128)(2,1)}, bf16[4,256,128]{2,1,0:T(8,128)(2,1)}, bf16...) custom-call(s32[32]{0:T(128)} %stack.102.tab, ...), custom_call_target="tpu_custom_call" | custom-call | flops 6899999744 | bytes 8716416 | tf_op jit(solution)/shard_map/pallas_call | solution.py:619
  74.5 6.2 %collective-permute-done.14.refs_10_ = bf16[2,128,512]{2,1,0:T(8,128)(2,1)S(1)} collective-permute-done((bf16[2,128,512]{2,1,0:T(8,128)(2,1)S(1)}, bf16[2,128,512]{2,1,0:T(8,128)(2,1)S(1)}, u32[]{:S(2)}, u32[]{:S(2)}) %collective-permute-start.14) | collective-permute-done | bytes 262176 | tf_op jit(solution)/shard_map/ppermute | solution.py:704
  82.2 9.4 %shard_map.440 = (f32[256,512]{1,0:T(8,128)}, bf16[256,512]{1,0:T(8,128)(2,1)}, bf16[4,256,128]{2,1,0:T(8,128)(2,1)}, bf16[4,1024,128]{2,1,0:T(8,128)(2,1)}, bf1...) custom-call(s32[32]{0:T(128)} %stack.102.tab, ...), custom_call_target="tpu_custom_call" | custom-call | flops 12650000384 | bytes 12103808 | tf_op jit(solution)/shard_map/pallas_call | solution.py:619
  93.0 11.0 %shard_map.441 = (bf16[256,512]{1,0:T(8,128)(2,1)}, f32[256,512]{1,0:T(8,128)}, f32[1,512]{1,0:T(1,128)}, bf16[4,4,64,1024]{3,2,1,0:T(8,128)(2,1)}, bf16[4,4,64,1024]{3,2,1,0:T(8,128)(2,1)}) custom-call(s32[32]{0:T(128)} %stack.102.tab, f32[8,512]{1,0:T(8,128)} %get-tuple-element.65.gains, f32[256,512]{1,0:T(8,128)} %get-tuple-element.70.before, ...), custom_call_target="tpu_custom_call" | custom-call | flops 11500000256 | bytes 10766464 | tf_op jit(solution)/shard_map/pallas_call | solution.py:619
  104.6 9.1 %shard_map.442 = (f32[256,512]{1,0:T(8,128)}, f32[1,512]{1,0:T(1,128)}, bf16[4,256,128]{2,1,0:T(8,128)(2,1)}, bf16[4,1024,128]{2,1,0:T(8,128)(2,1)}, bf16[4,1024,128]{2,1,0:T(8,128)(2,1)}) custom-call(s32[32]{0:T(128)} %stack.102.tab, s32[8,128]{1,0:T(8,128)} %targets.7, s32[8,512]{1,0:T(8,128)} %sources.3, f32[8,512]{1,0:T(8,128)} %get-tuple-element.65.gains, ...), custom_call_target="tpu_custom_call" | custom-call | flops 11500000256 | bytes 11581568 | tf_op jit(solution)/shard_map/pallas_call | solution.py:619
  115.9 8.5 %shard_map.443 = (bf16[4,128,512]{2,1,0:T(8,128)(2,1)}, bf16[4,4,80,512]{3,2,1,0:T(8,128)(2,1)}, bf16[4,4,80,512]{3,2,1,0:T(8,128)(2,1)}) custom-call(s32[32]{0:T(128)} %stack.102.tab, s32[8,128]{1,0:T(8,128)} %targets.7, bf16[128,128]{1,0:T(8,128)(2,1)} %constant.53.clone.onehot, f32[8,512]{1,0:T(8,128)} %get-tuple-element.65.gains, ...), custom_call_target="tpu_custom_call" | custom-call | flops 11500000256 | bytes 12652672 | tf_op jit(solution)/shard_map/pallas_call | solution.py:619
  124.5 5.0 %collective-permute-done.25 = bf16[2,4,64,1024]{3,2,1,0:T(8,128)(2,1)S(1)} collective-permute-done((bf16[2,4,64,1024]{3,2,1,0:T(8,128)(2,1)S(1)}, bf16[2,4,64,1024]{3,2,1,0:T(8,128)(2,1)S(1)}, u32[]{:S(2)}, u32[]{:S(2)}) %collective-permute-start.25) | collective-permute-done | bytes 1048608 | tf_op jit(solution)/shard_map/ppermute | solution.py:713
  133.8 6.8 %shard_map.444 = (bf16[4,4,64,512]{3,2,1,0:T(8,128)(2,1)}, bf16[4,4,64,512]{3,2,1,0:T(8,128)(2,1)}) custom-call(s32[32]{0:T(128)} %stack.102.tab, f32[256,512]{1,0:T(8,128)} %get-tuple-element.71.grad_after, bf16[256,512]{1,0:T(8,128)(2,1)} %get-tuple-element.89.normed, bf16[4,256,128]{2,1,0:T(8,128)(2,1)} %get-tuple-element.90.mixed, ...), custom_call_target="tpu_custom_call" | custom-call | flops 8049999872 | bytes 7733376 | tf_op jit(solution)/shard_map/pallas_call | solution.py:619
  142.5 2.4 %collective-permute-start.30 = (bf16[4,128,512]{2,1,0:T(8,128)(2,1)}, bf16[4,128,512]{2,1,0:T(8,128)(2,1)S(1)}, u32[]{:S(2)}, u32[]{:S(2)}) collective-permute-start(bf16[4,128,512]{2,1,0:T(8,128)(2,1)} %get-tuple-element.88.refs_0_), channel_id=1, source_target_pairs={{0,1},{1,0},{2,3},{3,2},{4,5},{5,4},{6,7},{7,6},{8,9},{9,8},{10,11... | collective-permute-start | bytes 1572872 | tf_op jit(solution)/shard_map/ppermute | solution.py:704
  147.6 3.7 %collective-permute-done.28 = bf16[2,4,80,512]{3,2,1,0:T(8,128)(2,1)S(1)} collective-permute-done((bf16[2,4,80,512]{3,2,1,0:T(8,128)(2,1)S(1)}, bf16[2,4,80,512]{3,2,1,0:T(8,128)(2,1)S(1)}, u32[]{:S(2)}, u32[]{:S(2)}) %collective-permute-start.28) | collective-permute-done | bytes 655392 | tf_op jit(solution)/shard_map/ppermute | solution.py:713
  154.0 2.3 %add_convert_fusion.4 = (bf16[2,4,64,512]{3,2,1,0:T(8,128)(2,1)}, bf16[2,4,64,512]{3,2,1,0:T(8,128)(2,1)S(1)}) fusion(bf16[4,4,64,512]{3,2,1,0:T(8,128)(2,1)} %shard_map.447, bf16[4,4,64,512]{3,2,1,0:T(8,128)(2,1)S(1)} %collective-permute-done.27), kind=kLoop, calls=%fused_computation.4 | loop fusion | flops 2097152 | bytes 3145728 | tf_op jit(solution)/shard_map/convert_element_type | solution.py:683
  157.3 16.0 %collective-permute-done.34 = bf16[2,64,1024]{2,1,0:T(8,128)(2,1)S(1)} collective-permute-done((bf16[2,64,1024]{2,1,0:T(8,128)(2,1)S(1)}, bf16[2,64,1024]{2,1,0:T(8,128)(2,1)S(1)}, u32[]{:S(2)}, u32[]{:S(2)}) %collective-permute-start.34) | collective-permute-done | bytes 262176 | tf_op jit(solution)/shard_map/ppermute | solution.py:704
  183.3 2.1 collective-permute-done.36
  194.7 4.9 %collective-permute-done.37 = bf16[2,64,512]{2,1,0:T(8,128)(2,1)S(1)} collective-permute-done((bf16[2,64,512]{2,1,0:T(8,128)(2,1)S(1)}, bf16[2,64,512]{2,1,0:T(8,128)(2,1)S(1)}, u32[]{:S(2)}, u32[]{:S(2)}) %collective-permute-start.37) | collective-permute-done | bytes 131104 | tf_op jit(solution)/shard_map/ppermute | solution.py:704
  204.5 3.0 %shard_map.454 = (bf16[8,128,512]{2,1,0:T(8,128)(2,1)}, bf16[8,128,512]{2,1,0:T(8,128)(2,1)}) custom-call(s32[32]{0:T(128)} %stack.102.tab, bf16[4,128,512]{2,1,0:T(8,128)(2,1)} %get-tuple-element.88.refs_0_, bf16[4,128,512]{2,1,0:T(8,128)(2,1)} %shard_map.448.refs_1_, bf16[4,128,512]{2,1,0:T(8,128)(2,1)} %copy-done.42, bf16[4,128,512]{2,1,0:T(8,128)(2,1)} %copy-done.44, ...), custom_call_target="tpu_custom_call" | custom-call | flops 1150000000 | bytes 4259968 | tf_op jit(solution)/shard_map/pallas_call | solution.py:619
  (243 shorter events, 69.2 us)
Async XLA Ops:
  3.2 12.1 %collective-permute-start = (bf16[80,1024]{1,0:T(8,128)(2,1)}, bf16[80,1024]{1,0:T(8,128)(2,1)S(1)}, u32[]{:S(2)}, u32[]{:S(2)}) collective-permute-start(bf16[80,1024]{1,0:T(8,128)(2,1)} %shard_map.434.refs_0_), channel_id=1, source_target_pairs={{0,2},{1,3},{2,0},{3,1},{4,6},{5,7},{6,4},{7,5},{8,10},{9,11},{10,... | collective-permute-start | bytes 491528 | tf_op jit(solution)/shard_map/ppermute | solution.py:704
  7.2 13.1 %collective-permute-start.1 = (bf16[80,1024]{1,0:T(8,128)(2,1)}, bf16[80,1024]{1,0:T(8,128)(2,1)S(1)}, u32[]{:S(2)}, u32[]{:S(2)}) collective-permute-start(bf16[80,1024]{1,0:T(8,128)(2,1)} %shard_map.434.refs_0_), channel_id=1, source_target_pairs={{0,1},{1,0},{2,3},{3,2},{4,5},{5,4},{6,7},{7,6},{8,9},{9,8},{10,11... | collective-permute-start | bytes 491528 | tf_op jit(solution)/shard_map/ppermute | solution.py:704
  23.7 16.2 %collective-permute-start.6 = (bf16[4,80,1024]{2,1,0:T(8,128)(2,1)}, bf16[4,80,1024]{2,1,0:T(8,128)(2,1)S(1)}, u32[]{:S(2)}, u32[]{:S(2)}) collective-permute-start(bf16[4,80,1024]{2,1,0:T(8,128)(2,1)} %shard_map.437.refs_0_.refs_4_.refs_6_), channel_id=1, source_target_pairs={{0,8},{1,9},{2,10},{3,11},{4,20},{5,21},{6,22},{7,23},{8,0},{9,1},... | collective-permute-start | bytes 1966088 | tf_op jit(solution)/shard_map/ppermute | solution.py:710
  43.5 12.2 %collective-permute-start.9 = (bf16[4,80,1024]{2,1,0:T(8,128)(2,1)S(1)}, bf16[4,80,1024]{2,1,0:T(8,128)(2,1)S(1)}, u32[]{:S(2)}, u32[]{:S(2)}) collective-permute-start(bf16[4,80,1024]{2,1,0:T(8,128)(2,1)S(1)} %copy-done.34), channel_id=1, source_target_pairs={{0,4},{1,5},{2,6},{3,7},{4,0},{5,1},{6,2},{7,3},{8,12},{9,13},{10,... | collective-permute-start | bytes 1966088 | tf_op jit(solution)/shard_map/ppermute | solution.py:707
  43.8 20.0 %collective-permute-start.10 = (bf16[4,80,1024]{2,1,0:T(8,128)(2,1)}, bf16[4,80,1024]{2,1,0:T(8,128)(2,1)S(1)}, u32[]{:S(2)}, u32[]{:S(2)}) collective-permute-start(bf16[4,80,1024]{2,1,0:T(8,128)(2,1)} %get-tuple-element.63.refs_1_.refs_5_.refs_7_), channel_id=1, source_target_pairs={{0,4},{1,5},{2,6},{3,7},{4,0},{5,1},{6,2},{7,3},{8,12},{9,13},{10,... | collective-permute-start | bytes 1966088 | tf_op jit(solution)/shard_map/ppermute | solution.py:707
  45.3 21.1 %collective-permute-start.11 = (bf16[4,80,1024]{2,1,0:T(8,128)(2,1)S(1)}, bf16[4,80,1024]{2,1,0:T(8,128)(2,1)S(1)}, u32[]{:S(2)}, u32[]{:S(2)}) collective-permute-start(bf16[4,80,1024]{2,1,0:T(8,128)(2,1)S(1)} %collective-permute-done.7.refs_2_.refs_6_.refs_8_), channel_id=1, source_target_pairs={{0,4},{1,5},{2,6},{3,7},{4,0},{5,1},{6,2},{7,3},{8,12},{9,13},{10,... | collective-permute-start | bytes 1966088 | tf_op jit(solution)/shard_map/ppermute | solution.py:707
  54.1 13.2 %collective-permute-start.12 = (bf16[4,80,1024]{2,1,0:T(8,128)(2,1)S(1)}, bf16[4,80,1024]{2,1,0:T(8,128)(2,1)S(1)}, u32[]{:S(2)}, u32[]{:S(2)}) collective-permute-start(bf16[4,80,1024]{2,1,0:T(8,128)(2,1)S(1)} %collective-permute-done.8.refs_3_.refs_7_.refs_9_), channel_id=1, source_target_pairs={{0,4},{1,5},{2,6},{3,7},{4,0},{5,1},{6,2},{7,3},{8,12},{9,13},{10,... | collective-permute-start | bytes 1966088 | tf_op jit(solution)/shard_map/ppermute | solution.py:707
  55.7 18.6 %collective-permute-start.13 = (bf16[2,128,512]{2,1,0:T(8,128)(2,1)S(1)}, bf16[2,128,512]{2,1,0:T(8,128)(2,1)S(1)}, u32[]{:S(2)}, u32[]{:S(2)}) collective-permute-start(bf16[2,128,512]{2,1,0:T(8,128)(2,1)S(1)} %copy-done.55), channel_id=1, source_target_pairs={{0,2},{1,3},{2,0},{3,1},{4,6},{5,7},{6,4},{7,5},{8,10},{9,11},{10,... | collective-permute-start | bytes 786440 | tf_op jit(solution)/shard_map/ppermute | solution.py:704
  63.5 17.2 %collective-permute-start.14 = (bf16[2,128,512]{2,1,0:T(8,128)(2,1)S(1)}, bf16[2,128,512]{2,1,0:T(8,128)(2,1)S(1)}, u32[]{:S(2)}, u32[]{:S(2)}) collective-permute-start(bf16[2,128,512]{2,1,0:T(8,128)(2,1)S(1)} %copy-done.54), channel_id=1, source_target_pairs={{0,1},{1,0},{2,3},{3,2},{4,5},{5,4},{6,7},{7,6},{8,9},{9,8},{10,11... | collective-permute-start | bytes 786440 | tf_op jit(solution)/shard_map/ppermute | solution.py:704
  63.8 17.7 %collective-permute-start.15 = (bf16[2,128,512]{2,1,0:T(8,128)(2,1)S(1)}, bf16[2,128,512]{2,1,0:T(8,128)(2,1)S(1)}, u32[]{:S(2)}, u32[]{:S(2)}) collective-permute-start(bf16[2,128,512]{2,1,0:T(8,128)(2,1)S(1)} %copy-done.53), channel_id=1, source_target_pairs={{0,3},{1,2},{2,1},{3,0},{4,7},{5,6},{6,5},{7,4},{8,11},{9,10},{10,... | collective-permute-start | bytes 786440 | tf_op jit(solution)/shard_map/ppermute | solution.py:704
  66.5 14.2 %collective-permute-start.17 = (bf16[4,64,1024]{2,1,0:T(8,128)(2,1)}, bf16[4,64,1024]{2,1,0:T(8,128)(2,1)S(1)}, u32[]{:S(2)}, u32[]{:S(2)}) collective-permute-start(bf16[4,64,1024]{2,1,0:T(8,128)(2,1)} %get-tuple-element.64.refs_8_.refs_0_), channel_id=1, source_target_pairs={{0,16},{1,17},{2,18},{3,19},{4,12},{5,13},{6,14},{7,15},{8,24},{9,... | collective-permute-start | bytes 1572872 | tf_op jit(solution)/shard_map/ppermute | solution.py:713
  67.3 14.2 %collective-permute-start.18 = (bf16[4,64,1024]{2,1,0:T(8,128)(2,1)S(1)}, bf16[4,64,1024]{2,1,0:T(8,128)(2,1)S(1)}, u32[]{:S(2)}, u32[]{:S(2)}) collective-permute-start(bf16[4,64,1024]{2,1,0:T(8,128)(2,1)S(1)} %collective-permute-done.16.refs_1_), channel_id=1, source_target_pairs={{0,16},{1,17},{2,18},{3,19},{4,12},{5,13},{6,14},{7,15},{8,24},{9,... | collective-permute-start | bytes 1572872 | tf_op jit(solution)/shard_map/ppermute | solution.py:713
  74.4 17.3 %collective-permute-start.19 = (bf16[4,64,1024]{2,1,0:T(8,128)(2,1)S(1)}, bf16[4,64,1024]{2,1,0:T(8,128)(2,1)S(1)}, u32[]{:S(2)}, u32[]{:S(2)}) collective-permute-start(bf16[4,64,1024]{2,1,0:T(8,128)(2,1)S(1)} %copy-done.43), channel_id=1, source_target_pairs={{0,4},{1,5},{2,6},{3,7},{4,0},{5,1},{6,2},{7,3},{8,12},{9,13},{10,... | collective-permute-start | bytes 1572872 | tf_op jit(solution)/shard_map/ppermute | solution.py:707
  114.7 14.9 %collective-permute-start.25 = (bf16[2,4,64,1024]{3,2,1,0:T(8,128)(2,1)S(1)}, bf16[2,4,64,1024]{3,2,1,0:T(8,128)(2,1)S(1)}, u32[]{:S(2)}, u32[]{:S(2)}) collective-permute-start(bf16[2,4,64,1024]{3,2,1,0:T(8,128)(2,1)S(1)} %get-tuple-element.123.refs_14_), channel_id=1, source_target_pairs={{0,16},{1,17},{2,18},{3,19},{4,12},{5,13},{6,14},{7,15},{8,24},{9,... | collective-permute-start | bytes 3145736 | tf_op jit(solution)/shard_map/ppermute | solution.py:713
  130.8 14.1 %collective-permute-start.29 = (bf16[4,64,1024]{2,1,0:T(8,128)(2,1)S(1)}, bf16[4,64,1024]{2,1,0:T(8,128)(2,1)S(1)}, u32[]{:S(2)}, u32[]{:S(2)}) collective-permute-start(bf16[4,64,1024]{2,1,0:T(8,128)(2,1)S(1)} %get-tuple-element.129.refs_0_), channel_id=1, source_target_pairs={{0,8},{1,9},{2,10},{3,11},{4,20},{5,21},{6,22},{7,23},{8,0},{9,1},... | collective-permute-start | bytes 1572872 | tf_op jit(solution)/shard_map/ppermute | solution.py:710
  140.5 13.5 %collective-permute-start.27 = (bf16[4,4,64,512]{3,2,1,0:T(8,128)(2,1)}, bf16[4,4,64,512]{3,2,1,0:T(8,128)(2,1)S(1)}, u32[]{:S(2)}, u32[]{:S(2)}) collective-permute-start(bf16[4,4,64,512]{3,2,1,0:T(8,128)(2,1)} %get-tuple-element.97), channel_id=1, source_target_pairs={{0,4},{1,5},{2,6},{3,7},{4,0},{5,1},{6,2},{7,3},{8,12},{9,13},{10,... | collective-permute-start | bytes 3145736 | tf_op jit(solution)/shard_map/ppermute | solution.py:707
  141.6 37.2 %collective-permute-start.24 = (bf16[4,128,512]{2,1,0:T(8,128)(2,1)}, bf16[4,128,512]{2,1,0:T(8,128)(2,1)S(1)}, u32[]{:S(2)}, u32[]{:S(2)}) collective-permute-start(bf16[4,128,512]{2,1,0:T(8,128)(2,1)} %get-tuple-element.88.refs_0_), channel_id=1, source_target_pairs={{0,2},{1,3},{2,0},{3,1},{4,6},{5,7},{6,4},{7,5},{8,10},{9,11},{10,... | collective-permute-start | bytes 1572872 | tf_op jit(solution)/shard_map/ppermute | solution.py:704
  142.5 60.4 %collective-permute-start.30 = (bf16[4,128,512]{2,1,0:T(8,128)(2,1)}, bf16[4,128,512]{2,1,0:T(8,128)(2,1)S(1)}, u32[]{:S(2)}, u32[]{:S(2)}) collective-permute-start(bf16[4,128,512]{2,1,0:T(8,128)(2,1)} %get-tuple-element.88.refs_0_), channel_id=1, source_target_pairs={{0,1},{1,0},{2,3},{3,2},{4,5},{5,4},{6,7},{7,6},{8,9},{9,8},{10,11... | collective-permute-start | bytes 1572872 | tf_op jit(solution)/shard_map/ppermute | solution.py:704
  146.8 26.4 %collective-permute-start.34 = (bf16[2,64,1024]{2,1,0:T(8,128)(2,1)S(1)}, bf16[2,64,1024]{2,1,0:T(8,128)(2,1)S(1)}, u32[]{:S(2)}, u32[]{:S(2)}) collective-permute-start(bf16[2,64,1024]{2,1,0:T(8,128)(2,1)S(1)} %get-tuple-element.135.refs_1_), channel_id=1, source_target_pairs={{0,1},{1,0},{2,3},{3,2},{4,5},{5,4},{6,7},{7,6},{8,9},{9,8},{10,11... | collective-permute-start | bytes 786440 | tf_op jit(solution)/shard_map/ppermute | solution.py:704
  153.3 22.3 %collective-permute-start.33 = (bf16[4,80,512]{2,1,0:T(8,128)(2,1)S(1)}, bf16[4,80,512]{2,1,0:T(8,128)(2,1)S(1)}, u32[]{:S(2)}, u32[]{:S(2)}) collective-permute-start(bf16[4,80,512]{2,1,0:T(8,128)(2,1)S(1)} %get-tuple-element.131.refs_1_), channel_id=1, source_target_pairs={{0,8},{1,9},{2,10},{3,11},{4,20},{5,21},{6,22},{7,23},{8,0},{9,1},... | collective-permute-start | bytes 983048 | tf_op jit(solution)/shard_map/ppermute | solution.py:710
  156.3 23.9 %collective-permute-start.32 = (bf16[2,4,64,512]{3,2,1,0:T(8,128)(2,1)S(1)}, bf16[2,4,64,512]{3,2,1,0:T(8,128)(2,1)S(1)}, u32[]{:S(2)}, u32[]{:S(2)}) collective-permute-start(bf16[2,4,64,512]{3,2,1,0:T(8,128)(2,1)S(1)} %get-tuple-element.127.refs_1_), channel_id=1, source_target_pairs={{0,16},{1,17},{2,18},{3,19},{4,12},{5,13},{6,14},{7,15},{8,24},{9,... | collective-permute-start | bytes 1572872 | tf_op jit(solution)/shard_map/ppermute | solution.py:713
  174.9 13.4 %collective-permute-start.40 = (bf16[64,1024]{1,0:T(8,128)(2,1)S(1)}, bf16[64,1024]{1,0:T(8,128)(2,1)S(1)}, u32[]{:S(2)}, u32[]{:S(2)}) collective-permute-start(bf16[64,1024]{1,0:T(8,128)(2,1)S(1)} %get-tuple-element.139.refs_1_), channel_id=1, source_target_pairs={{0,2},{1,3},{2,0},{3,1},{4,6},{5,7},{6,4},{7,5},{8,10},{9,11},{10,... | collective-permute-start | bytes 393224 | tf_op jit(solution)/shard_map/ppermute | solution.py:704
  179.6 23.3 %collective-permute-start.31 = (bf16[4,128,512]{2,1,0:T(8,128)(2,1)}, bf16[4,128,512]{2,1,0:T(8,128)(2,1)S(1)}, u32[]{:S(2)}, u32[]{:S(2)}) collective-permute-start(bf16[4,128,512]{2,1,0:T(8,128)(2,1)} %shard_map.448.refs_1_), channel_id=1, source_target_pairs={{0,1},{1,0},{2,3},{3,2},{4,5},{5,4},{6,7},{7,6},{8,9},{9,8},{10,11... | collective-permute-start | bytes 1572872 | tf_op jit(solution)/shard_map/ppermute | solution.py:704
  187.0 13.4 %collective-permute-start.38 = (bf16[80,512]{1,0:T(8,128)(2,1)S(1)}, bf16[80,512]{1,0:T(8,128)(2,1)S(1)}, u32[]{:S(2)}, u32[]{:S(2)}) collective-permute-start(bf16[80,512]{1,0:T(8,128)(2,1)S(1)} %get-tuple-element.143.refs_1_), channel_id=1, source_target_pairs={{0,2},{1,3},{2,0},{3,1},{4,6},{5,7},{6,4},{7,5},{8,10},{9,11},{10,... | collective-permute-start | bytes 245768 | tf_op jit(solution)/shard_map/ppermute | solution.py:704
  (83 other events, 522.7 us)

commit v3 on v2

--- a/solution.py
+++ b/solution.py
@@ -459,7 +459,7 @@
 
 
 def self_back_kernel(
-    n_slots, n_outs, n_after, rows_held, tab, targets, onehot, gains, falls, gain_two, gain_three, grad_after, low_out, x_all, *refs
+    n_slots, n_outs, n_after, rows_held, tab, targets, onehot, gains, falls, gain_two, gain_three, grad_after, x_all, *refs
 ):
     normed, query, key, value, mixed, totals = refs[:6]
     slots, refs = refs[6 : 6 + n_slots], refs[6 + n_slots + n_after :]
@@ -514,8 +514,7 @@
     fetch_x.wait()
     resident = x_rows[...].reshape(grad_in.shape).astype(f32)
     through, gain_one = root_back(resident, gains[0:1], grad_normed)
-    low_grad[0:rows_held] = low_out[...].reshape(x_rows.shape)
-    low_grad[rows_held:] = (grad_in + through).astype(bf16).reshape(x_rows.shape)
+    low_grad[...] = (grad_in + through).astype(bf16)
     table = lax.dot_general(
         bias_rows[...],
         onehot[...].astype(f32),
@@ -587,11 +586,9 @@
 
 
 def spread_kernel(rows_held, tab, *refs):
-    pieces, outs = refs[:4], refs[-2:]
-    for number, piece in enumerate(pieces):
-        for side, out in enumerate(outs):
-            here = piece[side * rows_held : (side + 1) * rows_held]
-            out[pl.ds(tab[16 + number] * rows_held, rows_held)] = here
+    for side, out in enumerate(refs[-2:]):
+        for number, piece in enumerate(refs[4 * side : 4 * side + 4]):
+            out[pl.ds(tab[16 + number] * rows_held, rows_held)] = piece[...]
 
 
 def shape(dims, dtype):
@@ -610,9 +607,13 @@
     return [(array, "vmem") for array in arrays]
 
 
-def call(kernel, operands, outs, scratch, micros=1, aliases=None, any_outs=()):
+def call(kernel, operands, outs, scratch, micros=1, aliases=None, any_outs=(), room=2):
     spaces = {"smem": pltpu.SMEM, "vmem": pltpu.VMEM, "any": pl.ANY}
     arrays = [array for array, _ in operands]
+    held = [a for a, place in operands if place == "vmem"]
+    held += [o for i, o in enumerate(outs) if i not in any_outs and i not in (aliases or {}).values()]
+    held += [x for x in scratch if hasattr(x, "shape") and hasattr(x, "dtype") and x.dtype in (f32, bf16)]
+    vmem = sum(math.prod(x.shape) * jnp.dtype(x.dtype).itemsize for x in held) + room * 2**20
     moved = sum(a.size * a.dtype.itemsize for a in arrays) + sum(
         math.prod(o.shape) * o.dtype.itemsize for o in outs
     )
@@ -626,7 +627,7 @@
         ),
         input_output_aliases=aliases or {},
         scratch_shapes=scratch,
-        compiler_params=pltpu.CompilerParams(vmem_limit_bytes=VMEM_BYTES),
+        compiler_params=pltpu.CompilerParams(vmem_limit_bytes=min(vmem, VMEM_BYTES)),
         cost_estimate=pl.CostEstimate(flops=int(micros * 1.15e9), bytes_accessed=moved if micros else 0, transcendentals=0),
     )(*arrays)
 
@@ -666,20 +667,36 @@
     pass
 
 
-def gate(array, after):
+def gate(array, after, micros=1):
     (same,) = call(
-        gate_kernel, anys([array] + list(after)), [shape(array.shape, array.dtype)], [], aliases={0: 0}
+        gate_kernel,
+        anys([array] + list(after)),
+        [shape(array.shape, array.dtype)],
+        [],
+        micros=micros,
+        aliases={0: 0},
     )
     return same
 
 
-def fold(arrived, kept, after=()):
+def fold_kernel(arrived, kept, *refs):
+    sent, stays = refs[-2:]
+    half = arrived.shape[0] // 2
+    both = [(arrived[i : i + half], kept[i : i + half]) for i in (half, 0)]
+    for out, (x, y) in zip((sent, stays), both):
+        out[...] = (x.astype(f32) + y.astype(f32)).astype(bf16).reshape(out.shape)
+
+
+def fold(arrived, kept, after=(), plain=True, micros=1):
+    half = arrived.shape[0] // 2
+    dims = ((half,) if half > 1 else ()) + arrived.shape[1:]
+    if not plain:
+        return call(
+            fold_kernel, vmems((arrived, kept)) + anys(after), [shape(dims, bf16)] * 2, [], micros=0
+        )
     if after:
-        kept = gate(kept, after)
-    half = arrived.shape[0] // 2
-    parts = [(arrived[i : i + half], kept[i : i + half]) for i in (half, 0)]
-    if half == 1:
-        parts = [(x[0], y[0]) for x, y in parts]
+        kept = gate(kept, after, micros)
+    parts = [(arrived[i : i + half].reshape(dims), kept[i : i + half].reshape(dims)) for i in (half, 0)]
     return [(x.astype(f32) + y.astype(f32)).astype(bf16) for x, y in parts]
 
 
@@ -719,8 +736,11 @@
         peer = [place_dp ^ 1 ^ (a * second) ^ (b * first) for b in range(2) for a in range(2)]
         return own + peer, [place_mp ^ j for j in self.order]
 
-    def along_z(self, own, after=()):
-        across, near = self.hop_z(own, 2), self.hop_z(own, 1)
+    def along_z(self, own):
+        return [own, self.hop_z(own, 2), self.hop_z(own, 1)]
+
+    def whole_z(self, pieces, after=()):
+        own, across, near = pieces
         if after:
             across = gate(across, after)
         return [own, across, near, self.hop_z(across, 1)]
@@ -754,6 +774,7 @@
             [(tab, "smem")] + vmems((query, keyval, output, gains, table)),
             [shape((rows + EXTRA, 8 * columns), bf16)],
             [],
+            room=56,
         )
         return own
 
@@ -767,7 +788,9 @@
         return own
 
     def weights(self, tab, query, keyval, output, inner, outer, gains, table, encoder, rows_held):
-        attention = self.along_z(self.attention_shard(tab, query, keyval, output, gains, table))
+        attention = self.whole_z(
+            self.along_z(self.attention_shard(tab, query, keyval, output, gains, table))
+        )
         parts = call(
             functools.partial(split_encoder_kernel, rows_held),
             [(tab, "smem")] + anys([encoder]),
@@ -775,7 +798,7 @@
             [dma_sems(3)],
         )
         own_feed = self.feed_shard(inner, outer, [attention[1], parts[0]])
-        feed = self.along_z(own_feed)
+        feed = self.whole_z(self.along_z(own_feed))
         base = self.stack(attention, [own_feed])
         near, far = self.hop_first(base), self.hop_second(base)
         feed_base, near = self.stack_through(feed, near)
@@ -784,18 +807,18 @@
         feed = self.in_plane(feed_base, self.hop_first(feed_base), self.hop_second(feed_base))
         return attention, feed, sources, feed_base
 
-    def reduce_core(self, parts, after=()):
+    def reduce_core(self, parts, *how):
         own, peer = parts
-        return fold(self.hop_core(peer), own, after)
-
-    def reduce_second(self, pair, after=()):
-        return fold(self.hop_second(pair[0]), pair[1], after)
-
-    def reduce_first(self, pair, after=()):
-        return fold(self.hop_first(pair[0]), pair[1], after)
-
-    def reduce_near(self, pair, after=()):
-        return fold(self.hop_z(pair[0], 1), pair[1], after)
+        return fold(self.hop_core(peer), own, *how)
+
+    def reduce_second(self, pair, *how):
+        return fold(self.hop_second(pair[0]), pair[1], *how)
+
+    def reduce_first(self, pair, *how):
+        return fold(self.hop_first(pair[0]), pair[1], *how)
+
+    def reduce_near(self, pair, *how):
+        return fold(self.hop_z(pair[0], 1), pair[1], *how)
 
     def reduce_across(self, pair, after=()):
         sent, kept = pair
@@ -804,11 +827,12 @@
         total = self.hop_z(sent, 2).astype(f32) + kept.astype(f32)
         return total, total[D // self.n_dp :]
 
-    def finish(self, tab, rows_out, feed, cross, own):
+    def finish(self, tab, outputs, row_grads, feed, cross, own):
+        row_grads = self.along_z(row_grads)
         feed = self.reduce_first(feed, [cross[0]])
         own = self.reduce_second(own, [feed[0]])
-        cross = self.reduce_core(cross, [own[0]])
-        pieces = self.along_z(rows_out, [cross[0]])
+        cross = self.reduce_core(cross, [own[0], outputs[3]] + row_grads[1:], True, 20)
+        row_grads = self.whole_z(row_grads, [cross[0]])
         feed = self.reduce_near(feed, [cross[0]])
         own = self.reduce_first(own, [feed[0]])
         cross = self.reduce_second(cross, [own[0]])
@@ -816,18 +840,18 @@
         own = self.reduce_near(own, [cross[0]])
         cross = self.reduce_first(cross, [own[0]])
         cross = self.reduce_near(cross)
-        rows = self.spread(tab, pieces, [cross[0]])
-        return rows, [feed, self.reduce_across(cross), self.reduce_across(own, [cross[0]])]
+        own = self.reduce_across(own, [cross[0]])
+        return self.spread(tab, outputs + row_grads, [own[0]]), [feed, self.reduce_across(cross), own]
 
     def spread(self, tab, pieces, after):
-        piece = pieces[0]
-        half = piece.shape[0] // 2
-        out = shape((half * self.n_mp,) + piece.shape[1:], piece.dtype)
+        rows_held = pieces[0].shape[0]
+        out = shape((rows_held * self.n_mp,) + pieces[0].shape[1:], pieces[0].dtype)
         return call(
-            functools.partial(spread_kernel, half),
+            functools.partial(spread_kernel, rows_held),
             [(tab, "smem")] + vmems(pieces) + anys(after),
             [out, out],
             [],
+            micros=0,
         )
 
 
@@ -865,7 +889,7 @@
         sources = lax.all_to_all(encoder, "mp", split_axis=0, concat_axis=1, tiled=True)
         return [jnp.concatenate((attention, tile), axis=1)], [feed], [sources], feed
 
-    def reduce_core(self, parts):
+    def reduce_core(self, parts, *how):
         return parts
 
     def reduce(self, grads):
@@ -877,15 +901,18 @@
         ).astype(f32)
         return total, lax.psum(grads[0, D:].astype(f32), ALL) if grads.shape[1] > D else None
 
-    def finish(self, tab, rows_out, feed, cross, own):
-        half = rows_out.shape[0] // 2
-        rows = [
-            lax.all_gather(rows_out[i : i + half], "mp", axis=0, tiled=True) for i in (0, half)
-        ]
+    def along_z(self, own):
+        return [own]
+
+    def finish(self, tab, outputs, row_grads, feed, cross, own):
+        rows = [lax.all_gather(x, "mp", axis=0, tiled=True) for x in (outputs[0], row_grads)]
         return rows, [self.reduce(parts[0][0]) for parts in (feed, cross, own)]
 
-    def reduce_second(self, parts):
+    def reduce_second(self, parts, after):
         return parts
+
+    def whole_z(self, pieces, after):
+        return pieces
 
 
 def shards(
@@ -966,7 +993,8 @@
             dma_sems(n_slots),
             pltpu.SemaphoreType.DMA,
         ],
-        micros=6,
+        room=56,
+        micros=30,
     )
     after_cross, normed_two, q_two, k_two, v_two, mix_two, sum_two, source_rows = call(
         functools.partial(cross_forward_kernel, n_slots, n_pieces, rows_held),
@@ -984,6 +1012,7 @@
             shape((rows_held, source_length, D), bf16),
         ],
         [attn_weights, dma_sems(n_slots, PAIRS), dma_sems(n_pieces)],
+        room=56,
         micros=11,
     )
 
@@ -1009,6 +1038,7 @@
             dma_sems(n_outs, PAIRS),
         ],
         any_outs=range(3, 3 + n_outs),
+        room=56,
         micros=10,
     )
     low_out, grad_second, gain_three = feed_result[:3]
@@ -1021,16 +1051,17 @@
         + anys(attn_slots),
         [shape(flat, f32), shape((1, D), f32), shape(paired, bf16), shape(wide, bf16), shape(wide, bf16)],
         [attn_weights, dma_sems(n_slots, PAIRS)],
+        room=56,
         micros=10,
     )
     self_result = call(
         functools.partial(self_back_kernel, n_slots, n_outs, 1, rows_held),
         [(tab, "smem")]
-        + vmems((target_segments, onehot, gain_rows, falls, gain_two, gain_three, grad_first, low_out))
+        + vmems((target_segments, onehot, gain_rows, falls, gain_two, gain_three, grad_first))
         + anys([inputs])
         + vmems((normed_one, q_one, k_one, v_one, mix_one, sum_one))
         + anys(attn_slots + [core_feed[0]]),
-        [shape((2 * rows_held, length, D), bf16)] + grad_outs(EXTRA, 4 * PAIR),
+        [shape(flat, bf16)] + grad_outs(EXTRA, 4 * PAIR),
         [
             attn_weights,
             VM((rows_held, length, D), bf16),
@@ -1045,10 +1076,13 @@
             dma_sems(n_outs, 2 * PAIRS),
         ],
         any_outs=range(1, 1 + n_outs),
+        room=12,
         micros=10,
     )
-    second_feed = plan.reduce_second(core_feed)
-    core_self = plan.reduce_core(self_result[1:])
+    out_pieces = plan.along_z(gate(low_out.reshape(rows_held, length, D), [core_feed[0]]))
+    second_feed = plan.reduce_second(core_feed, out_pieces[1:])
+    core_self = plan.reduce_core(self_result[1:], second_feed[:1], True, 20)
+    out_pieces = plan.whole_z(out_pieces, second_feed[:1])
     cross_grads = call(
         functools.partial(cross_weights_kernel, n_slots, n_outs, 2),
         [(tab, "smem")]
@@ -1066,10 +1100,11 @@
             dma_sems(n_outs, PAIRS),
         ],
         any_outs=range(n_outs),
+        room=12,
         micros=7,
     )
     (outputs, input_grad), ((grad_feed, _), (grad_cross, _), (grad_self, tile)) = plan.finish(
-        tab, self_result[0], second_feed, cross_grads, core_self
+        tab, out_pieces, self_result[0].reshape(rows_held, length, D), second_feed, cross_grads, core_self
     )
 
     def kind(grads, number):

time: 211 us -> 182 us (0.86)
  other arithmetic: 25 us -> 8.21 us
  Pallas kernels: 63.6 us -> 51.6 us
  starting transfers between devices: 38.9 us -> 48.4 us
  waiting for transfers between devices: 71.1 us -> 66 us
  local copies, waits for them, and re-layouts: 9.93 us -> 5.6 us
    convert_element_type x12, other arithmetic: 17.9 us -> 3 us  [fold(): return [(x.astype(f32) + y.astype(f32)).astype(bf16) for x, y in parts]]
    pallas_call x23 -> x27, Pallas kernels: 63.6 us -> 51.6 us  [call(): pl.pallas_call(kernel, out_shape=tuple(outs), in_specs=[pl.BlockSpec(memo...]
    ppermute x18 -> x21, starting transfers between devices: 24.5 us -> 33.7 us  [hop_z(): return lax.ppermute(array, ALL, self.pairs(lambda d, m: (d, m ^ number)))]
    ppermute x18 -> x21, waiting for transfers between devices: 45.5 us -> 39.2 us  [hop_z(): return lax.ppermute(array, ALL, self.pairs(lambda d, m: (d, m ^ number)))]
    unnamed x132 -> x154, local copies, waits for them, and re-layouts: 9.27 us -> 4.94 us
    ppermute x5, waiting for transfers between devices: 6.43 us -> 10.5 us  [hop_first(): lax.ppermute(array, ALL, self.pairs(lambda d, m: (d ^ (4 if d & 1 else 2)...]
    ppermute x7, waiting for transfers between devices: 19.1 us -> 15.6 us  [hop_second(): lax.ppermute(array, ALL, self.pairs(lambda d, m: (d ^ (2 if d & 1 else 4)...]
  transfers between devices with their start and end apart: 41 -> 44, of which waited for: 15 -> 17; matrix products, arithmetic and copies ran while one was open for 10% -> 3% of each run, Pallas kernels for 23% -> 21%
where the time goes in v3:
time: 182 us
  waiting for transfers between devices  66 us (36%)
  Pallas kernels  51.6 us (28%)
  starting transfers between devices  48.4 us (27%)
  other arithmetic  8.21 us (5%)
  local copies, waits for them, and re-layouts  5.6 us (3%)
    pallas_call x27, Pallas kernels, call(): pl.pallas_call(kernel, out_shape=tuple(outs), in_specs=[pl.BlockSpec(memo...  51.6 us
    ppermute x21, waiting for transfers between devices, hop_z(): return lax.ppermute(array, ALL, self.pairs(lambda d, m: (d, m ^ number)))  39.2 us
    ppermute x21, starting transfers between devices, hop_z(): return lax.ppermute(array, ALL, self.pairs(lambda d, m: (d, m ^ number)))  33.7 us
    ppermute x7, waiting for transfers between devices, hop_second(): lax.ppermute(array, ALL, self.pairs(lambda d, m: (d ^ (2 if d & 1 else 4)...  15.6 us
    ppermute x5, waiting for transfers between devices, hop_first(): lax.ppermute(array, ALL, self.pairs(lambda d, m: (d ^ (4 if d & 1 else 2)...  10.5 us
    ppermute x5, starting transfers between devices, hop_first(): lax.ppermute(array, ALL, self.pairs(lambda d, m: (d ^ (4 if d & 1 else 2)...  7.57 us
    ppermute x7, starting transfers between devices, hop_second(): lax.ppermute(array, ALL, self.pairs(lambda d, m: (d ^ (2 if d & 1 else 4)...  5.54 us
    sub x7, other arithmetic, adam_step(): return (new_first, new_second, weight - rate * (ratio + decay * weight))  5.13 us
  transfers between devices with their start and end apart: 44, of which 17 were waited for; matrix products, arithmetic and copies ran while one was open for 3% of the time, Pallas kernels for 21%

profile of v3, /device:TPU:0, one launch (start us, length us, event | category | flops | bytes accessed | tf_op | source)
XLA Modules:
  0.0 181.6 jit_solution(3777478640110454964)
XLA Ops:
  3.3 4.0 %collective-permute-start = (bf16[80,1024]{1,0:T(8,128)(2,1)}, bf16[80,1024]{1,0:T(8,128)(2,1)S(1)}, u32[]{:S(2)}, u32[]{:S(2)}) collective-permute-start(bf16[80,1024]{1,0:T(8,128)(2,1)} %shard_map.434.refs_0_), channel_id=1, source_target_pairs={{0,2},{1,3},{2,0},{3,1},{4,6},{5,7},{6,4},{7,5},{8,10},{9,11},{10,... | collective-permute-start | bytes 491528 | tf_op jit(solution)/shard_map/ppermute | solution.py:721
  8.9 6.4 %collective-permute-done.refs_0_.refs_1_ = bf16[80,1024]{1,0:T(8,128)(2,1)S(1)} collective-permute-done((bf16[80,1024]{1,0:T(8,128)(2,1)}, bf16[80,1024]{1,0:T(8,128)(2,1)S(1)}, u32[]{:S(2)}, u32[]{:S(2)}) %collective-permute-start) | collective-permute-done | bytes 163872 | tf_op jit(solution)/shard_map/ppermute | solution.py:721
  16.8 3.9 %collective-permute-done.2.refs_3_ = bf16[80,1024]{1,0:T(8,128)(2,1)S(1)} collective-permute-done((bf16[80,1024]{1,0:T(8,128)(2,1)S(1)}, bf16[80,1024]{1,0:T(8,128)(2,1)S(1)}, u32[]{:S(2)}, u32[]{:S(2)}) %collective-permute-start.2) | collective-permute-done | bytes 163872 | tf_op jit(solution)/shard_map/ppermute | solution.py:721
  22.3 3.0 %collective-permute-start.3 = (bf16[64,1024]{1,0:T(8,128)(2,1)S(1)}, bf16[64,1024]{1,0:T(8,128)(2,1)S(1)}, u32[]{:S(2)}, u32[]{:S(2)}) collective-permute-start(bf16[64,1024]{1,0:T(8,128)(2,1)S(1)} %shard_map.436.refs_4_.refs_0_), channel_id=1, source_target_pairs={{0,2},{1,3},{2,0},{3,1},{4,6},{5,7},{6,4},{7,5},{8,10},{9,11},{10,... | collective-permute-start | bytes 393224 | tf_op jit(solution)/shard_map/ppermute | solution.py:721
  27.1 4.0 %collective-permute-done.3.refs_1_ = bf16[64,1024]{1,0:T(8,128)(2,1)S(1)} collective-permute-done((bf16[64,1024]{1,0:T(8,128)(2,1)S(1)}, bf16[64,1024]{1,0:T(8,128)(2,1)S(1)}, u32[]{:S(2)}, u32[]{:S(2)}) %collective-permute-start.3) | collective-permute-done | bytes 131104 | tf_op jit(solution)/shard_map/ppermute | solution.py:721
  32.3 3.7 %collective-permute-done.5.refs_3_ = bf16[64,1024]{1,0:T(8,128)(2,1)S(1)} collective-permute-done((bf16[64,1024]{1,0:T(8,128)(2,1)S(1)}, bf16[64,1024]{1,0:T(8,128)(2,1)S(1)}, u32[]{:S(2)}, u32[]{:S(2)}) %collective-permute-start.5) | collective-permute-done | bytes 131104 | tf_op jit(solution)/shard_map/ppermute | solution.py:721
  37.3 5.0 %collective-permute-done.7.refs_2_.refs_6_.refs_8_ = bf16[4,80,1024]{2,1,0:T(8,128)(2,1)S(1)} collective-permute-done((bf16[4,80,1024]{2,1,0:T(8,128)(2,1)S(1)}, bf16[4,80,1024]{2,1,0:T(8,128)(2,1)S(1)}, u32[]{:S(2)}, u32[]{:S(2)}) %collective-permute-start.7) | collective-permute-done | bytes 655392 | tf_op jit(solution)/shard_map/ppermute | solution.py:730
  42.3 7.0 %collective-permute-done.8.refs_3_.refs_7_.refs_9_ = bf16[4,80,1024]{2,1,0:T(8,128)(2,1)S(1)} collective-permute-done((bf16[4,80,1024]{2,1,0:T(8,128)(2,1)S(1)}, bf16[4,80,1024]{2,1,0:T(8,128)(2,1)S(1)}, u32[]{:S(2)}, u32[]{:S(2)}) %collective-permute-start.8) | collective-permute-done | bytes 655392 | tf_op jit(solution)/shard_map/ppermute | solution.py:730
  50.8 3.4 %collective-permute-start.13 = (bf16[2,128,512]{2,1,0:T(8,128)(2,1)S(1)}, bf16[2,128,512]{2,1,0:T(8,128)(2,1)S(1)}, u32[]{:S(2)}, u32[]{:S(2)}) collective-permute-start(bf16[2,128,512]{2,1,0:T(8,128)(2,1)S(1)} %get-tuple-element.62.refs_1_), channel_id=1, source_target_pairs={{0,2},{1,3},{2,0},{3,1},{4,6},{5,7},{6,4},{7,5},{8,10},{9,11},{10,... | collective-permute-start | bytes 786440 | tf_op jit(solution)/shard_map/ppermute | solution.py:721
  54.2 4.3 %collective-permute-done.16.refs_1_ = bf16[4,64,1024]{2,1,0:T(8,128)(2,1)S(1)} collective-permute-done((bf16[4,64,1024]{2,1,0:T(8,128)(2,1)S(1)}, bf16[4,64,1024]{2,1,0:T(8,128)(2,1)S(1)}, u32[]{:S(2)}, u32[]{:S(2)}) %collective-permute-start.16) | collective-permute-done | bytes 524320 | tf_op jit(solution)/shard_map/ppermute | solution.py:727
  59.9 3.4 %collective-permute-start.15 = (bf16[2,128,512]{2,1,0:T(8,128)(2,1)S(1)}, bf16[2,128,512]{2,1,0:T(8,128)(2,1)S(1)}, u32[]{:S(2)}, u32[]{:S(2)}) collective-permute-start(bf16[2,128,512]{2,1,0:T(8,128)(2,1)S(1)} %get-tuple-element.68), channel_id=1, source_target_pairs={{0,3},{1,2},{2,1},{3,0},{4,7},{5,6},{6,5},{7,4},{8,11},{9,10},{10,... | collective-permute-start | bytes 786440 | tf_op jit(solution)/shard_map/ppermute | solution.py:721
  65.5 5.8 %shard_map.439 = (f32[256,512]{1,0:T(8,128)}, bf16[256,512]{1,0:T(8,128)(2,1)}, bf16[4,256,128]{2,1,0:T(8,128)(2,1)}, bf16[4,256,128]{2,1,0:T(8,128)(2,1)}, bf16...) custom-call(s32[32]{0:T(128)} %stack.102.tab, ...), custom_call_target="tpu_custom_call" | custom-call | flops 34500001792 | bytes 8716416 | tf_op jit(solution)/shard_map/pallas_call | solution.py:620
  71.4 5.5 %collective-permute-done.14.refs_10_ = bf16[2,128,512]{2,1,0:T(8,128)(2,1)S(1)} collective-permute-done((bf16[2,128,512]{2,1,0:T(8,128)(2,1)S(1)}, bf16[2,128,512]{2,1,0:T(8,128)(2,1)S(1)}, u32[]{:S(2)}, u32[]{:S(2)}) %collective-permute-start.14) | collective-permute-done | bytes 262176 | tf_op jit(solution)/shard_map/ppermute | solution.py:721
  79.0 9.4 %shard_map.440 = (f32[256,512]{1,0:T(8,128)}, bf16[256,512]{1,0:T(8,128)(2,1)}, bf16[4,256,128]{2,1,0:T(8,128)(2,1)}, bf16[4,1024,128]{2,1,0:T(8,128)(2,1)}, bf1...) custom-call(s32[32]{0:T(128)} %stack.102.tab, ...), custom_call_target="tpu_custom_call" | custom-call | flops 12650000384 | bytes 12103808 | tf_op jit(solution)/shard_map/pallas_call | solution.py:620
  89.7 11.1 %shard_map.441 = (bf16[256,512]{1,0:T(8,128)(2,1)}, f32[256,512]{1,0:T(8,128)}, f32[1,512]{1,0:T(1,128)}, bf16[4,4,64,1024]{3,2,1,0:T(8,128)(2,1)}, bf16[4,4,64,1024]{3,2,1,0:T(8,128)(2,1)}) custom-call(s32[32]{0:T(128)} %stack.102.tab, f32[8,512]{1,0:T(8,128)} %get-tuple-element.65.gains, f32[256,512]{1,0:T(8,128)} %get-tuple-element.69.before, ...), custom_call_target="tpu_custom_call" | custom-call | flops 11500000256 | bytes 10766464 | tf_op jit(solution)/shard_map/pallas_call | solution.py:620
  101.4 9.0 %shard_map.445 = (f32[256,512]{1,0:T(8,128)}, f32[1,512]{1,0:T(1,128)}, bf16[4,256,128]{2,1,0:T(8,128)(2,1)}, bf16[4,1024,128]{2,1,0:T(8,128)(2,1)}, bf16[4,1024,128]{2,1,0:T(8,128)(2,1)}) custom-call(s32[32]{0:T(128)} %stack.102.tab, s32[8,128]{1,0:T(8,128)} %targets.7, s32[8,512]{1,0:T(8,128)} %sources.3, f32[8,512]{1,0:T(8,128)} %get-tuple-element.65.gains, ...), custom_call_target="tpu_custom_call" | custom-call | flops 11500000256 | bytes 11581568 | tf_op jit(solution)/shard_map/pallas_call | solution.py:620
  114.7 6.9 %shard_map.446 = (bf16[256,512]{1,0:T(8,128)(2,1)S(1)}, bf16[4,4,80,512]{3,2,1,0:T(8,128)(2,1)S(1)}, bf16[4,4,80,512]{3,2,1,0:T(8,128)(2,1)S(1)}) custom-call(s32[32]{0:T(128)S(1)} %copy-done.6, s32[8,128]{1,0:T(8,128)S(1)} %copy-done.27, bf16[128,128]{1,0:T(8,128)(2,1)S(1)} %copy-done.28, f32[8,512]{1,0:T(8,128)S(1)} %copy-done.42, ...), custom_call_target="tpu_custom_call" | custom-call | flops 11500000256 | bytes 12128384 | tf_op jit(solution)/shard_map/pallas_call | solution.py:620
  126.0 2.5 %collective-permute-done.25 = bf16[2,4,64,1024]{3,2,1,0:T(8,128)(2,1)S(1)} collective-permute-done((bf16[2,4,64,1024]{3,2,1,0:T(8,128)(2,1)S(1)}, bf16[2,4,64,1024]{3,2,1,0:T(8,128)(2,1)S(1)}, u32[]{:S(2)}, u32[]{:S(2)}) %collective-permute-start.25) | collective-permute-done | bytes 1048608 | tf_op jit(solution)/shard_map/ppermute | solution.py:730
  132.9 4.7 %shard_map.448 = (bf16[4,4,64,512]{3,2,1,0:T(8,128)(2,1)S(1)}, bf16[4,4,64,512]{3,2,1,0:T(8,128)(2,1)S(1)}) custom-call(s32[32]{0:T(128)S(1)} %copy-done.6, f32[256,512]{1,0:T(8,128)S(1)} %copy-done.32, bf16[256,512]{1,0:T(8,128)(2,1)S(1)} %copy-done.34, bf16[4,256,128]{2,1,0:T(8,128)(2,1)S(1)} %copy-done.35, bf16[2,512,512]{2,1,0:T(8,128)(2,1)S(1)} %copy-done.29, ...), custom_call_target="tpu_custom_call" | custom-call | flops 8049999872 | bytes 7733376 | tf_op jit(solution)/shard_map/pallas_call | solution.py:620
  137.6 6.2 %collective-permute-done.32 = bf16[4,64,1024]{2,1,0:T(8,128)(2,1)S(1)} collective-permute-done((bf16[4,64,1024]{2,1,0:T(8,128)(2,1)S(1)}, bf16[4,64,1024]{2,1,0:T(8,128)(2,1)S(1)}, u32[]{:S(2)}, u32[]{:S(2)}) %collective-permute-start.32) | collective-permute-done | bytes 524320 | tf_op jit(solution)/shard_map/ppermute | solution.py:727
  147.5 5.3 %collective-permute-done.36 = bf16[2,64,1024]{2,1,0:T(8,128)(2,1)S(1)} collective-permute-done((bf16[2,64,1024]{2,1,0:T(8,128)(2,1)S(1)}, bf16[2,64,1024]{2,1,0:T(8,128)(2,1)S(1)}, u32[]{:S(2)}, u32[]{:S(2)}) %collective-permute-start.36) | collective-permute-done | bytes 262176 | tf_op jit(solution)/shard_map/ppermute | solution.py:721
  158.6 6.4 %collective-permute-done.37 = bf16[2,80,512]{2,1,0:T(8,128)(2,1)S(1)} collective-permute-done((bf16[2,80,512]{2,1,0:T(8,128)(2,1)S(1)}, bf16[2,80,512]{2,1,0:T(8,128)(2,1)S(1)}, u32[]{:S(2)}, u32[]{:S(2)}) %collective-permute-start.37) | collective-permute-done | bytes 163872 | tf_op jit(solution)/shard_map/ppermute | solution.py:721
  167.7 2.7 %collective-permute-start.41 = (bf16[2,64,512]{2,1,0:T(8,128)(2,1)S(1)}, bf16[2,64,512]{2,1,0:T(8,128)(2,1)S(1)}, u32[]{:S(2)}, u32[]{:S(2)}) collective-permute-start(bf16[2,64,512]{2,1,0:T(8,128)(2,1)S(1)} %get-tuple-element.140), channel_id=1, source_target_pairs={{0,1},{1,0},{2,3},{3,2},{4,5},{5,4},{6,7},{7,6},{8,9},{9,8},{10,11... | collective-permute-start | bytes 393224 | tf_op jit(solution)/shard_map/ppermute | solution.py:721
  171.2 2.3 %collective-permute-done.41 = bf16[2,64,512]{2,1,0:T(8,128)(2,1)S(1)} collective-permute-done((bf16[2,64,512]{2,1,0:T(8,128)(2,1)S(1)}, bf16[2,64,512]{2,1,0:T(8,128)(2,1)S(1)}, u32[]{:S(2)}, u32[]{:S(2)}) %collective-permute-start.41) | collective-permute-done | bytes 131104 | tf_op jit(solution)/shard_map/ppermute | solution.py:721
  (275 shorter events, 53.7 us)
Async XLA Ops:
  3.3 12.1 %collective-permute-start = (bf16[80,1024]{1,0:T(8,128)(2,1)}, bf16[80,1024]{1,0:T(8,128)(2,1)S(1)}, u32[]{:S(2)}, u32[]{:S(2)}) collective-permute-start(bf16[80,1024]{1,0:T(8,128)(2,1)} %shard_map.434.refs_0_), channel_id=1, source_target_pairs={{0,2},{1,3},{2,0},{3,1},{4,6},{5,7},{6,4},{7,5},{8,10},{9,11},{10,... | collective-permute-start | bytes 491528 | tf_op jit(solution)/shard_map/ppermute | solution.py:721
  20.7 15.3 %collective-permute-start.6 = (bf16[4,80,1024]{2,1,0:T(8,128)(2,1)S(1)}, bf16[4,80,1024]{2,1,0:T(8,128)(2,1)S(1)}, u32[]{:S(2)}, u32[]{:S(2)}) collective-permute-start(bf16[4,80,1024]{2,1,0:T(8,128)(2,1)S(1)} %shard_map.437.refs_0_.refs_4_.refs_6_), channel_id=1, source_target_pairs={{0,8},{1,9},{2,10},{3,11},{4,20},{5,21},{6,22},{7,23},{8,0},{9,1},... | collective-permute-start | bytes 1966088 | tf_op jit(solution)/shard_map/ppermute | solution.py:727
  36.1 13.2 %collective-permute-start.8 = (bf16[4,80,1024]{2,1,0:T(8,128)(2,1)S(1)}, bf16[4,80,1024]{2,1,0:T(8,128)(2,1)S(1)}, u32[]{:S(2)}, u32[]{:S(2)}) collective-permute-start(bf16[4,80,1024]{2,1,0:T(8,128)(2,1)S(1)} %get-tuple-element.63.refs_1_.refs_5_.refs_7_), channel_id=1, source_target_pairs={{0,16},{1,17},{2,18},{3,19},{4,12},{5,13},{6,14},{7,15},{8,24},{9,... | collective-permute-start | bytes 1966088 | tf_op jit(solution)/shard_map/ppermute | solution.py:730
  36.8 14.0 %collective-permute-start.9 = (bf16[4,80,1024]{2,1,0:T(8,128)(2,1)S(1)}, bf16[4,80,1024]{2,1,0:T(8,128)(2,1)S(1)}, u32[]{:S(2)}, u32[]{:S(2)}) collective-permute-start(bf16[4,80,1024]{2,1,0:T(8,128)(2,1)S(1)} %shard_map.437.refs_0_.refs_4_.refs_6_), channel_id=1, source_target_pairs={{0,4},{1,5},{2,6},{3,7},{4,0},{5,1},{6,2},{7,3},{8,12},{9,13},{10,... | collective-permute-start | bytes 1966088 | tf_op jit(solution)/shard_map/ppermute | solution.py:724
  36.8 23.1 %collective-permute-start.10 = (bf16[4,80,1024]{2,1,0:T(8,128)(2,1)S(1)}, bf16[4,80,1024]{2,1,0:T(8,128)(2,1)S(1)}, u32[]{:S(2)}, u32[]{:S(2)}) collective-permute-start(bf16[4,80,1024]{2,1,0:T(8,128)(2,1)S(1)} %get-tuple-element.63.refs_1_.refs_5_.refs_7_), channel_id=1, source_target_pairs={{0,4},{1,5},{2,6},{3,7},{4,0},{5,1},{6,2},{7,3},{8,12},{9,13},{10,... | collective-permute-start | bytes 1966088 | tf_op jit(solution)/shard_map/ppermute | solution.py:724
  42.3 21.1 %collective-permute-start.11 = (bf16[4,80,1024]{2,1,0:T(8,128)(2,1)S(1)}, bf16[4,80,1024]{2,1,0:T(8,128)(2,1)S(1)}, u32[]{:S(2)}, u32[]{:S(2)}) collective-permute-start(bf16[4,80,1024]{2,1,0:T(8,128)(2,1)S(1)} %collective-permute-done.7.refs_2_.refs_6_.refs_8_), channel_id=1, source_target_pairs={{0,4},{1,5},{2,6},{3,7},{4,0},{5,1},{6,2},{7,3},{8,12},{9,13},{10,... | collective-permute-start | bytes 1966088 | tf_op jit(solution)/shard_map/ppermute | solution.py:724
  49.3 14.7 %collective-permute-start.12 = (bf16[4,80,1024]{2,1,0:T(8,128)(2,1)S(1)}, bf16[4,80,1024]{2,1,0:T(8,128)(2,1)S(1)}, u32[]{:S(2)}, u32[]{:S(2)}) collective-permute-start(bf16[4,80,1024]{2,1,0:T(8,128)(2,1)S(1)} %collective-permute-done.8.refs_3_.refs_7_.refs_9_), channel_id=1, source_target_pairs={{0,4},{1,5},{2,6},{3,7},{4,0},{5,1},{6,2},{7,3},{8,12},{9,13},{10,... | collective-permute-start | bytes 1966088 | tf_op jit(solution)/shard_map/ppermute | solution.py:724
  50.8 20.4 %collective-permute-start.13 = (bf16[2,128,512]{2,1,0:T(8,128)(2,1)S(1)}, bf16[2,128,512]{2,1,0:T(8,128)(2,1)S(1)}, u32[]{:S(2)}, u32[]{:S(2)}) collective-permute-start(bf16[2,128,512]{2,1,0:T(8,128)(2,1)S(1)} %get-tuple-element.62.refs_1_), channel_id=1, source_target_pairs={{0,2},{1,3},{2,0},{3,1},{4,6},{5,7},{6,4},{7,5},{8,10},{9,11},{10,... | collective-permute-start | bytes 786440 | tf_op jit(solution)/shard_map/ppermute | solution.py:721
  58.5 18.4 %collective-permute-start.14 = (bf16[2,128,512]{2,1,0:T(8,128)(2,1)S(1)}, bf16[2,128,512]{2,1,0:T(8,128)(2,1)S(1)}, u32[]{:S(2)}, u32[]{:S(2)}) collective-permute-start(bf16[2,128,512]{2,1,0:T(8,128)(2,1)S(1)} %get-tuple-element.67), channel_id=1, source_target_pairs={{0,1},{1,0},{2,3},{3,2},{4,5},{5,4},{6,7},{7,6},{8,9},{9,8},{10,11... | collective-permute-start | bytes 786440 | tf_op jit(solution)/shard_map/ppermute | solution.py:721
  59.9 18.3 %collective-permute-start.15 = (bf16[2,128,512]{2,1,0:T(8,128)(2,1)S(1)}, bf16[2,128,512]{2,1,0:T(8,128)(2,1)S(1)}, u32[]{:S(2)}, u32[]{:S(2)}) collective-permute-start(bf16[2,128,512]{2,1,0:T(8,128)(2,1)S(1)} %get-tuple-element.68), channel_id=1, source_target_pairs={{0,3},{1,2},{2,1},{3,0},{4,7},{5,6},{6,5},{7,4},{8,11},{9,10},{10,... | collective-permute-start | bytes 786440 | tf_op jit(solution)/shard_map/ppermute | solution.py:721
  63.4 13.6 %collective-permute-start.17 = (bf16[4,64,1024]{2,1,0:T(8,128)(2,1)S(1)}, bf16[4,64,1024]{2,1,0:T(8,128)(2,1)S(1)}, u32[]{:S(2)}, u32[]{:S(2)}) collective-permute-start(bf16[4,64,1024]{2,1,0:T(8,128)(2,1)S(1)} %get-tuple-element.64.refs_8_.refs_0_), channel_id=1, source_target_pairs={{0,16},{1,17},{2,18},{3,19},{4,12},{5,13},{6,14},{7,15},{8,24},{9,... | collective-permute-start | bytes 1572872 | tf_op jit(solution)/shard_map/ppermute | solution.py:730
  64.0 14.2 %collective-permute-start.18 = (bf16[4,64,1024]{2,1,0:T(8,128)(2,1)S(1)}, bf16[4,64,1024]{2,1,0:T(8,128)(2,1)S(1)}, u32[]{:S(2)}, u32[]{:S(2)}) collective-permute-start(bf16[4,64,1024]{2,1,0:T(8,128)(2,1)S(1)} %collective-permute-done.16.refs_1_), channel_id=1, source_target_pairs={{0,16},{1,17},{2,18},{3,19},{4,12},{5,13},{6,14},{7,15},{8,24},{9,... | collective-permute-start | bytes 1572872 | tf_op jit(solution)/shard_map/ppermute | solution.py:730
  71.3 17.1 %collective-permute-start.19 = (bf16[4,64,1024]{2,1,0:T(8,128)(2,1)}, bf16[4,64,1024]{2,1,0:T(8,128)(2,1)S(1)}, u32[]{:S(2)}, u32[]{:S(2)}) collective-permute-start(bf16[4,64,1024]{2,1,0:T(8,128)(2,1)} %copy-done.25), channel_id=1, source_target_pairs={{0,4},{1,5},{2,6},{3,7},{4,0},{5,1},{6,2},{7,3},{8,12},{9,13},{10,... | collective-permute-start | bytes 1572872 | tf_op jit(solution)/shard_map/ppermute | solution.py:724
  76.9 11.5 %collective-permute-start.20 = (bf16[4,64,1024]{2,1,0:T(8,128)(2,1)S(1)}, bf16[4,64,1024]{2,1,0:T(8,128)(2,1)S(1)}, u32[]{:S(2)}, u32[]{:S(2)}) collective-permute-start(bf16[4,64,1024]{2,1,0:T(8,128)(2,1)S(1)} %collective-permute-done.16.refs_1_), channel_id=1, source_target_pairs={{0,4},{1,5},{2,6},{3,7},{4,0},{5,1},{6,2},{7,3},{8,12},{9,13},{10,... | collective-permute-start | bytes 1572872 | tf_op jit(solution)/shard_map/ppermute | solution.py:724
  111.7 14.2 %collective-permute-start.24 = (bf16[2,128,512]{2,1,0:T(8,128)(2,1)S(1)}, bf16[2,128,512]{2,1,0:T(8,128)(2,1)S(1)}, u32[]{:S(2)}, u32[]{:S(2)}) collective-permute-start(bf16[2,128,512]{2,1,0:T(8,128)(2,1)S(1)} %shard_map.442.refs_0_), channel_id=1, source_target_pairs={{0,2},{1,3},{2,0},{3,1},{4,6},{5,7},{6,4},{7,5},{8,10},{9,11},{10,... | collective-permute-start | bytes 786440 | tf_op jit(solution)/shard_map/ppermute | solution.py:721
  111.8 14.2 %collective-permute-start.26 = (bf16[2,128,512]{2,1,0:T(8,128)(2,1)S(1)}, bf16[2,128,512]{2,1,0:T(8,128)(2,1)S(1)}, u32[]{:S(2)}, u32[]{:S(2)}) collective-permute-start(bf16[2,128,512]{2,1,0:T(8,128)(2,1)S(1)} %shard_map.442.refs_0_), channel_id=1, source_target_pairs={{0,1},{1,0},{2,3},{3,2},{4,5},{5,4},{6,7},{7,6},{8,9},{9,8},{10,11... | collective-permute-start | bytes 786440 | tf_op jit(solution)/shard_map/ppermute | solution.py:721
  113.6 14.8 %collective-permute-start.25 = (bf16[2,4,64,1024]{3,2,1,0:T(8,128)(2,1)S(1)}, bf16[2,4,64,1024]{3,2,1,0:T(8,128)(2,1)S(1)}, u32[]{:S(2)}, u32[]{:S(2)}) collective-permute-start(bf16[2,4,64,1024]{3,2,1,0:T(8,128)(2,1)S(1)} %get-tuple-element.123.refs_1_.refs_14_), channel_id=1, source_target_pairs={{0,16},{1,17},{2,18},{3,19},{4,12},{5,13},{6,14},{7,15},{8,24},{9,... | collective-permute-start | bytes 3145736 | tf_op jit(solution)/shard_map/ppermute | solution.py:730
  121.5 22.7 %collective-permute-start.28 = (bf16[2,128,512]{2,1,0:T(8,128)(2,1)S(1)}, bf16[2,128,512]{2,1,0:T(8,128)(2,1)S(1)}, u32[]{:S(2)}, u32[]{:S(2)}) collective-permute-start(bf16[2,128,512]{2,1,0:T(8,128)(2,1)S(1)} %bitcast.84), channel_id=1, source_target_pairs={{0,2},{1,3},{2,0},{3,1},{4,6},{5,7},{6,4},{7,5},{8,10},{9,11},{10,... | collective-permute-start | bytes 786440 | tf_op jit(solution)/shard_map/ppermute | solution.py:721
  122.5 23.3 %collective-permute-start.33 = (bf16[2,128,512]{2,1,0:T(8,128)(2,1)S(1)}, bf16[2,128,512]{2,1,0:T(8,128)(2,1)S(1)}, u32[]{:S(2)}, u32[]{:S(2)}) collective-permute-start(bf16[2,128,512]{2,1,0:T(8,128)(2,1)S(1)} %bitcast.85), channel_id=1, source_target_pairs={{0,1},{1,0},{2,3},{3,2},{4,5},{5,4},{6,7},{7,6},{8,9},{9,8},{10,11... | collective-permute-start | bytes 786440 | tf_op jit(solution)/shard_map/ppermute | solution.py:721
  128.9 14.9 %collective-permute-start.32 = (bf16[4,64,1024]{2,1,0:T(8,128)(2,1)S(1)}, bf16[4,64,1024]{2,1,0:T(8,128)(2,1)S(1)}, u32[]{:S(2)}, u32[]{:S(2)}) collective-permute-start(bf16[4,64,1024]{2,1,0:T(8,128)(2,1)S(1)} %get-tuple-element.129.refs_1_.refs_0_), channel_id=1, source_target_pairs={{0,8},{1,9},{2,10},{3,11},{4,20},{5,21},{6,22},{7,23},{8,0},{9,1},... | collective-permute-start | bytes 1572872 | tf_op jit(solution)/shard_map/ppermute | solution.py:727
  130.3 15.4 %collective-permute-start.27 = (bf16[2,128,512]{2,1,0:T(8,128)(2,1)S(1)}, bf16[2,128,512]{2,1,0:T(8,128)(2,1)S(1)}, u32[]{:S(2)}, u32[]{:S(2)}) collective-permute-start(bf16[2,128,512]{2,1,0:T(8,128)(2,1)S(1)} %shard_map.444.refs_1_), channel_id=1, source_target_pairs={{0,1},{1,0},{2,3},{3,2},{4,5},{5,4},{6,7},{7,6},{8,9},{9,8},{10,11... | collective-permute-start | bytes 786440 | tf_op jit(solution)/shard_map/ppermute | solution.py:721
  131.2 12.8 %collective-permute-start.31 = (bf16[2,4,80,512]{3,2,1,0:T(8,128)(2,1)S(1)}, bf16[2,4,80,512]{3,2,1,0:T(8,128)(2,1)S(1)}, u32[]{:S(2)}, u32[]{:S(2)}) collective-permute-start(bf16[2,4,80,512]{3,2,1,0:T(8,128)(2,1)S(1)} %get-tuple-element.125.refs_1_), channel_id=1, source_target_pairs={{0,16},{1,17},{2,18},{3,19},{4,12},{5,13},{6,14},{7,15},{8,24},{9,... | collective-permute-start | bytes 1966088 | tf_op jit(solution)/shard_map/ppermute | solution.py:730
  152.9 12.8 %collective-permute-start.43 = (bf16[64,1024]{1,0:T(8,128)(2,1)S(1)}, bf16[64,1024]{1,0:T(8,128)(2,1)S(1)}, u32[]{:S(2)}, u32[]{:S(2)}) collective-permute-start(bf16[64,1024]{1,0:T(8,128)(2,1)S(1)} %get-tuple-element.139.refs_1_), channel_id=1, source_target_pairs={{0,2},{1,3},{2,0},{3,1},{4,6},{5,7},{6,4},{7,5},{8,10},{9,11},{10,... | collective-permute-start | bytes 393224 | tf_op jit(solution)/shard_map/ppermute | solution.py:721
  156.5 20.7 %collective-permute-start.34 = (bf16[2,128,512]{2,1,0:T(8,128)(2,1)S(1)}, bf16[2,128,512]{2,1,0:T(8,128)(2,1)S(1)}, u32[]{:S(2)}, u32[]{:S(2)}) collective-permute-start(bf16[2,128,512]{2,1,0:T(8,128)(2,1)S(1)} %shard_map.452.refs_5_), channel_id=1, source_target_pairs={{0,1},{1,0},{2,3},{3,2},{4,5},{5,4},{6,7},{7,6},{8,9},{9,8},{10,11... | collective-permute-start | bytes 786440 | tf_op jit(solution)/shard_map/ppermute | solution.py:721
  (97 other events, 556.4 us)

commit v4 on v3

--- a/solution.py
+++ b/solution.py
@@ -20,7 +20,7 @@
 PAIR = 2 * HEAD_DIM
 HIDDEN = FF // PAIRS
 EXTRA = 16
-GROUPS = tuple((i, i + 1) for i in range(0, PAIRS, 2))
+GROUPS = (tuple(range(PAIRS)),)
 VMEM_BYTES = 56 * 1024 * 1024
 
 norm_eps = 1e-06
@@ -123,23 +123,19 @@
 
 def weight_copies(slots, weights, tab, sems, first=0):
     copies = []
-    for pair in range(PAIRS):
-        row = []
-        for number, slot in enumerate(slots):
-            rows = weights.shape[1] // len(slots)
-            start = pl.multiple_of(tab[number] * rows, rows)
-            row.append(
-                pltpu.make_async_copy(
-                    slot.at[pair, pl.ds(0, rows), pl.ds(first, weights.shape[2])],
-                    weights.at[pair, pl.ds(start, rows), :],
-                    sems.at[number, pair],
-                )
+    for number, slot in enumerate(slots):
+        rows = weights.shape[1] // len(slots)
+        start = pl.multiple_of(tab[number] * rows, rows)
+        copies.append(
+            pltpu.make_async_copy(
+                slot.at[:, pl.ds(0, rows), pl.ds(first, weights.shape[2])],
+                weights.at[:, pl.ds(start, rows), :],
+                sems.at[number, 0],
             )
-        copies.append(row)
-    for row in copies:
-        for copy in row:
-            copy.start()
-    return copies
+        )
+    for copy in copies:
+        copy.start()
+    return [copies] + [[]] * (PAIRS - 1)
 
 
 def wait_for(copies):
@@ -691,6 +687,8 @@
     half = arrived.shape[0] // 2
     dims = ((half,) if half > 1 else ()) + arrived.shape[1:]
     if not plain:
+        if micros > 1:
+            kept, after = gate(kept, after, micros), ()
         return call(
             fold_kernel, vmems((arrived, kept)) + anys(after), [shape(dims, bf16)] * 2, [], micros=0
         )
@@ -829,19 +827,20 @@
 
     def finish(self, tab, outputs, row_grads, feed, cross, own):
         row_grads = self.along_z(row_grads)
+        cross = self.reduce_core(cross, [own[0]] + row_grads[1:], False, 20)
+        row_grads = self.whole_z(row_grads, [cross[0]])
         feed = self.reduce_first(feed, [cross[0]])
         own = self.reduce_second(own, [feed[0]])
-        cross = self.reduce_core(cross, [own[0], outputs[3]] + row_grads[1:], True, 20)
-        row_grads = self.whole_z(row_grads, [cross[0]])
-        feed = self.reduce_near(feed, [cross[0]])
-        own = self.reduce_first(own, [feed[0]])
-        cross = self.reduce_second(cross, [own[0]])
+        cross = self.reduce_second(cross, [own[0], outputs[3]])
+        own = self.reduce_first(own, [cross[0]])
+        feed = self.reduce_near(feed, [own[0]])
+        cross = self.reduce_first(cross, [feed[0]])
+        rows = self.spread(tab, outputs + row_grads, [cross[0]])
+        own = self.reduce_near(own, [cross[0], rows[0]])
+        cross = self.reduce_near(cross, [own[0]])
         feed = self.reduce_across(feed, [cross[0]])
-        own = self.reduce_near(own, [cross[0]])
-        cross = self.reduce_first(cross, [own[0]])
-        cross = self.reduce_near(cross)
-        own = self.reduce_across(own, [cross[0]])
-        return self.spread(tab, outputs + row_grads, [own[0]]), [feed, self.reduce_across(cross), own]
+        own = self.reduce_across(own, [feed[0]])
+        return rows, [feed, self.reduce_across(cross, [own[0]]), own]
 
     def spread(self, tab, pieces, after):
         rows_held = pieces[0].shape[0]
@@ -1042,7 +1041,7 @@
         micros=10,
     )
     low_out, grad_second, gain_three = feed_result[:3]
-    core_feed = plan.reduce_core(feed_result[3:])
+    core_feed = plan.reduce_core(feed_result[3:], (), True)
     grad_first, gain_two, dq_two, dk_two, dv_two = call(
         functools.partial(cross_back_kernel, n_slots, n_pieces, rows_held),
         [(tab, "smem")]
@@ -1079,15 +1078,11 @@
         room=12,
         micros=10,
     )
-    out_pieces = plan.along_z(gate(low_out.reshape(rows_held, length, D), [core_feed[0]]))
-    second_feed = plan.reduce_second(core_feed, out_pieces[1:])
-    core_self = plan.reduce_core(self_result[1:], second_feed[:1], True, 20)
-    out_pieces = plan.whole_z(out_pieces, second_feed[:1])
     cross_grads = call(
-        functools.partial(cross_weights_kernel, n_slots, n_outs, 2),
+        functools.partial(cross_weights_kernel, n_slots, n_outs, 1),
         [(tab, "smem")]
         + vmems((grad_second, normed_two, mix_two, source_rows, dq_two, dk_two, dv_two))
-        + anys([second_feed[0], core_self[0]]),
+        + anys([self_result[1]]),
         grad_outs(0, 4 * PAIR),
         [
             VM((D, tokens), bf16),
@@ -1103,6 +1098,10 @@
         room=12,
         micros=7,
     )
+    out_pieces = plan.along_z(gate(low_out.reshape(rows_held, length, D), [core_feed[0]]))
+    second_feed = plan.reduce_second(core_feed, out_pieces[1:] + [cross_grads[0]])
+    core_self = plan.reduce_core(self_result[1:], second_feed[:1], True, 20)
+    out_pieces = plan.whole_z(out_pieces, second_feed[:1])
     (outputs, input_grad), ((grad_feed, _), (grad_cross, _), (grad_self, tile)) = plan.finish(
         tab, out_pieces, self_result[0].reshape(rows_held, length, D), second_feed, cross_grads, core_self
     )

time: 182 us -> 177 us (0.973)
  Pallas kernels: 51.6 us -> 48.4 us
  waiting for transfers between devices: 66 us -> 63.5 us
    ppermute x7, waiting for transfers between devices: 15.6 us -> 26.3 us  [hop_second(): lax.ppermute(array, ALL, self.pairs(lambda d, m: (d ^ (2 if d & 1 else 4)...]
    ppermute x21, waiting for transfers between devices: 39.2 us -> 30.5 us  [hop_z(): return lax.ppermute(array, ALL, self.pairs(lambda d, m: (d, m ^ number)))]
    ppermute x5, waiting for transfers between devices: 10.5 us -> 6.01 us  [hop_first(): lax.ppermute(array, ALL, self.pairs(lambda d, m: (d ^ (4 if d & 1 else 2)...]
    pallas_call x27 -> x30, Pallas kernels: 51.6 us -> 48.4 us  [call(): pl.pallas_call(kernel, out_shape=tuple(outs), in_specs=[pl.BlockSpec(memo...]
    unnamed x154 -> x158, local copies, waits for them, and re-layouts: 4.94 us -> 5.07 us
  transfers between devices with their start and end apart: 44 -> 44, of which waited for: 17 -> 17; matrix products, arithmetic and copies ran while one was open for 3% -> 2% of each run, Pallas kernels for 21% -> 20%
where the time goes in v4:
time: 177 us
  waiting for transfers between devices  63.5 us (36%)
  starting transfers between devices  49.4 us (28%)
  Pallas kernels  48.4 us (27%)
  other arithmetic  7.85 us (4%)
  local copies, waits for them, and re-layouts  5.73 us (3%)
  between operations  1.9 us (1%)
    pallas_call x30, Pallas kernels, call(): pl.pallas_call(kernel, out_shape=tuple(outs), in_specs=[pl.BlockSpec(memo...  48.4 us
    ppermute x21, starting transfers between devices, hop_z(): return lax.ppermute(array, ALL, self.pairs(lambda d, m: (d, m ^ number)))  33.6 us
    ppermute x21, waiting for transfers between devices, hop_z(): return lax.ppermute(array, ALL, self.pairs(lambda d, m: (d, m ^ number)))  30.5 us
    ppermute x7, waiting for transfers between devices, hop_second(): lax.ppermute(array, ALL, self.pairs(lambda d, m: (d ^ (2 if d & 1 else 4)...  26.3 us
    ppermute x5, starting transfers between devices, hop_first(): lax.ppermute(array, ALL, self.pairs(lambda d, m: (d ^ (4 if d & 1 else 2)...  7.4 us
    ppermute x7, starting transfers between devices, hop_second(): lax.ppermute(array, ALL, self.pairs(lambda d, m: (d ^ (2 if d & 1 else 4)...  6.17 us
    ppermute x5, waiting for transfers between devices, hop_first(): lax.ppermute(array, ALL, self.pairs(lambda d, m: (d ^ (4 if d & 1 else 2)...  6.01 us
    sub x7, other arithmetic, adam_step(): return (new_first, new_second, weight - rate * (ratio + decay * weight))  5.15 us
  transfers between devices with their start and end apart: 44, of which 17 were waited for; matrix products, arithmetic and copies ran while one was open for 2% of the time, Pallas kernels for 20%

profile of v4, /device:TPU:0, one launch (start us, length us, event | category | flops | bytes accessed | tf_op | source)
XLA Modules:
  0.0 176.8 jit_solution(15639286129936369857)
XLA Ops:
  3.3 4.0 %collective-permute-start = (bf16[80,1024]{1,0:T(8,128)(2,1)}, bf16[80,1024]{1,0:T(8,128)(2,1)S(1)}, u32[]{:S(2)}, u32[]{:S(2)}) collective-permute-start(bf16[80,1024]{1,0:T(8,128)(2,1)} %shard_map.434.refs_0_), channel_id=1, source_target_pairs={{0,2},{1,3},{2,0},{3,1},{4,6},{5,7},{6,4},{7,5},{8,10},{9,11},{10,... | collective-permute-start | bytes 491528 | tf_op jit(solution)/shard_map/ppermute | solution.py:719
  8.9 6.4 %collective-permute-done.refs_0_.refs_1_ = bf16[80,1024]{1,0:T(8,128)(2,1)S(1)} collective-permute-done((bf16[80,1024]{1,0:T(8,128)(2,1)}, bf16[80,1024]{1,0:T(8,128)(2,1)S(1)}, u32[]{:S(2)}, u32[]{:S(2)}) %collective-permute-start) | collective-permute-done | bytes 163872 | tf_op jit(solution)/shard_map/ppermute | solution.py:719
  16.8 3.9 %collective-permute-done.2.refs_3_ = bf16[80,1024]{1,0:T(8,128)(2,1)S(1)} collective-permute-done((bf16[80,1024]{1,0:T(8,128)(2,1)S(1)}, bf16[80,1024]{1,0:T(8,128)(2,1)S(1)}, u32[]{:S(2)}, u32[]{:S(2)}) %collective-permute-start.2) | collective-permute-done | bytes 163872 | tf_op jit(solution)/shard_map/ppermute | solution.py:719
  22.3 3.0 %collective-permute-start.3 = (bf16[64,1024]{1,0:T(8,128)(2,1)S(1)}, bf16[64,1024]{1,0:T(8,128)(2,1)S(1)}, u32[]{:S(2)}, u32[]{:S(2)}) collective-permute-start(bf16[64,1024]{1,0:T(8,128)(2,1)S(1)} %shard_map.436.refs_4_.refs_0_), channel_id=1, source_target_pairs={{0,2},{1,3},{2,0},{3,1},{4,6},{5,7},{6,4},{7,5},{8,10},{9,11},{10,... | collective-permute-start | bytes 393224 | tf_op jit(solution)/shard_map/ppermute | solution.py:719
  27.1 4.0 %collective-permute-done.3.refs_1_ = bf16[64,1024]{1,0:T(8,128)(2,1)S(1)} collective-permute-done((bf16[64,1024]{1,0:T(8,128)(2,1)S(1)}, bf16[64,1024]{1,0:T(8,128)(2,1)S(1)}, u32[]{:S(2)}, u32[]{:S(2)}) %collective-permute-start.3) | collective-permute-done | bytes 131104 | tf_op jit(solution)/shard_map/ppermute | solution.py:719
  32.3 3.7 %collective-permute-done.5.refs_3_ = bf16[64,1024]{1,0:T(8,128)(2,1)S(1)} collective-permute-done((bf16[64,1024]{1,0:T(8,128)(2,1)S(1)}, bf16[64,1024]{1,0:T(8,128)(2,1)S(1)}, u32[]{:S(2)}, u32[]{:S(2)}) %collective-permute-start.5) | collective-permute-done | bytes 131104 | tf_op jit(solution)/shard_map/ppermute | solution.py:719
  37.3 5.0 %collective-permute-done.7.refs_2_.refs_6_.refs_8_ = bf16[4,80,1024]{2,1,0:T(8,128)(2,1)S(1)} collective-permute-done((bf16[4,80,1024]{2,1,0:T(8,128)(2,1)S(1)}, bf16[4,80,1024]{2,1,0:T(8,128)(2,1)S(1)}, u32[]{:S(2)}, u32[]{:S(2)}) %collective-permute-start.7) | collective-permute-done | bytes 655392 | tf_op jit(solution)/shard_map/ppermute | solution.py:728
  42.3 7.0 %collective-permute-done.8.refs_3_.refs_7_.refs_9_ = bf16[4,80,1024]{2,1,0:T(8,128)(2,1)S(1)} collective-permute-done((bf16[4,80,1024]{2,1,0:T(8,128)(2,1)S(1)}, bf16[4,80,1024]{2,1,0:T(8,128)(2,1)S(1)}, u32[]{:S(2)}, u32[]{:S(2)}) %collective-permute-start.8) | collective-permute-done | bytes 655392 | tf_op jit(solution)/shard_map/ppermute | solution.py:728
  50.8 3.4 %collective-permute-start.13 = (bf16[2,128,512]{2,1,0:T(8,128)(2,1)S(1)}, bf16[2,128,512]{2,1,0:T(8,128)(2,1)S(1)}, u32[]{:S(2)}, u32[]{:S(2)}) collective-permute-start(bf16[2,128,512]{2,1,0:T(8,128)(2,1)S(1)} %get-tuple-element.64.refs_1_), channel_id=1, source_target_pairs={{0,2},{1,3},{2,0},{3,1},{4,6},{5,7},{6,4},{7,5},{8,10},{9,11},{10,... | collective-permute-start | bytes 786440 | tf_op jit(solution)/shard_map/ppermute | solution.py:719
  54.2 4.3 %collective-permute-done.16.refs_1_ = bf16[4,64,1024]{2,1,0:T(8,128)(2,1)S(1)} collective-permute-done((bf16[4,64,1024]{2,1,0:T(8,128)(2,1)S(1)}, bf16[4,64,1024]{2,1,0:T(8,128)(2,1)S(1)}, u32[]{:S(2)}, u32[]{:S(2)}) %collective-permute-start.16) | collective-permute-done | bytes 524320 | tf_op jit(solution)/shard_map/ppermute | solution.py:725
  59.9 3.4 %collective-permute-start.15 = (bf16[2,128,512]{2,1,0:T(8,128)(2,1)S(1)}, bf16[2,128,512]{2,1,0:T(8,128)(2,1)S(1)}, u32[]{:S(2)}, u32[]{:S(2)}) collective-permute-start(bf16[2,128,512]{2,1,0:T(8,128)(2,1)S(1)} %get-tuple-element.70), channel_id=1, source_target_pairs={{0,3},{1,2},{2,1},{3,0},{4,7},{5,6},{6,5},{7,4},{8,11},{9,10},{10,... | collective-permute-start | bytes 786440 | tf_op jit(solution)/shard_map/ppermute | solution.py:719
  65.5 5.4 %shard_map.439 = (f32[256,512]{1,0:T(8,128)}, bf16[256,512]{1,0:T(8,128)(2,1)}, bf16[4,256,128]{2,1,0:T(8,128)(2,1)}, bf16[4,256,128]{2,1,0:T(8,128)(2,1)}, bf16...) custom-call(s32[32]{0:T(128)} %stack.102.tab, ...), custom_call_target="tpu_custom_call" | custom-call | flops 34500001792 | bytes 8716416 | tf_op jit(solution)/shard_map/pallas_call | solution.py:616
  71.0 5.9 %collective-permute-done.14.refs_10_ = bf16[2,128,512]{2,1,0:T(8,128)(2,1)S(1)} collective-permute-done((bf16[2,128,512]{2,1,0:T(8,128)(2,1)S(1)}, bf16[2,128,512]{2,1,0:T(8,128)(2,1)S(1)}, u32[]{:S(2)}, u32[]{:S(2)}) %collective-permute-start.14) | collective-permute-done | bytes 262176 | tf_op jit(solution)/shard_map/ppermute | solution.py:719
  78.9 7.8 %shard_map.440 = (f32[256,512]{1,0:T(8,128)}, bf16[256,512]{1,0:T(8,128)(2,1)}, bf16[4,256,128]{2,1,0:T(8,128)(2,1)}, bf16[4,1024,128]{2,1,0:T(8,128)(2,1)}, bf1...) custom-call(s32[32]{0:T(128)} %stack.102.tab, ...), custom_call_target="tpu_custom_call" | custom-call | flops 12650000384 | bytes 12103808 | tf_op jit(solution)/shard_map/pallas_call | solution.py:616
  88.1 10.2 %shard_map.441 = (bf16[256,512]{1,0:T(8,128)(2,1)}, f32[256,512]{1,0:T(8,128)}, f32[1,512]{1,0:T(1,128)}, bf16[4,4,64,1024]{3,2,1,0:T(8,128)(2,1)}, bf16[4,4,64,1024]{3,2,1,0:T(8,128)(2,1)}) custom-call(s32[32]{0:T(128)} %stack.102.tab, f32[8,512]{1,0:T(8,128)} %get-tuple-element.67.gains, f32[256,512]{1,0:T(8,128)} %get-tuple-element.71.before, ...), custom_call_target="tpu_custom_call" | custom-call | flops 11500000256 | bytes 10766464 | tf_op jit(solution)/shard_map/pallas_call | solution.py:616
  98.9 9.1 %shard_map.443 = (f32[256,512]{1,0:T(8,128)}, f32[1,512]{1,0:T(1,128)}, bf16[4,256,128]{2,1,0:T(8,128)(2,1)}, bf16[4,1024,128]{2,1,0:T(8,128)(2,1)}, bf16[4,1024,128]{2,1,0:T(8,128)(2,1)}) custom-call(s32[32]{0:T(128)} %stack.102.tab, s32[8,128]{1,0:T(8,128)} %targets.7, s32[8,512]{1,0:T(8,128)} %sources.3, f32[8,512]{1,0:T(8,128)} %get-tuple-element.67.gains, ...), custom_call_target="tpu_custom_call" | custom-call | flops 11500000256 | bytes 11581568 | tf_op jit(solution)/shard_map/pallas_call | solution.py:616
  112.3 6.1 %shard_map.444 = (bf16[256,512]{1,0:T(8,128)(2,1)S(1)}, bf16[4,4,80,512]{3,2,1,0:T(8,128)(2,1)S(1)}, bf16[4,4,80,512]{3,2,1,0:T(8,128)(2,1)S(1)}) custom-call(s32[32]{0:T(128)S(1)} %copy-done.7, s32[8,128]{1,0:T(8,128)S(1)} %copy-done.29, bf16[128,128]{1,0:T(8,128)(2,1)S(1)} %copy-done.30, f32[8,512]{1,0:T(8,128)S(1)} %copy-done.44, ...), custom_call_target="tpu_custom_call" | custom-call | flops 11500000256 | bytes 12128384 | tf_op jit(solution)/shard_map/pallas_call | solution.py:616
  121.3 4.9 %shard_map.445 = (bf16[4,4,64,512]{3,2,1,0:T(8,128)(2,1)S(1)}, bf16[4,4,64,512]{3,2,1,0:T(8,128)(2,1)S(1)}) custom-call(s32[32]{0:T(128)S(1)} %copy-done.7, f32[256,512]{1,0:T(8,128)S(1)} %copy-done.34, bf16[256,512]{1,0:T(8,128)(2,1)S(1)} %copy-done.36, bf16[4,256,128]{2,1,0:T(8,128)(2,1)S(1)} %copy-done.37, bf16[2,512,512]{2,1,0:T(8,128)(2,1)S(1)} %copy-done.31, ...), custom_call_target="tpu_custom_call" | custom-call | flops 8049999872 | bytes 7864448 | tf_op jit(solution)/shard_map/pallas_call | solution.py:616
  129.8 4.5 %collective-permute-done.28.refs_2_.refs_0_ = bf16[2,128,512]{2,1,0:T(8,128)(2,1)S(1)} collective-permute-done((bf16[2,128,512]{2,1,0:T(8,128)(2,1)S(1)}, bf16[2,128,512]{2,1,0:T(8,128)(2,1)S(1)}, u32[]{:S(2)}, u32[]{:S(2)}) %collective-permute-start.28) | collective-permute-done | bytes 262176 | tf_op jit(solution)/shard_map/ppermute | solution.py:719
  136.9 2.1 %collective-permute-start.37 = (bf16[2,64,1024]{2,1,0:T(8,128)(2,1)S(1)}, bf16[2,64,1024]{2,1,0:T(8,128)(2,1)S(1)}, u32[]{:S(2)}, u32[]{:S(2)}) collective-permute-start(bf16[2,64,1024]{2,1,0:T(8,128)(2,1)S(1)} %get-tuple-element.137.refs_1_), channel_id=1, source_target_pairs={{0,1},{1,0},{2,3},{3,2},{4,5},{5,4},{6,7},{7,6},{8,9},{9,8},{10,11... | collective-permute-start | bytes 786440 | tf_op jit(solution)/shard_map/ppermute | solution.py:719
  138.9 6.0 %collective-permute-done.34 = bf16[2,4,80,512]{3,2,1,0:T(8,128)(2,1)S(1)} collective-permute-done((bf16[2,4,80,512]{3,2,1,0:T(8,128)(2,1)S(1)}, bf16[2,4,80,512]{3,2,1,0:T(8,128)(2,1)S(1)}, u32[]{:S(2)}, u32[]{:S(2)}) %collective-permute-start.34) | collective-permute-done | bytes 655392 | tf_op jit(solution)/shard_map/ppermute | solution.py:728
  146.5 7.6 %collective-permute-done.33 = bf16[2,4,64,512]{3,2,1,0:T(8,128)(2,1)S(1)} collective-permute-done((bf16[2,4,64,512]{3,2,1,0:T(8,128)(2,1)S(1)}, bf16[2,4,64,512]{3,2,1,0:T(8,128)(2,1)S(1)}, u32[]{:S(2)}, u32[]{:S(2)}) %collective-permute-start.33) | collective-permute-done | bytes 524320 | tf_op jit(solution)/shard_map/ppermute | solution.py:728
  156.0 3.0 %collective-permute-start.41 = (bf16[64,1024]{1,0:T(8,128)(2,1)S(1)}, bf16[64,1024]{1,0:T(8,128)(2,1)S(1)}, u32[]{:S(2)}, u32[]{:S(2)}) collective-permute-start(bf16[64,1024]{1,0:T(8,128)(2,1)S(1)} %get-tuple-element.141.refs_1_), channel_id=1, source_target_pairs={{0,2},{1,3},{2,0},{3,1},{4,6},{5,7},{6,4},{7,5},{8,10},{9,11},{10,... | collective-permute-start | bytes 393224 | tf_op jit(solution)/shard_map/ppermute | solution.py:719
  164.5 2.5 %collective-permute-start.40 = (bf16[80,512]{1,0:T(8,128)(2,1)S(1)}, bf16[80,512]{1,0:T(8,128)(2,1)S(1)}, u32[]{:S(2)}, u32[]{:S(2)}) collective-permute-start(bf16[80,512]{1,0:T(8,128)(2,1)S(1)} %get-tuple-element.145.refs_1_), channel_id=1, source_target_pairs={{0,2},{1,3},{2,0},{3,1},{4,6},{5,7},{6,4},{7,5},{8,10},{9,11},{10,... | collective-permute-start | bytes 245768 | tf_op jit(solution)/shard_map/ppermute | solution.py:719
  (283 shorter events, 51.5 us)
Async XLA Ops:
  3.3 12.1 %collective-permute-start = (bf16[80,1024]{1,0:T(8,128)(2,1)}, bf16[80,1024]{1,0:T(8,128)(2,1)S(1)}, u32[]{:S(2)}, u32[]{:S(2)}) collective-permute-start(bf16[80,1024]{1,0:T(8,128)(2,1)} %shard_map.434.refs_0_), channel_id=1, source_target_pairs={{0,2},{1,3},{2,0},{3,1},{4,6},{5,7},{6,4},{7,5},{8,10},{9,11},{10,... | collective-permute-start | bytes 491528 | tf_op jit(solution)/shard_map/ppermute | solution.py:719
  20.7 15.3 %collective-permute-start.6 = (bf16[4,80,1024]{2,1,0:T(8,128)(2,1)S(1)}, bf16[4,80,1024]{2,1,0:T(8,128)(2,1)S(1)}, u32[]{:S(2)}, u32[]{:S(2)}) collective-permute-start(bf16[4,80,1024]{2,1,0:T(8,128)(2,1)S(1)} %shard_map.437.refs_0_.refs_4_.refs_6_), channel_id=1, source_target_pairs={{0,8},{1,9},{2,10},{3,11},{4,20},{5,21},{6,22},{7,23},{8,0},{9,1},... | collective-permute-start | bytes 1966088 | tf_op jit(solution)/shard_map/ppermute | solution.py:725
  36.1 13.2 %collective-permute-start.8 = (bf16[4,80,1024]{2,1,0:T(8,128)(2,1)S(1)}, bf16[4,80,1024]{2,1,0:T(8,128)(2,1)S(1)}, u32[]{:S(2)}, u32[]{:S(2)}) collective-permute-start(bf16[4,80,1024]{2,1,0:T(8,128)(2,1)S(1)} %get-tuple-element.65.refs_1_.refs_5_.refs_7_), channel_id=1, source_target_pairs={{0,16},{1,17},{2,18},{3,19},{4,12},{5,13},{6,14},{7,15},{8,24},{9,... | collective-permute-start | bytes 1966088 | tf_op jit(solution)/shard_map/ppermute | solution.py:728
  36.8 14.0 %collective-permute-start.9 = (bf16[4,80,1024]{2,1,0:T(8,128)(2,1)S(1)}, bf16[4,80,1024]{2,1,0:T(8,128)(2,1)S(1)}, u32[]{:S(2)}, u32[]{:S(2)}) collective-permute-start(bf16[4,80,1024]{2,1,0:T(8,128)(2,1)S(1)} %shard_map.437.refs_0_.refs_4_.refs_6_), channel_id=1, source_target_pairs={{0,4},{1,5},{2,6},{3,7},{4,0},{5,1},{6,2},{7,3},{8,12},{9,13},{10,... | collective-permute-start | bytes 1966088 | tf_op jit(solution)/shard_map/ppermute | solution.py:722
  36.8 23.1 %collective-permute-start.10 = (bf16[4,80,1024]{2,1,0:T(8,128)(2,1)S(1)}, bf16[4,80,1024]{2,1,0:T(8,128)(2,1)S(1)}, u32[]{:S(2)}, u32[]{:S(2)}) collective-permute-start(bf16[4,80,1024]{2,1,0:T(8,128)(2,1)S(1)} %get-tuple-element.65.refs_1_.refs_5_.refs_7_), channel_id=1, source_target_pairs={{0,4},{1,5},{2,6},{3,7},{4,0},{5,1},{6,2},{7,3},{8,12},{9,13},{10,... | collective-permute-start | bytes 1966088 | tf_op jit(solution)/shard_map/ppermute | solution.py:722
  42.3 21.1 %collective-permute-start.11 = (bf16[4,80,1024]{2,1,0:T(8,128)(2,1)S(1)}, bf16[4,80,1024]{2,1,0:T(8,128)(2,1)S(1)}, u32[]{:S(2)}, u32[]{:S(2)}) collective-permute-start(bf16[4,80,1024]{2,1,0:T(8,128)(2,1)S(1)} %collective-permute-done.7.refs_2_.refs_6_.refs_8_), channel_id=1, source_target_pairs={{0,4},{1,5},{2,6},{3,7},{4,0},{5,1},{6,2},{7,3},{8,12},{9,13},{10,... | collective-permute-start | bytes 1966088 | tf_op jit(solution)/shard_map/ppermute | solution.py:722
  49.3 14.7 %collective-permute-start.12 = (bf16[4,80,1024]{2,1,0:T(8,128)(2,1)S(1)}, bf16[4,80,1024]{2,1,0:T(8,128)(2,1)S(1)}, u32[]{:S(2)}, u32[]{:S(2)}) collective-permute-start(bf16[4,80,1024]{2,1,0:T(8,128)(2,1)S(1)} %collective-permute-done.8.refs_3_.refs_7_.refs_9_), channel_id=1, source_target_pairs={{0,4},{1,5},{2,6},{3,7},{4,0},{5,1},{6,2},{7,3},{8,12},{9,13},{10,... | collective-permute-start | bytes 1966088 | tf_op jit(solution)/shard_map/ppermute | solution.py:722
  50.8 20.0 %collective-permute-start.13 = (bf16[2,128,512]{2,1,0:T(8,128)(2,1)S(1)}, bf16[2,128,512]{2,1,0:T(8,128)(2,1)S(1)}, u32[]{:S(2)}, u32[]{:S(2)}) collective-permute-start(bf16[2,128,512]{2,1,0:T(8,128)(2,1)S(1)} %get-tuple-element.64.refs_1_), channel_id=1, source_target_pairs={{0,2},{1,3},{2,0},{3,1},{4,6},{5,7},{6,4},{7,5},{8,10},{9,11},{10,... | collective-permute-start | bytes 786440 | tf_op jit(solution)/shard_map/ppermute | solution.py:719
  58.5 18.4 %collective-permute-start.14 = (bf16[2,128,512]{2,1,0:T(8,128)(2,1)S(1)}, bf16[2,128,512]{2,1,0:T(8,128)(2,1)S(1)}, u32[]{:S(2)}, u32[]{:S(2)}) collective-permute-start(bf16[2,128,512]{2,1,0:T(8,128)(2,1)S(1)} %get-tuple-element.69), channel_id=1, source_target_pairs={{0,1},{1,0},{2,3},{3,2},{4,5},{5,4},{6,7},{7,6},{8,9},{9,8},{10,11... | collective-permute-start | bytes 786440 | tf_op jit(solution)/shard_map/ppermute | solution.py:719
  59.9 18.3 %collective-permute-start.15 = (bf16[2,128,512]{2,1,0:T(8,128)(2,1)S(1)}, bf16[2,128,512]{2,1,0:T(8,128)(2,1)S(1)}, u32[]{:S(2)}, u32[]{:S(2)}) collective-permute-start(bf16[2,128,512]{2,1,0:T(8,128)(2,1)S(1)} %get-tuple-element.70), channel_id=1, source_target_pairs={{0,3},{1,2},{2,1},{3,0},{4,7},{5,6},{6,5},{7,4},{8,11},{9,10},{10,... | collective-permute-start | bytes 786440 | tf_op jit(solution)/shard_map/ppermute | solution.py:719
  63.4 13.6 %collective-permute-start.17 = (bf16[4,64,1024]{2,1,0:T(8,128)(2,1)S(1)}, bf16[4,64,1024]{2,1,0:T(8,128)(2,1)S(1)}, u32[]{:S(2)}, u32[]{:S(2)}) collective-permute-start(bf16[4,64,1024]{2,1,0:T(8,128)(2,1)S(1)} %get-tuple-element.66.refs_8_.refs_0_), channel_id=1, source_target_pairs={{0,16},{1,17},{2,18},{3,19},{4,12},{5,13},{6,14},{7,15},{8,24},{9,... | collective-permute-start | bytes 1572872 | tf_op jit(solution)/shard_map/ppermute | solution.py:728
  64.0 14.2 %collective-permute-start.18 = (bf16[4,64,1024]{2,1,0:T(8,128)(2,1)S(1)}, bf16[4,64,1024]{2,1,0:T(8,128)(2,1)S(1)}, u32[]{:S(2)}, u32[]{:S(2)}) collective-permute-start(bf16[4,64,1024]{2,1,0:T(8,128)(2,1)S(1)} %collective-permute-done.16.refs_1_), channel_id=1, source_target_pairs={{0,16},{1,17},{2,18},{3,19},{4,12},{5,13},{6,14},{7,15},{8,24},{9,... | collective-permute-start | bytes 1572872 | tf_op jit(solution)/shard_map/ppermute | solution.py:728
  70.9 15.8 %collective-permute-start.19 = (bf16[4,64,1024]{2,1,0:T(8,128)(2,1)}, bf16[4,64,1024]{2,1,0:T(8,128)(2,1)S(1)}, u32[]{:S(2)}, u32[]{:S(2)}) collective-permute-start(bf16[4,64,1024]{2,1,0:T(8,128)(2,1)} %copy-done.27), channel_id=1, source_target_pairs={{0,4},{1,5},{2,6},{3,7},{4,0},{5,1},{6,2},{7,3},{8,12},{9,13},{10,... | collective-permute-start | bytes 1572872 | tf_op jit(solution)/shard_map/ppermute | solution.py:722
  109.3 17.0 %collective-permute-start.24 = (bf16[2,128,512]{2,1,0:T(8,128)(2,1)S(1)}, bf16[2,128,512]{2,1,0:T(8,128)(2,1)S(1)}, u32[]{:S(2)}, u32[]{:S(2)}) collective-permute-start(bf16[2,128,512]{2,1,0:T(8,128)(2,1)S(1)} %shard_map.442.refs_0_), channel_id=1, source_target_pairs={{0,2},{1,3},{2,0},{3,1},{4,6},{5,7},{6,4},{7,5},{8,10},{9,11},{10,... | collective-permute-start | bytes 786440 | tf_op jit(solution)/shard_map/ppermute | solution.py:719
  109.3 17.0 %collective-permute-start.26 = (bf16[2,128,512]{2,1,0:T(8,128)(2,1)S(1)}, bf16[2,128,512]{2,1,0:T(8,128)(2,1)S(1)}, u32[]{:S(2)}, u32[]{:S(2)}) collective-permute-start(bf16[2,128,512]{2,1,0:T(8,128)(2,1)S(1)} %shard_map.442.refs_0_), channel_id=1, source_target_pairs={{0,1},{1,0},{2,3},{3,2},{4,5},{5,4},{6,7},{7,6},{8,9},{9,8},{10,11... | collective-permute-start | bytes 786440 | tf_op jit(solution)/shard_map/ppermute | solution.py:719
  111.2 15.6 %collective-permute-start.25 = (bf16[2,4,64,1024]{3,2,1,0:T(8,128)(2,1)S(1)}, bf16[2,4,64,1024]{3,2,1,0:T(8,128)(2,1)S(1)}, u32[]{:S(2)}, u32[]{:S(2)}) collective-permute-start(bf16[2,4,64,1024]{3,2,1,0:T(8,128)(2,1)S(1)} %get-tuple-element.127.refs_1_.refs_14_), channel_id=1, source_target_pairs={{0,16},{1,17},{2,18},{3,19},{4,12},{5,13},{6,14},{7,15},{8,24},{9,... | collective-permute-start | bytes 3145736 | tf_op jit(solution)/shard_map/ppermute | solution.py:728
  118.4 16.0 %collective-permute-start.28 = (bf16[2,128,512]{2,1,0:T(8,128)(2,1)S(1)}, bf16[2,128,512]{2,1,0:T(8,128)(2,1)S(1)}, u32[]{:S(2)}, u32[]{:S(2)}) collective-permute-start(bf16[2,128,512]{2,1,0:T(8,128)(2,1)S(1)} %bitcast.81), channel_id=1, source_target_pairs={{0,2},{1,3},{2,0},{3,1},{4,6},{5,7},{6,4},{7,5},{8,10},{9,11},{10,... | collective-permute-start | bytes 786440 | tf_op jit(solution)/shard_map/ppermute | solution.py:719
  119.3 16.3 %collective-permute-start.31 = (bf16[2,128,512]{2,1,0:T(8,128)(2,1)S(1)}, bf16[2,128,512]{2,1,0:T(8,128)(2,1)S(1)}, u32[]{:S(2)}, u32[]{:S(2)}) collective-permute-start(bf16[2,128,512]{2,1,0:T(8,128)(2,1)S(1)} %bitcast.82), channel_id=1, source_target_pairs={{0,1},{1,0},{2,3},{3,2},{4,5},{5,4},{6,7},{7,6},{8,9},{9,8},{10,11... | collective-permute-start | bytes 786440 | tf_op jit(solution)/shard_map/ppermute | solution.py:719
  129.3 17.2 %collective-permute-start.27 = (bf16[2,128,512]{2,1,0:T(8,128)(2,1)S(1)}, bf16[2,128,512]{2,1,0:T(8,128)(2,1)S(1)}, u32[]{:S(2)}, u32[]{:S(2)}) collective-permute-start(bf16[2,128,512]{2,1,0:T(8,128)(2,1)S(1)} %shard_map.447.refs_1_), channel_id=1, source_target_pairs={{0,1},{1,0},{2,3},{3,2},{4,5},{5,4},{6,7},{7,6},{8,9},{9,8},{10,11... | collective-permute-start | bytes 786440 | tf_op jit(solution)/shard_map/ppermute | solution.py:719
  135.8 18.3 %collective-permute-start.33 = (bf16[2,4,64,512]{3,2,1,0:T(8,128)(2,1)S(1)}, bf16[2,4,64,512]{3,2,1,0:T(8,128)(2,1)S(1)}, u32[]{:S(2)}, u32[]{:S(2)}) collective-permute-start(bf16[2,4,64,512]{3,2,1,0:T(8,128)(2,1)S(1)} %get-tuple-element.101.refs_1_), channel_id=1, source_target_pairs={{0,16},{1,17},{2,18},{3,19},{4,12},{5,13},{6,14},{7,15},{8,24},{9,... | collective-permute-start | bytes 1572872 | tf_op jit(solution)/shard_map/ppermute | solution.py:728
  136.7 24.2 %collective-permute-start.32 = (bf16[2,128,512]{2,1,0:T(8,128)(2,1)S(1)}, bf16[2,128,512]{2,1,0:T(8,128)(2,1)S(1)}, u32[]{:S(2)}, u32[]{:S(2)}) collective-permute-start(bf16[2,128,512]{2,1,0:T(8,128)(2,1)S(1)} %shard_map.451.refs_5_), channel_id=1, source_target_pairs={{0,1},{1,0},{2,3},{3,2},{4,5},{5,4},{6,7},{7,6},{8,9},{9,8},{10,11... | collective-permute-start | bytes 786440 | tf_op jit(solution)/shard_map/ppermute | solution.py:719
  136.9 19.0 %collective-permute-start.37 = (bf16[2,64,1024]{2,1,0:T(8,128)(2,1)S(1)}, bf16[2,64,1024]{2,1,0:T(8,128)(2,1)S(1)}, u32[]{:S(2)}, u32[]{:S(2)}) collective-permute-start(bf16[2,64,1024]{2,1,0:T(8,128)(2,1)S(1)} %get-tuple-element.137.refs_1_), channel_id=1, source_target_pairs={{0,1},{1,0},{2,3},{3,2},{4,5},{5,4},{6,7},{7,6},{8,9},{9,8},{10,11... | collective-permute-start | bytes 786440 | tf_op jit(solution)/shard_map/ppermute | solution.py:719
  145.1 10.6 %collective-permute-start.38 = (bf16[4,80,512]{2,1,0:T(8,128)(2,1)S(1)}, bf16[4,80,512]{2,1,0:T(8,128)(2,1)S(1)}, u32[]{:S(2)}, u32[]{:S(2)}) collective-permute-start(bf16[4,80,512]{2,1,0:T(8,128)(2,1)S(1)} %get-tuple-element.133.refs_1_), channel_id=1, source_target_pairs={{0,8},{1,9},{2,10},{3,11},{4,20},{5,21},{6,22},{7,23},{8,0},{9,1},... | collective-permute-start | bytes 983048 | tf_op jit(solution)/shard_map/ppermute | solution.py:725
  156.0 12.2 %collective-permute-start.41 = (bf16[64,1024]{1,0:T(8,128)(2,1)S(1)}, bf16[64,1024]{1,0:T(8,128)(2,1)S(1)}, u32[]{:S(2)}, u32[]{:S(2)}) collective-permute-start(bf16[64,1024]{1,0:T(8,128)(2,1)S(1)} %get-tuple-element.141.refs_1_), channel_id=1, source_target_pairs={{0,2},{1,3},{2,0},{3,1},{4,6},{5,7},{6,4},{7,5},{8,10},{9,11},{10,... | collective-permute-start | bytes 393224 | tf_op jit(solution)/shard_map/ppermute | solution.py:719
  (101 other events, 612.7 us)

commit v5 on v4

--- a/solution.py
+++ b/solution.py
@@ -761,8 +761,11 @@
             aliases={len(pieces): 1},
         )
 
-    def in_plane(self, base, near, far):
-        slots = [base, near, far, self.hop_second(near)]
+    def in_plane(self, base, near, far, after=()):
+        both = self.hop_second(near)
+        if after:
+            both = gate(both, after, 0)
+        slots = [base, near, far, both]
         return slots + [self.hop_core(slot) for slot in slots]
 
     def attention_shard(self, tab, query, keyval, output, gains, table):
@@ -800,10 +803,16 @@
         base = self.stack(attention, [own_feed])
         near, far = self.hop_first(base), self.hop_second(base)
         feed_base, near = self.stack_through(feed, near)
-        attention = self.in_plane(base, near, far)
         sources = [encoder] + [self.hop_z(part, j) for part, j in zip(parts, self.order[1:])]
-        feed = self.in_plane(feed_base, self.hop_first(feed_base), self.hop_second(feed_base))
+        attention = self.in_plane(base, near, far, sources[3:4])
+        near = self.hop_first(feed_base)
+        feed = [feed_base, near, self.hop_second(feed_base), self.hop_second(near)]
         return attention, feed, sources, feed_base
+
+    def feed_slots(self, feed, after):
+        base, near, far, both = feed
+        slots = [base, near, gate(far, after, 0), gate(both, after, 0)]
+        return slots + [self.hop_core(slot) for slot in slots]
 
     def reduce_core(self, parts, *how):
         own, peer = parts
@@ -887,6 +896,9 @@
         tile = jnp.concatenate((tile, jnp.zeros((PAIRS - 1,) + tile.shape[1:], bf16)))
         sources = lax.all_to_all(encoder, "mp", split_axis=0, concat_axis=1, tiled=True)
         return [jnp.concatenate((attention, tile), axis=1)], [feed], [sources], feed
+
+    def feed_slots(self, feed, after):
+        return feed
 
     def reduce_core(self, parts, *how):
         return parts
@@ -955,7 +967,7 @@
     entries = entries + [place_mp * rows_held, place_dp, place_mp] + [0] * 5
     tab = jnp.stack([jnp.asarray(entry, jnp.int32) for entry in entries])
     onehot = bucket_onehot(length)
-    attn_slots, feed_slots, pieces, feed_base = plan.weights(
+    attn_slots, feed, pieces, feed_base = plan.weights(
         tab,
         query_weight,
         keyval_weight,
@@ -1020,6 +1032,7 @@
             shape((count, PAIRS, D // n_slots + extra, width_out), bf16) for count in out_slots
         ]
 
+    feed_slots = plan.feed_slots(feed, [after_cross])
     feed_result = call(
         functools.partial(feed_kernel, n_slots, n_outs, rows_held),
         [(tab, "smem")] + vmems((gain_rows, after_cross)) + anys([cotangent] + feed_slots),

time: 177 us -> 173 us (0.977)
  waiting for transfers between devices: 63.5 us -> 60 us
    ppermute x7, waiting for transfers between devices: 26.3 us -> 17.4 us  [hop_second(): lax.ppermute(array, ALL, self.pairs(lambda d, m: (d ^ (2 if d & 1 else 4)...]
    ppermute x11, waiting for transfers between devices: 0.68 us -> 3.81 us  [hop_core(): return lax.ppermute(array, ALL, self.pairs(lambda d, m: (d ^ 1, m)))]
    pallas_call x30 -> x33, Pallas kernels: 48.4 us -> 48.5 us  [call(): pl.pallas_call(kernel, out_shape=tuple(outs), in_specs=[pl.BlockSpec(memo...]
    unnamed x158 -> x156, local copies, waits for them, and re-layouts: 5.07 us -> 4.97 us
  transfers between devices with their start and end apart: 44 -> 44, of which waited for: 17 -> 19; matrix products, arithmetic and copies ran while one was open for 2% -> 2% of each run, Pallas kernels for 20% -> 21%
where the time goes in v5:
time: 173 us
  waiting for transfers between devices  60 us (35%)
  starting transfers between devices  49.1 us (28%)
  Pallas kernels  48.5 us (28%)
  other arithmetic  7.85 us (5%)
  local copies, waits for them, and re-layouts  5.63 us (3%)
  between operations  1.89 us (1%)
    pallas_call x33, Pallas kernels, call(): pl.pallas_call(kernel, out_shape=tuple(outs), in_specs=[pl.BlockSpec(memo...  48.5 us
    ppermute x21, starting transfers between devices, hop_z(): return lax.ppermute(array, ALL, self.pairs(lambda d, m: (d, m ^ number)))  35 us
    ppermute x21, waiting for transfers between devices, hop_z(): return lax.ppermute(array, ALL, self.pairs(lambda d, m: (d, m ^ number)))  31.9 us
    ppermute x7, waiting for transfers between devices, hop_second(): lax.ppermute(array, ALL, self.pairs(lambda d, m: (d ^ (2 if d & 1 else 4)...  17.4 us
    ppermute x5, waiting for transfers between devices, hop_first(): lax.ppermute(array, ALL, self.pairs(lambda d, m: (d ^ (4 if d & 1 else 2)...  6.83 us
    ppermute x5, starting transfers between devices, hop_first(): lax.ppermute(array, ALL, self.pairs(lambda d, m: (d ^ (4 if d & 1 else 2)...  6.35 us
    ppermute x7, starting transfers between devices, hop_second(): lax.ppermute(array, ALL, self.pairs(lambda d, m: (d ^ (2 if d & 1 else 4)...  5.9 us
    sub x7, other arithmetic, adam_step(): return (new_first, new_second, weight - rate * (ratio + decay * weight))  5.15 us
  transfers between devices with their start and end apart: 44, of which 19 were waited for; matrix products, arithmetic and copies ran while one was open for 2% of the time, Pallas kernels for 21%

profile of v5, /device:TPU:0, one launch (start us, length us, event | category | flops | bytes accessed | tf_op | source)
XLA Modules:
  0.0 173.0 jit_solution(6968633051674624032)
XLA Ops:
  3.3 4.0 %collective-permute-start = (bf16[80,1024]{1,0:T(8,128)(2,1)}, bf16[80,1024]{1,0:T(8,128)(2,1)S(1)}, u32[]{:S(2)}, u32[]{:S(2)}) collective-permute-start(bf16[80,1024]{1,0:T(8,128)(2,1)} %shard_map.434.refs_0_), channel_id=1, source_target_pairs={{0,2},{1,3},{2,0},{3,1},{4,6},{5,7},{6,4},{7,5},{8,10},{9,11},{10,... | collective-permute-start | bytes 491528 | tf_op jit(solution)/shard_map/ppermute | solution.py:719
  8.9 6.4 %collective-permute-done.refs_0_.refs_1_ = bf16[80,1024]{1,0:T(8,128)(2,1)S(1)} collective-permute-done((bf16[80,1024]{1,0:T(8,128)(2,1)}, bf16[80,1024]{1,0:T(8,128)(2,1)S(1)}, u32[]{:S(2)}, u32[]{:S(2)}) %collective-permute-start) | collective-permute-done | bytes 163872 | tf_op jit(solution)/shard_map/ppermute | solution.py:719
  16.8 3.9 %collective-permute-done.2.refs_3_ = bf16[80,1024]{1,0:T(8,128)(2,1)S(1)} collective-permute-done((bf16[80,1024]{1,0:T(8,128)(2,1)S(1)}, bf16[80,1024]{1,0:T(8,128)(2,1)S(1)}, u32[]{:S(2)}, u32[]{:S(2)}) %collective-permute-start.2) | collective-permute-done | bytes 163872 | tf_op jit(solution)/shard_map/ppermute | solution.py:719
  22.3 3.0 %collective-permute-start.3 = (bf16[64,1024]{1,0:T(8,128)(2,1)S(1)}, bf16[64,1024]{1,0:T(8,128)(2,1)S(1)}, u32[]{:S(2)}, u32[]{:S(2)}) collective-permute-start(bf16[64,1024]{1,0:T(8,128)(2,1)S(1)} %shard_map.436.refs_4_.refs_0_), channel_id=1, source_target_pairs={{0,2},{1,3},{2,0},{3,1},{4,6},{5,7},{6,4},{7,5},{8,10},{9,11},{10,... | collective-permute-start | bytes 393224 | tf_op jit(solution)/shard_map/ppermute | solution.py:719
  27.1 4.0 %collective-permute-done.3.refs_1_ = bf16[64,1024]{1,0:T(8,128)(2,1)S(1)} collective-permute-done((bf16[64,1024]{1,0:T(8,128)(2,1)S(1)}, bf16[64,1024]{1,0:T(8,128)(2,1)S(1)}, u32[]{:S(2)}, u32[]{:S(2)}) %collective-permute-start.3) | collective-permute-done | bytes 131104 | tf_op jit(solution)/shard_map/ppermute | solution.py:719
  32.3 3.7 %collective-permute-done.5.refs_3_ = bf16[64,1024]{1,0:T(8,128)(2,1)S(1)} collective-permute-done((bf16[64,1024]{1,0:T(8,128)(2,1)S(1)}, bf16[64,1024]{1,0:T(8,128)(2,1)S(1)}, u32[]{:S(2)}, u32[]{:S(2)}) %collective-permute-start.5) | collective-permute-done | bytes 131104 | tf_op jit(solution)/shard_map/ppermute | solution.py:719
  36.8 3.5 %collective-permute-start.9 = (bf16[2,128,512]{2,1,0:T(8,128)(2,1)S(1)}, bf16[2,128,512]{2,1,0:T(8,128)(2,1)S(1)}, u32[]{:S(2)}, u32[]{:S(2)}) collective-permute-start(bf16[2,128,512]{2,1,0:T(8,128)(2,1)S(1)} %get-tuple-element.66), channel_id=1, source_target_pairs={{0,3},{1,2},{2,1},{3,0},{4,7},{5,6},{6,5},{7,4},{8,11},{9,10},{10,... | collective-permute-start | bytes 786440 | tf_op jit(solution)/shard_map/ppermute | solution.py:719
  42.3 4.6 %collective-permute-done.9.refs_1_.refs_11_ = bf16[2,128,512]{2,1,0:T(8,128)(2,1)S(1)} collective-permute-done((bf16[2,128,512]{2,1,0:T(8,128)(2,1)S(1)}, bf16[2,128,512]{2,1,0:T(8,128)(2,1)S(1)}, u32[]{:S(2)}, u32[]{:S(2)}) %collective-permute-start.9) | collective-permute-done | bytes 262176 | tf_op jit(solution)/shard_map/ppermute | solution.py:719
  47.0 2.4 %collective-permute-done.8.refs_0_ = bf16[4,80,1024]{2,1,0:T(8,128)(2,1)S(1)} collective-permute-done((bf16[4,80,1024]{2,1,0:T(8,128)(2,1)S(1)}, bf16[4,80,1024]{2,1,0:T(8,128)(2,1)S(1)}, u32[]{:S(2)}, u32[]{:S(2)}) %collective-permute-start.8) | collective-permute-done | bytes 655392 | tf_op jit(solution)/shard_map/ppermute | solution.py:728
  50.8 3.4 %collective-permute-start.14 = (bf16[2,128,512]{2,1,0:T(8,128)(2,1)S(1)}, bf16[2,128,512]{2,1,0:T(8,128)(2,1)S(1)}, u32[]{:S(2)}, u32[]{:S(2)}) collective-permute-start(bf16[2,128,512]{2,1,0:T(8,128)(2,1)S(1)} %get-tuple-element.64.refs_1_), channel_id=1, source_target_pairs={{0,2},{1,3},{2,0},{3,1},{4,6},{5,7},{6,4},{7,5},{8,10},{9,11},{10,... | collective-permute-start | bytes 786440 | tf_op jit(solution)/shard_map/ppermute | solution.py:719
  54.2 4.4 %collective-permute-done.16.refs_1_ = bf16[4,64,1024]{2,1,0:T(8,128)(2,1)} collective-permute-done((bf16[4,64,1024]{2,1,0:T(8,128)(2,1)S(1)}, bf16[4,64,1024]{2,1,0:T(8,128)(2,1)}, u32[]{:S(2)}, u32[]{:S(2)}) %collective-permute-start.16) | collective-permute-done | bytes 524320 | tf_op jit(solution)/shard_map/ppermute | solution.py:725
  58.6 3.0 %collective-permute-start.15 = (bf16[2,128,512]{2,1,0:T(8,128)(2,1)S(1)}, bf16[2,128,512]{2,1,0:T(8,128)(2,1)}, u32[]{:S(2)}, u32[]{:S(2)}) collective-permute-start(bf16[2,128,512]{2,1,0:T(8,128)(2,1)S(1)} %get-tuple-element.70), channel_id=1, source_target_pairs={{0,1},{1,0},{2,3},{3,2},{4,5},{5,4},{6,7},{7,6},{8,9},{9,8},{10,11... | collective-permute-start | bytes 786440 | tf_op jit(solution)/shard_map/ppermute | solution.py:719
  63.8 5.4 %shard_map.440 = (f32[256,512]{1,0:T(8,128)}, bf16[256,512]{1,0:T(8,128)(2,1)}, bf16[4,256,128]{2,1,0:T(8,128)(2,1)}, bf16[4,256,128]{2,1,0:T(8,128)(2,1)}, bf16...) custom-call(s32[32]{0:T(128)} %stack.102.tab, ...), custom_call_target="tpu_custom_call" | custom-call | flops 34500001792 | bytes 8716416 | tf_op jit(solution)/shard_map/pallas_call | solution.py:616
  69.3 2.5 %collective-permute-done.15.refs_10_ = bf16[2,128,512]{2,1,0:T(8,128)(2,1)} collective-permute-done((bf16[2,128,512]{2,1,0:T(8,128)(2,1)S(1)}, bf16[2,128,512]{2,1,0:T(8,128)(2,1)}, u32[]{:S(2)}, u32[]{:S(2)}) %collective-permute-start.15) | collective-permute-done | bytes 262176 | tf_op jit(solution)/shard_map/ppermute | solution.py:719
  71.8 7.8 %shard_map.441 = (f32[256,512]{1,0:T(8,128)}, bf16[256,512]{1,0:T(8,128)(2,1)}, bf16[4,256,128]{2,1,0:T(8,128)(2,1)}, bf16[4,1024,128]{2,1,0:T(8,128)(2,1)}, bf1...) custom-call(s32[32]{0:T(128)} %stack.102.tab, ...), custom_call_target="tpu_custom_call" | custom-call | flops 12650000384 | bytes 12103808 | tf_op jit(solution)/shard_map/pallas_call | solution.py:616
  84.3 10.3 %shard_map.444 = (bf16[256,512]{1,0:T(8,128)(2,1)}, f32[256,512]{1,0:T(8,128)}, f32[1,512]{1,0:T(1,128)}, bf16[4,4,64,1024]{3,2,1,0:T(8,128)(2,1)}, bf16[4,4,64,1024]{3,2,1,0:T(8,128)(2,1)}) custom-call(s32[32]{0:T(128)} %stack.102.tab, f32[8,512]{1,0:T(8,128)} %get-tuple-element.68.gains, f32[256,512]{1,0:T(8,128)} %get-tuple-element.71.refs_1_.before, ...), custom_call_target="tpu_custom_call" | custom-call | flops 11500000256 | bytes 10766464 | tf_op jit(solution)/shard_map/pallas_call | solution.py:616
  94.8 9.1 %shard_map.446 = (f32[256,512]{1,0:T(8,128)}, f32[1,512]{1,0:T(1,128)}, bf16[4,256,128]{2,1,0:T(8,128)(2,1)}, bf16[4,1024,128]{2,1,0:T(8,128)(2,1)}, bf16[4,1024,128]{2,1,0:T(8,128)(2,1)}) custom-call(s32[32]{0:T(128)} %stack.102.tab, s32[8,128]{1,0:T(8,128)} %targets.7, s32[8,512]{1,0:T(8,128)} %sources.3, f32[8,512]{1,0:T(8,128)} %get-tuple-element.68.gains, ...), custom_call_target="tpu_custom_call" | custom-call | flops 11500000256 | bytes 11581568 | tf_op jit(solution)/shard_map/pallas_call | solution.py:616
  108.3 6.1 %shard_map.447 = (bf16[256,512]{1,0:T(8,128)(2,1)S(1)}, bf16[4,4,80,512]{3,2,1,0:T(8,128)(2,1)S(1)}, bf16[4,4,80,512]{3,2,1,0:T(8,128)(2,1)S(1)}) custom-call(s32[32]{0:T(128)S(1)} %copy-done.13, s32[8,128]{1,0:T(8,128)S(1)} %copy-done.33, bf16[128,128]{1,0:T(8,128)(2,1)S(1)} %copy-done.34, f32[8,512]{1,0:T(8,128)S(1)} %copy-done.48, ...), custom_call_target="tpu_custom_call" | custom-call | flops 11500000256 | bytes 12128384 | tf_op jit(solution)/shard_map/pallas_call | solution.py:616
  117.8 4.9 %shard_map.448 = (bf16[4,4,64,512]{3,2,1,0:T(8,128)(2,1)S(1)}, bf16[4,4,64,512]{3,2,1,0:T(8,128)(2,1)S(1)}) custom-call(s32[32]{0:T(128)S(1)} %copy-done.13, f32[256,512]{1,0:T(8,128)S(1)} %copy-done.38, bf16[256,512]{1,0:T(8,128)(2,1)S(1)} %copy-done.40, bf16[4,256,128]{2,1,0:T(8,128)(2,1)S(1)} %copy-done.41, bf16[2,512,512]{2,1,0:T(8,128)(2,1)S(1)} %copy-done.35, ...), custom_call_target="tpu_custom_call" | custom-call | flops 8049999872 | bytes 7864448 | tf_op jit(solution)/shard_map/pallas_call | solution.py:616
  126.3 4.4 %collective-permute-done.28.refs_2_.refs_0_ = bf16[2,128,512]{2,1,0:T(8,128)(2,1)S(1)} collective-permute-done((bf16[2,128,512]{2,1,0:T(8,128)(2,1)S(1)}, bf16[2,128,512]{2,1,0:T(8,128)(2,1)S(1)}, u32[]{:S(2)}, u32[]{:S(2)}) %collective-permute-start.28) | collective-permute-done | bytes 262176 | tf_op jit(solution)/shard_map/ppermute | solution.py:719
  135.3 6.0 %collective-permute-done.34 = bf16[2,4,80,512]{3,2,1,0:T(8,128)(2,1)S(1)} collective-permute-done((bf16[2,4,80,512]{3,2,1,0:T(8,128)(2,1)S(1)}, bf16[2,4,80,512]{3,2,1,0:T(8,128)(2,1)S(1)}, u32[]{:S(2)}, u32[]{:S(2)}) %collective-permute-start.34) | collective-permute-done | bytes 655392 | tf_op jit(solution)/shard_map/ppermute | solution.py:728
  142.9 7.6 %collective-permute-done.33 = bf16[2,4,64,512]{3,2,1,0:T(8,128)(2,1)S(1)} collective-permute-done((bf16[2,4,64,512]{3,2,1,0:T(8,128)(2,1)S(1)}, bf16[2,4,64,512]{3,2,1,0:T(8,128)(2,1)S(1)}, u32[]{:S(2)}, u32[]{:S(2)}) %collective-permute-start.33) | collective-permute-done | bytes 524320 | tf_op jit(solution)/shard_map/ppermute | solution.py:728
  152.3 2.3 %collective-permute-start.41 = (bf16[64,1024]{1,0:T(8,128)(2,1)S(1)}, bf16[64,1024]{1,0:T(8,128)(2,1)S(1)}, u32[]{:S(2)}, u32[]{:S(2)}) collective-permute-start(bf16[64,1024]{1,0:T(8,128)(2,1)S(1)} %get-tuple-element.141.refs_1_), channel_id=1, source_target_pairs={{0,2},{1,3},{2,0},{3,1},{4,6},{5,7},{6,4},{7,5},{8,10},{9,11},{10,... | collective-permute-start | bytes 393224 | tf_op jit(solution)/shard_map/ppermute | solution.py:719
  154.7 2.4 %collective-permute-done.36 = bf16[4,64,512]{2,1,0:T(8,128)(2,1)S(1)} collective-permute-done((bf16[4,64,512]{2,1,0:T(8,128)(2,1)S(1)}, bf16[4,64,512]{2,1,0:T(8,128)(2,1)S(1)}, u32[]{:S(2)}, u32[]{:S(2)}) %collective-permute-start.36) | collective-permute-done | bytes 262176 | tf_op jit(solution)/shard_map/ppermute | solution.py:725
  (284 shorter events, 55.9 us)
Async XLA Ops:
  3.3 12.1 %collective-permute-start = (bf16[80,1024]{1,0:T(8,128)(2,1)}, bf16[80,1024]{1,0:T(8,128)(2,1)S(1)}, u32[]{:S(2)}, u32[]{:S(2)}) collective-permute-start(bf16[80,1024]{1,0:T(8,128)(2,1)} %shard_map.434.refs_0_), channel_id=1, source_target_pairs={{0,2},{1,3},{2,0},{3,1},{4,6},{5,7},{6,4},{7,5},{8,10},{9,11},{10,... | collective-permute-start | bytes 491528 | tf_op jit(solution)/shard_map/ppermute | solution.py:719
  20.7 15.3 %collective-permute-start.6 = (bf16[4,80,1024]{2,1,0:T(8,128)(2,1)S(1)}, bf16[4,80,1024]{2,1,0:T(8,128)(2,1)S(1)}, u32[]{:S(2)}, u32[]{:S(2)}) collective-permute-start(bf16[4,80,1024]{2,1,0:T(8,128)(2,1)S(1)} %shard_map.437.refs_0_.refs_4_.refs_6_), channel_id=1, source_target_pairs={{0,8},{1,9},{2,10},{3,11},{4,20},{5,21},{6,22},{7,23},{8,0},{9,1},... | collective-permute-start | bytes 1966088 | tf_op jit(solution)/shard_map/ppermute | solution.py:725
  31.7 10.6 %collective-permute-start.7 = (bf16[4,80,1024]{2,1,0:T(8,128)(2,1)S(1)}, bf16[4,80,1024]{2,1,0:T(8,128)(2,1)S(1)}, u32[]{:S(2)}, u32[]{:S(2)}) collective-permute-start(bf16[4,80,1024]{2,1,0:T(8,128)(2,1)S(1)} %shard_map.437.refs_0_.refs_4_.refs_6_), channel_id=1, source_target_pairs={{0,16},{1,17},{2,18},{3,19},{4,12},{5,13},{6,14},{7,15},{8,24},{9,... | collective-permute-start | bytes 1966088 | tf_op jit(solution)/shard_map/ppermute | solution.py:728
  36.1 13.2 %collective-permute-start.8 = (bf16[4,80,1024]{2,1,0:T(8,128)(2,1)S(1)}, bf16[4,80,1024]{2,1,0:T(8,128)(2,1)S(1)}, u32[]{:S(2)}, u32[]{:S(2)}) collective-permute-start(bf16[4,80,1024]{2,1,0:T(8,128)(2,1)S(1)} %get-tuple-element.65.refs_1_.refs_5_.refs_7_), channel_id=1, source_target_pairs={{0,16},{1,17},{2,18},{3,19},{4,12},{5,13},{6,14},{7,15},{8,24},{9,... | collective-permute-start | bytes 1966088 | tf_op jit(solution)/shard_map/ppermute | solution.py:728
  40.3 21.4 %collective-permute-start.11 = (bf16[4,80,1024]{2,1,0:T(8,128)(2,1)S(1)}, bf16[4,80,1024]{2,1,0:T(8,128)(2,1)S(1)}, u32[]{:S(2)}, u32[]{:S(2)}) collective-permute-start(bf16[4,80,1024]{2,1,0:T(8,128)(2,1)S(1)} %get-tuple-element.65.refs_1_.refs_5_.refs_7_), channel_id=1, source_target_pairs={{0,4},{1,5},{2,6},{3,7},{4,0},{5,1},{6,2},{7,3},{8,12},{9,13},{10,... | collective-permute-start | bytes 1966088 | tf_op jit(solution)/shard_map/ppermute | solution.py:722
  42.3 19.3 %collective-permute-start.12 = (bf16[4,80,1024]{2,1,0:T(8,128)(2,1)S(1)}, bf16[4,80,1024]{2,1,0:T(8,128)(2,1)S(1)}, u32[]{:S(2)}, u32[]{:S(2)}) collective-permute-start(bf16[4,80,1024]{2,1,0:T(8,128)(2,1)S(1)} %collective-permute-done.7.refs_2_.refs_6_.refs_8_), channel_id=1, source_target_pairs={{0,4},{1,5},{2,6},{3,7},{4,0},{5,1},{6,2},{7,3},{8,12},{9,13},{10,... | collective-permute-start | bytes 1966088 | tf_op jit(solution)/shard_map/ppermute | solution.py:722
  49.3 12.4 %collective-permute-start.13 = (bf16[4,80,1024]{2,1,0:T(8,128)(2,1)S(1)}, bf16[4,80,1024]{2,1,0:T(8,128)(2,1)S(1)}, u32[]{:S(2)}, u32[]{:S(2)}) collective-permute-start(bf16[4,80,1024]{2,1,0:T(8,128)(2,1)S(1)} %shard_map.439.refs_3_.refs_7_.refs_9_), channel_id=1, source_target_pairs={{0,4},{1,5},{2,6},{3,7},{4,0},{5,1},{6,2},{7,3},{8,12},{9,13},{10,... | collective-permute-start | bytes 1966088 | tf_op jit(solution)/shard_map/ppermute | solution.py:722
  50.8 18.4 %collective-permute-start.14 = (bf16[2,128,512]{2,1,0:T(8,128)(2,1)S(1)}, bf16[2,128,512]{2,1,0:T(8,128)(2,1)S(1)}, u32[]{:S(2)}, u32[]{:S(2)}) collective-permute-start(bf16[2,128,512]{2,1,0:T(8,128)(2,1)S(1)} %get-tuple-element.64.refs_1_), channel_id=1, source_target_pairs={{0,2},{1,3},{2,0},{3,1},{4,6},{5,7},{6,4},{7,5},{8,10},{9,11},{10,... | collective-permute-start | bytes 786440 | tf_op jit(solution)/shard_map/ppermute | solution.py:719
  58.6 13.2 %collective-permute-start.15 = (bf16[2,128,512]{2,1,0:T(8,128)(2,1)S(1)}, bf16[2,128,512]{2,1,0:T(8,128)(2,1)}, u32[]{:S(2)}, u32[]{:S(2)}) collective-permute-start(bf16[2,128,512]{2,1,0:T(8,128)(2,1)S(1)} %get-tuple-element.70), channel_id=1, source_target_pairs={{0,1},{1,0},{2,3},{3,2},{4,5},{5,4},{6,7},{7,6},{8,9},{9,8},{10,11... | collective-permute-start | bytes 786440 | tf_op jit(solution)/shard_map/ppermute | solution.py:719
  61.6 19.1 %collective-permute-start.17 = (bf16[4,64,1024]{2,1,0:T(8,128)(2,1)S(1)}, bf16[4,64,1024]{2,1,0:T(8,128)(2,1)S(1)}, u32[]{:S(2)}, u32[]{:S(2)}) collective-permute-start(bf16[4,64,1024]{2,1,0:T(8,128)(2,1)S(1)} %get-tuple-element.67.refs_8_.refs_0_), channel_id=1, source_target_pairs={{0,16},{1,17},{2,18},{3,19},{4,12},{5,13},{6,14},{7,15},{8,24},{9,... | collective-permute-start | bytes 1572872 | tf_op jit(solution)/shard_map/ppermute | solution.py:728
  61.7 19.6 %collective-permute-start.19 = (bf16[4,64,1024]{2,1,0:T(8,128)(2,1)S(1)}, bf16[4,64,1024]{2,1,0:T(8,128)(2,1)S(1)}, u32[]{:S(2)}, u32[]{:S(2)}) collective-permute-start(bf16[4,64,1024]{2,1,0:T(8,128)(2,1)S(1)} %get-tuple-element.67.refs_8_.refs_0_), channel_id=1, source_target_pairs={{0,4},{1,5},{2,6},{3,7},{4,0},{5,1},{6,2},{7,3},{8,12},{9,13},{10,... | collective-permute-start | bytes 1572872 | tf_op jit(solution)/shard_map/ppermute | solution.py:722
  61.8 17.9 %collective-permute-start.18 = (bf16[4,64,1024]{2,1,0:T(8,128)(2,1)}, bf16[4,64,1024]{2,1,0:T(8,128)(2,1)S(1)}, u32[]{:S(2)}, u32[]{:S(2)}) collective-permute-start(bf16[4,64,1024]{2,1,0:T(8,128)(2,1)} %collective-permute-done.16.refs_1_), channel_id=1, source_target_pairs={{0,16},{1,17},{2,18},{3,19},{4,12},{5,13},{6,14},{7,15},{8,24},{9,... | collective-permute-start | bytes 1572872 | tf_op jit(solution)/shard_map/ppermute | solution.py:728
  69.3 12.0 %collective-permute-start.20 = (bf16[4,64,1024]{2,1,0:T(8,128)(2,1)}, bf16[4,64,1024]{2,1,0:T(8,128)(2,1)S(1)}, u32[]{:S(2)}, u32[]{:S(2)}) collective-permute-start(bf16[4,64,1024]{2,1,0:T(8,128)(2,1)} %collective-permute-done.16.refs_1_), channel_id=1, source_target_pairs={{0,4},{1,5},{2,6},{3,7},{4,0},{5,1},{6,2},{7,3},{8,12},{9,13},{10,... | collective-permute-start | bytes 1572872 | tf_op jit(solution)/shard_map/ppermute | solution.py:722
  105.2 17.6 %collective-permute-start.24 = (bf16[2,128,512]{2,1,0:T(8,128)(2,1)S(1)}, bf16[2,128,512]{2,1,0:T(8,128)(2,1)S(1)}, u32[]{:S(2)}, u32[]{:S(2)}) collective-permute-start(bf16[2,128,512]{2,1,0:T(8,128)(2,1)S(1)} %shard_map.445.refs_0_), channel_id=1, source_target_pairs={{0,2},{1,3},{2,0},{3,1},{4,6},{5,7},{6,4},{7,5},{8,10},{9,11},{10,... | collective-permute-start | bytes 786440 | tf_op jit(solution)/shard_map/ppermute | solution.py:719
  105.2 17.6 %collective-permute-start.26 = (bf16[2,128,512]{2,1,0:T(8,128)(2,1)S(1)}, bf16[2,128,512]{2,1,0:T(8,128)(2,1)S(1)}, u32[]{:S(2)}, u32[]{:S(2)}) collective-permute-start(bf16[2,128,512]{2,1,0:T(8,128)(2,1)S(1)} %shard_map.445.refs_0_), channel_id=1, source_target_pairs={{0,1},{1,0},{2,3},{3,2},{4,5},{5,4},{6,7},{7,6},{8,9},{9,8},{10,11... | collective-permute-start | bytes 786440 | tf_op jit(solution)/shard_map/ppermute | solution.py:719
  107.4 15.9 %collective-permute-start.25 = (bf16[2,4,64,1024]{3,2,1,0:T(8,128)(2,1)S(1)}, bf16[2,4,64,1024]{3,2,1,0:T(8,128)(2,1)S(1)}, u32[]{:S(2)}, u32[]{:S(2)}) collective-permute-start(bf16[2,4,64,1024]{3,2,1,0:T(8,128)(2,1)S(1)} %get-tuple-element.127.refs_1_.refs_14_), channel_id=1, source_target_pairs={{0,16},{1,17},{2,18},{3,19},{4,12},{5,13},{6,14},{7,15},{8,24},{9,... | collective-permute-start | bytes 3145736 | tf_op jit(solution)/shard_map/ppermute | solution.py:728
  114.3 16.4 %collective-permute-start.28 = (bf16[2,128,512]{2,1,0:T(8,128)(2,1)S(1)}, bf16[2,128,512]{2,1,0:T(8,128)(2,1)S(1)}, u32[]{:S(2)}, u32[]{:S(2)}) collective-permute-start(bf16[2,128,512]{2,1,0:T(8,128)(2,1)S(1)} %bitcast.81), channel_id=1, source_target_pairs={{0,2},{1,3},{2,0},{3,1},{4,6},{5,7},{6,4},{7,5},{8,10},{9,11},{10,... | collective-permute-start | bytes 786440 | tf_op jit(solution)/shard_map/ppermute | solution.py:719
  115.8 16.0 %collective-permute-start.31 = (bf16[2,128,512]{2,1,0:T(8,128)(2,1)S(1)}, bf16[2,128,512]{2,1,0:T(8,128)(2,1)S(1)}, u32[]{:S(2)}, u32[]{:S(2)}) collective-permute-start(bf16[2,128,512]{2,1,0:T(8,128)(2,1)S(1)} %bitcast.82), channel_id=1, source_target_pairs={{0,1},{1,0},{2,3},{3,2},{4,5},{5,4},{6,7},{7,6},{8,9},{9,8},{10,11... | collective-permute-start | bytes 786440 | tf_op jit(solution)/shard_map/ppermute | solution.py:719
  125.9 17.0 %collective-permute-start.27 = (bf16[2,128,512]{2,1,0:T(8,128)(2,1)S(1)}, bf16[2,128,512]{2,1,0:T(8,128)(2,1)S(1)}, u32[]{:S(2)}, u32[]{:S(2)}) collective-permute-start(bf16[2,128,512]{2,1,0:T(8,128)(2,1)S(1)} %shard_map.450.refs_1_), channel_id=1, source_target_pairs={{0,1},{1,0},{2,3},{3,2},{4,5},{5,4},{6,7},{7,6},{8,9},{9,8},{10,11... | collective-permute-start | bytes 786440 | tf_op jit(solution)/shard_map/ppermute | solution.py:719
  130.7 10.6 %collective-permute-start.34 = (bf16[2,4,80,512]{3,2,1,0:T(8,128)(2,1)S(1)}, bf16[2,4,80,512]{3,2,1,0:T(8,128)(2,1)S(1)}, u32[]{:S(2)}, u32[]{:S(2)}) collective-permute-start(bf16[2,4,80,512]{3,2,1,0:T(8,128)(2,1)S(1)} %get-tuple-element.129.refs_1_), channel_id=1, source_target_pairs={{0,16},{1,17},{2,18},{3,19},{4,12},{5,13},{6,14},{7,15},{8,24},{9,... | collective-permute-start | bytes 1966088 | tf_op jit(solution)/shard_map/ppermute | solution.py:728
  132.0 18.4 %collective-permute-start.33 = (bf16[2,4,64,512]{3,2,1,0:T(8,128)(2,1)S(1)}, bf16[2,4,64,512]{3,2,1,0:T(8,128)(2,1)S(1)}, u32[]{:S(2)}, u32[]{:S(2)}) collective-permute-start(bf16[2,4,64,512]{3,2,1,0:T(8,128)(2,1)S(1)} %get-tuple-element.101.refs_1_), channel_id=1, source_target_pairs={{0,16},{1,17},{2,18},{3,19},{4,12},{5,13},{6,14},{7,15},{8,24},{9,... | collective-permute-start | bytes 1572872 | tf_op jit(solution)/shard_map/ppermute | solution.py:728
  133.1 24.2 %collective-permute-start.32 = (bf16[2,128,512]{2,1,0:T(8,128)(2,1)S(1)}, bf16[2,128,512]{2,1,0:T(8,128)(2,1)S(1)}, u32[]{:S(2)}, u32[]{:S(2)}) collective-permute-start(bf16[2,128,512]{2,1,0:T(8,128)(2,1)S(1)} %shard_map.454.refs_5_), channel_id=1, source_target_pairs={{0,1},{1,0},{2,3},{3,2},{4,5},{5,4},{6,7},{7,6},{8,9},{9,8},{10,11... | collective-permute-start | bytes 786440 | tf_op jit(solution)/shard_map/ppermute | solution.py:719
  133.3 19.0 %collective-permute-start.37 = (bf16[2,64,1024]{2,1,0:T(8,128)(2,1)S(1)}, bf16[2,64,1024]{2,1,0:T(8,128)(2,1)S(1)}, u32[]{:S(2)}, u32[]{:S(2)}) collective-permute-start(bf16[2,64,1024]{2,1,0:T(8,128)(2,1)S(1)} %get-tuple-element.137.refs_1_), channel_id=1, source_target_pairs={{0,1},{1,0},{2,3},{3,2},{4,5},{5,4},{6,7},{7,6},{8,9},{9,8},{10,11... | collective-permute-start | bytes 786440 | tf_op jit(solution)/shard_map/ppermute | solution.py:719
  152.3 12.1 %collective-permute-start.41 = (bf16[64,1024]{1,0:T(8,128)(2,1)S(1)}, bf16[64,1024]{1,0:T(8,128)(2,1)S(1)}, u32[]{:S(2)}, u32[]{:S(2)}) collective-permute-start(bf16[64,1024]{1,0:T(8,128)(2,1)S(1)} %get-tuple-element.141.refs_1_), channel_id=1, source_target_pairs={{0,2},{1,3},{2,0},{3,1},{4,6},{5,7},{6,4},{7,5},{8,10},{9,11},{10,... | collective-permute-start | bytes 393224 | tf_op jit(solution)/shard_map/ppermute | solution.py:719
  (100 other events, 582.6 us)

commit v6 on v5

--- a/solution.py
+++ b/solution.py
@@ -1005,7 +1005,7 @@
             pltpu.SemaphoreType.DMA,
         ],
         room=56,
-        micros=30,
+        micros=6,
     )
     after_cross, normed_two, q_two, k_two, v_two, mix_two, sum_two, source_rows = call(
         functools.partial(cross_forward_kernel, n_slots, n_pieces, rows_held),

time: 173 us -> 173 us (level)
    unnamed x156 -> x150, local copies, waits for them, and re-layouts: 4.97 us -> 4.91 us
where the time goes in v6:
time: 173 us
  waiting for transfers between devices  60.1 us (35%)
  starting transfers between devices  49.1 us (28%)
  Pallas kernels  48.4 us (28%)
  other arithmetic  7.85 us (5%)
  local copies, waits for them, and re-layouts  5.58 us (3%)
  between operations  1.85 us (1%)
    pallas_call x33, Pallas kernels, call(): pl.pallas_call(kernel, out_shape=tuple(outs), in_specs=[pl.BlockSpec(memo...  48.4 us
    ppermute x21, starting transfers between devices, hop_z(): return lax.ppermute(array, ALL, self.pairs(lambda d, m: (d, m ^ number)))  35 us
    ppermute x21, waiting for transfers between devices, hop_z(): return lax.ppermute(array, ALL, self.pairs(lambda d, m: (d, m ^ number)))  31.9 us
    ppermute x7, waiting for transfers between devices, hop_second(): lax.ppermute(array, ALL, self.pairs(lambda d, m: (d ^ (2 if d & 1 else 4)...  17.4 us
    ppermute x5, waiting for transfers between devices, hop_first(): lax.ppermute(array, ALL, self.pairs(lambda d, m: (d ^ (4 if d & 1 else 2)...  6.86 us
    ppermute x5, starting transfers between devices, hop_first(): lax.ppermute(array, ALL, self.pairs(lambda d, m: (d ^ (4 if d & 1 else 2)...  6.28 us
    ppermute x7, starting transfers between devices, hop_second(): lax.ppermute(array, ALL, self.pairs(lambda d, m: (d ^ (2 if d & 1 else 4)...  5.91 us
    sub x7, other arithmetic, adam_step(): return (new_first, new_second, weight - rate * (ratio + decay * weight))  5.14 us
  transfers between devices with their start and end apart: 44, of which 19 were waited for; matrix products, arithmetic and copies ran while one was open for 2% of the time, Pallas kernels for 21%

profile of v6, /device:TPU:0, one launch (start us, length us, event | category | flops | bytes accessed | tf_op | source)
XLA Modules:
  0.0 172.9 jit_solution(14117487261314627989)
XLA Ops:
  3.3 4.0 %collective-permute-start = (bf16[80,1024]{1,0:T(8,128)(2,1)}, bf16[80,1024]{1,0:T(8,128)(2,1)S(1)}, u32[]{:S(2)}, u32[]{:S(2)}) collective-permute-start(bf16[80,1024]{1,0:T(8,128)(2,1)} %shard_map.434.refs_0_), channel_id=1, source_target_pairs={{0,2},{1,3},{2,0},{3,1},{4,6},{5,7},{6,4},{7,5},{8,10},{9,11},{10,... | collective-permute-start | bytes 491528 | tf_op jit(solution)/shard_map/ppermute | solution.py:719
  8.9 6.4 %collective-permute-done.refs_0_.refs_1_ = bf16[80,1024]{1,0:T(8,128)(2,1)S(1)} collective-permute-done((bf16[80,1024]{1,0:T(8,128)(2,1)}, bf16[80,1024]{1,0:T(8,128)(2,1)S(1)}, u32[]{:S(2)}, u32[]{:S(2)}) %collective-permute-start) | collective-permute-done | bytes 163872 | tf_op jit(solution)/shard_map/ppermute | solution.py:719
  16.8 3.9 %collective-permute-done.2.refs_3_ = bf16[80,1024]{1,0:T(8,128)(2,1)S(1)} collective-permute-done((bf16[80,1024]{1,0:T(8,128)(2,1)S(1)}, bf16[80,1024]{1,0:T(8,128)(2,1)S(1)}, u32[]{:S(2)}, u32[]{:S(2)}) %collective-permute-start.2) | collective-permute-done | bytes 163872 | tf_op jit(solution)/shard_map/ppermute | solution.py:719
  22.3 3.0 %collective-permute-start.3 = (bf16[64,1024]{1,0:T(8,128)(2,1)S(1)}, bf16[64,1024]{1,0:T(8,128)(2,1)S(1)}, u32[]{:S(2)}, u32[]{:S(2)}) collective-permute-start(bf16[64,1024]{1,0:T(8,128)(2,1)S(1)} %shard_map.436.refs_4_.refs_0_), channel_id=1, source_target_pairs={{0,2},{1,3},{2,0},{3,1},{4,6},{5,7},{6,4},{7,5},{8,10},{9,11},{10,... | collective-permute-start | bytes 393224 | tf_op jit(solution)/shard_map/ppermute | solution.py:719
  27.1 4.0 %collective-permute-done.3.refs_1_ = bf16[64,1024]{1,0:T(8,128)(2,1)S(1)} collective-permute-done((bf16[64,1024]{1,0:T(8,128)(2,1)S(1)}, bf16[64,1024]{1,0:T(8,128)(2,1)S(1)}, u32[]{:S(2)}, u32[]{:S(2)}) %collective-permute-start.3) | collective-permute-done | bytes 131104 | tf_op jit(solution)/shard_map/ppermute | solution.py:719
  32.3 3.7 %collective-permute-done.5.refs_3_ = bf16[64,1024]{1,0:T(8,128)(2,1)S(1)} collective-permute-done((bf16[64,1024]{1,0:T(8,128)(2,1)S(1)}, bf16[64,1024]{1,0:T(8,128)(2,1)S(1)}, u32[]{:S(2)}, u32[]{:S(2)}) %collective-permute-start.5) | collective-permute-done | bytes 131104 | tf_op jit(solution)/shard_map/ppermute | solution.py:719
  36.8 3.5 %collective-permute-start.9 = (bf16[2,128,512]{2,1,0:T(8,128)(2,1)S(1)}, bf16[2,128,512]{2,1,0:T(8,128)(2,1)S(1)}, u32[]{:S(2)}, u32[]{:S(2)}) collective-permute-start(bf16[2,128,512]{2,1,0:T(8,128)(2,1)S(1)} %get-tuple-element.66), channel_id=1, source_target_pairs={{0,3},{1,2},{2,1},{3,0},{4,7},{5,6},{6,5},{7,4},{8,11},{9,10},{10,... | collective-permute-start | bytes 786440 | tf_op jit(solution)/shard_map/ppermute | solution.py:719
  42.3 4.6 %collective-permute-done.9.refs_1_.refs_11_ = bf16[2,128,512]{2,1,0:T(8,128)(2,1)S(1)} collective-permute-done((bf16[2,128,512]{2,1,0:T(8,128)(2,1)S(1)}, bf16[2,128,512]{2,1,0:T(8,128)(2,1)S(1)}, u32[]{:S(2)}, u32[]{:S(2)}) %collective-permute-start.9) | collective-permute-done | bytes 262176 | tf_op jit(solution)/shard_map/ppermute | solution.py:719
  47.0 2.4 %collective-permute-done.8.refs_0_ = bf16[4,80,1024]{2,1,0:T(8,128)(2,1)S(1)} collective-permute-done((bf16[4,80,1024]{2,1,0:T(8,128)(2,1)S(1)}, bf16[4,80,1024]{2,1,0:T(8,128)(2,1)S(1)}, u32[]{:S(2)}, u32[]{:S(2)}) %collective-permute-start.8) | collective-permute-done | bytes 655392 | tf_op jit(solution)/shard_map/ppermute | solution.py:728
  50.8 3.4 %collective-permute-start.14 = (bf16[2,128,512]{2,1,0:T(8,128)(2,1)S(1)}, bf16[2,128,512]{2,1,0:T(8,128)(2,1)}, u32[]{:S(2)}, u32[]{:S(2)}) collective-permute-start(bf16[2,128,512]{2,1,0:T(8,128)(2,1)S(1)} %get-tuple-element.64.refs_1_), channel_id=1, source_target_pairs={{0,2},{1,3},{2,0},{3,1},{4,6},{5,7},{6,4},{7,5},{8,10},{9,11},{10,... | collective-permute-start | bytes 786440 | tf_op jit(solution)/shard_map/ppermute | solution.py:719
  54.2 4.4 %collective-permute-done.16.refs_1_ = bf16[4,64,1024]{2,1,0:T(8,128)(2,1)} collective-permute-done((bf16[4,64,1024]{2,1,0:T(8,128)(2,1)S(1)}, bf16[4,64,1024]{2,1,0:T(8,128)(2,1)}, u32[]{:S(2)}, u32[]{:S(2)}) %collective-permute-start.16) | collective-permute-done | bytes 524320 | tf_op jit(solution)/shard_map/ppermute | solution.py:725
  58.6 3.0 %collective-permute-start.15 = (bf16[2,128,512]{2,1,0:T(8,128)(2,1)S(1)}, bf16[2,128,512]{2,1,0:T(8,128)(2,1)}, u32[]{:S(2)}, u32[]{:S(2)}) collective-permute-start(bf16[2,128,512]{2,1,0:T(8,128)(2,1)S(1)} %get-tuple-element.70), channel_id=1, source_target_pairs={{0,1},{1,0},{2,3},{3,2},{4,5},{5,4},{6,7},{7,6},{8,9},{9,8},{10,11... | collective-permute-start | bytes 786440 | tf_op jit(solution)/shard_map/ppermute | solution.py:719
  63.8 5.4 %shard_map.440 = (f32[256,512]{1,0:T(8,128)}, bf16[256,512]{1,0:T(8,128)(2,1)}, bf16[4,256,128]{2,1,0:T(8,128)(2,1)}, bf16[4,256,128]{2,1,0:T(8,128)(2,1)}, bf16...) custom-call(s32[32]{0:T(128)} %stack.102.tab, ...), custom_call_target="tpu_custom_call" | custom-call | flops 6899999744 | bytes 8716416 | tf_op jit(solution)/shard_map/pallas_call | solution.py:616
  69.3 2.5 %collective-permute-done.15.refs_10_ = bf16[2,128,512]{2,1,0:T(8,128)(2,1)} collective-permute-done((bf16[2,128,512]{2,1,0:T(8,128)(2,1)S(1)}, bf16[2,128,512]{2,1,0:T(8,128)(2,1)}, u32[]{:S(2)}, u32[]{:S(2)}) %collective-permute-start.15) | collective-permute-done | bytes 262176 | tf_op jit(solution)/shard_map/ppermute | solution.py:719
  71.8 7.8 %shard_map.441 = (f32[256,512]{1,0:T(8,128)}, bf16[256,512]{1,0:T(8,128)(2,1)}, bf16[4,256,128]{2,1,0:T(8,128)(2,1)}, bf16[4,1024,128]{2,1,0:T(8,128)(2,1)}, bf1...) custom-call(s32[32]{0:T(128)} %stack.102.tab, ...), custom_call_target="tpu_custom_call" | custom-call | flops 12650000384 | bytes 12103808 | tf_op jit(solution)/shard_map/pallas_call | solution.py:616
  84.3 10.3 %shard_map.444 = (bf16[256,512]{1,0:T(8,128)(2,1)}, f32[256,512]{1,0:T(8,128)}, f32[1,512]{1,0:T(1,128)}, bf16[4,4,64,1024]{3,2,1,0:T(8,128)(2,1)}, bf16[4,4,64,1024]{3,2,1,0:T(8,128)(2,1)}) custom-call(s32[32]{0:T(128)} %stack.102.tab, f32[8,512]{1,0:T(8,128)} %get-tuple-element.68.gains, f32[256,512]{1,0:T(8,128)} %get-tuple-element.71.refs_1_.before, ...), custom_call_target="tpu_custom_call" | custom-call | flops 11500000256 | bytes 10766464 | tf_op jit(solution)/shard_map/pallas_call | solution.py:616
  94.7 9.1 %shard_map.446 = (f32[256,512]{1,0:T(8,128)}, f32[1,512]{1,0:T(1,128)}, bf16[4,256,128]{2,1,0:T(8,128)(2,1)}, bf16[4,1024,128]{2,1,0:T(8,128)(2,1)}, bf16[4,1024,128]{2,1,0:T(8,128)(2,1)}) custom-call(s32[32]{0:T(128)} %stack.102.tab, s32[8,128]{1,0:T(8,128)} %targets.7, s32[8,512]{1,0:T(8,128)} %sources.3, f32[8,512]{1,0:T(8,128)} %get-tuple-element.68.gains, ...), custom_call_target="tpu_custom_call" | custom-call | flops 11500000256 | bytes 11581568 | tf_op jit(solution)/shard_map/pallas_call | solution.py:616
  108.2 6.0 %shard_map.447 = (bf16[256,512]{1,0:T(8,128)(2,1)S(1)}, bf16[4,4,80,512]{3,2,1,0:T(8,128)(2,1)S(1)}, bf16[4,4,80,512]{3,2,1,0:T(8,128)(2,1)S(1)}) custom-call(s32[32]{0:T(128)S(1)} %copy-done.11, s32[8,128]{1,0:T(8,128)S(1)} %copy-done.31, bf16[128,128]{1,0:T(8,128)(2,1)S(1)} %copy-done.32, f32[8,512]{1,0:T(8,128)S(1)} %copy-done.46, ...), custom_call_target="tpu_custom_call" | custom-call | flops 11500000256 | bytes 12128384 | tf_op jit(solution)/shard_map/pallas_call | solution.py:616
  117.9 4.9 %shard_map.448 = (bf16[4,4,64,512]{3,2,1,0:T(8,128)(2,1)S(1)}, bf16[4,4,64,512]{3,2,1,0:T(8,128)(2,1)S(1)}) custom-call(s32[32]{0:T(128)S(1)} %copy-done.11, f32[256,512]{1,0:T(8,128)S(1)} %copy-done.36, bf16[256,512]{1,0:T(8,128)(2,1)S(1)} %copy-done.43, bf16[4,256,128]{2,1,0:T(8,128)(2,1)S(1)} %copy-done.44, bf16[2,512,512]{2,1,0:T(8,128)(2,1)S(1)} %copy-done.33, ...), custom_call_target="tpu_custom_call" | custom-call | flops 8049999872 | bytes 7864448 | tf_op jit(solution)/shard_map/pallas_call | solution.py:616
  126.4 4.3 %collective-permute-done.28.refs_2_.refs_0_ = bf16[2,128,512]{2,1,0:T(8,128)(2,1)S(1)} collective-permute-done((bf16[2,128,512]{2,1,0:T(8,128)(2,1)S(1)}, bf16[2,128,512]{2,1,0:T(8,128)(2,1)S(1)}, u32[]{:S(2)}, u32[]{:S(2)}) %collective-permute-start.28) | collective-permute-done | bytes 262176 | tf_op jit(solution)/shard_map/ppermute | solution.py:719
  135.3 6.0 %collective-permute-done.34 = bf16[2,4,80,512]{3,2,1,0:T(8,128)(2,1)S(1)} collective-permute-done((bf16[2,4,80,512]{3,2,1,0:T(8,128)(2,1)S(1)}, bf16[2,4,80,512]{3,2,1,0:T(8,128)(2,1)S(1)}, u32[]{:S(2)}, u32[]{:S(2)}) %collective-permute-start.34) | collective-permute-done | bytes 655392 | tf_op jit(solution)/shard_map/ppermute | solution.py:728
  142.9 7.6 %collective-permute-done.33 = bf16[2,4,64,512]{3,2,1,0:T(8,128)(2,1)S(1)} collective-permute-done((bf16[2,4,64,512]{3,2,1,0:T(8,128)(2,1)S(1)}, bf16[2,4,64,512]{3,2,1,0:T(8,128)(2,1)S(1)}, u32[]{:S(2)}, u32[]{:S(2)}) %collective-permute-start.33) | collective-permute-done | bytes 524320 | tf_op jit(solution)/shard_map/ppermute | solution.py:728
  152.3 2.3 %collective-permute-start.41 = (bf16[64,1024]{1,0:T(8,128)(2,1)S(1)}, bf16[64,1024]{1,0:T(8,128)(2,1)S(1)}, u32[]{:S(2)}, u32[]{:S(2)}) collective-permute-start(bf16[64,1024]{1,0:T(8,128)(2,1)S(1)} %get-tuple-element.141.refs_1_), channel_id=1, source_target_pairs={{0,2},{1,3},{2,0},{3,1},{4,6},{5,7},{6,4},{7,5},{8,10},{9,11},{10,... | collective-permute-start | bytes 393224 | tf_op jit(solution)/shard_map/ppermute | solution.py:719
  154.6 2.4 %collective-permute-done.36 = bf16[4,64,512]{2,1,0:T(8,128)(2,1)S(1)} collective-permute-done((bf16[4,64,512]{2,1,0:T(8,128)(2,1)S(1)}, bf16[4,64,512]{2,1,0:T(8,128)(2,1)S(1)}, u32[]{:S(2)}, u32[]{:S(2)}) %collective-permute-start.36) | collective-permute-done | bytes 262176 | tf_op jit(solution)/shard_map/ppermute | solution.py:725
  (278 shorter events, 56.1 us)
Async XLA Ops:
  3.3 12.1 %collective-permute-start = (bf16[80,1024]{1,0:T(8,128)(2,1)}, bf16[80,1024]{1,0:T(8,128)(2,1)S(1)}, u32[]{:S(2)}, u32[]{:S(2)}) collective-permute-start(bf16[80,1024]{1,0:T(8,128)(2,1)} %shard_map.434.refs_0_), channel_id=1, source_target_pairs={{0,2},{1,3},{2,0},{3,1},{4,6},{5,7},{6,4},{7,5},{8,10},{9,11},{10,... | collective-permute-start | bytes 491528 | tf_op jit(solution)/shard_map/ppermute | solution.py:719
  20.7 15.3 %collective-permute-start.6 = (bf16[4,80,1024]{2,1,0:T(8,128)(2,1)S(1)}, bf16[4,80,1024]{2,1,0:T(8,128)(2,1)S(1)}, u32[]{:S(2)}, u32[]{:S(2)}) collective-permute-start(bf16[4,80,1024]{2,1,0:T(8,128)(2,1)S(1)} %shard_map.437.refs_0_.refs_4_.refs_6_), channel_id=1, source_target_pairs={{0,8},{1,9},{2,10},{3,11},{4,20},{5,21},{6,22},{7,23},{8,0},{9,1},... | collective-permute-start | bytes 1966088 | tf_op jit(solution)/shard_map/ppermute | solution.py:725
  31.7 10.6 %collective-permute-start.7 = (bf16[4,80,1024]{2,1,0:T(8,128)(2,1)S(1)}, bf16[4,80,1024]{2,1,0:T(8,128)(2,1)S(1)}, u32[]{:S(2)}, u32[]{:S(2)}) collective-permute-start(bf16[4,80,1024]{2,1,0:T(8,128)(2,1)S(1)} %shard_map.437.refs_0_.refs_4_.refs_6_), channel_id=1, source_target_pairs={{0,16},{1,17},{2,18},{3,19},{4,12},{5,13},{6,14},{7,15},{8,24},{9,... | collective-permute-start | bytes 1966088 | tf_op jit(solution)/shard_map/ppermute | solution.py:728
  36.1 13.2 %collective-permute-start.8 = (bf16[4,80,1024]{2,1,0:T(8,128)(2,1)S(1)}, bf16[4,80,1024]{2,1,0:T(8,128)(2,1)S(1)}, u32[]{:S(2)}, u32[]{:S(2)}) collective-permute-start(bf16[4,80,1024]{2,1,0:T(8,128)(2,1)S(1)} %get-tuple-element.65.refs_1_.refs_5_.refs_7_), channel_id=1, source_target_pairs={{0,16},{1,17},{2,18},{3,19},{4,12},{5,13},{6,14},{7,15},{8,24},{9,... | collective-permute-start | bytes 1966088 | tf_op jit(solution)/shard_map/ppermute | solution.py:728
  40.3 21.4 %collective-permute-start.11 = (bf16[4,80,1024]{2,1,0:T(8,128)(2,1)S(1)}, bf16[4,80,1024]{2,1,0:T(8,128)(2,1)S(1)}, u32[]{:S(2)}, u32[]{:S(2)}) collective-permute-start(bf16[4,80,1024]{2,1,0:T(8,128)(2,1)S(1)} %get-tuple-element.65.refs_1_.refs_5_.refs_7_), channel_id=1, source_target_pairs={{0,4},{1,5},{2,6},{3,7},{4,0},{5,1},{6,2},{7,3},{8,12},{9,13},{10,... | collective-permute-start | bytes 1966088 | tf_op jit(solution)/shard_map/ppermute | solution.py:722
  42.3 19.3 %collective-permute-start.12 = (bf16[4,80,1024]{2,1,0:T(8,128)(2,1)S(1)}, bf16[4,80,1024]{2,1,0:T(8,128)(2,1)S(1)}, u32[]{:S(2)}, u32[]{:S(2)}) collective-permute-start(bf16[4,80,1024]{2,1,0:T(8,128)(2,1)S(1)} %collective-permute-done.7.refs_2_.refs_6_.refs_8_), channel_id=1, source_target_pairs={{0,4},{1,5},{2,6},{3,7},{4,0},{5,1},{6,2},{7,3},{8,12},{9,13},{10,... | collective-permute-start | bytes 1966088 | tf_op jit(solution)/shard_map/ppermute | solution.py:722
  49.3 12.4 %collective-permute-start.13 = (bf16[4,80,1024]{2,1,0:T(8,128)(2,1)S(1)}, bf16[4,80,1024]{2,1,0:T(8,128)(2,1)S(1)}, u32[]{:S(2)}, u32[]{:S(2)}) collective-permute-start(bf16[4,80,1024]{2,1,0:T(8,128)(2,1)S(1)} %shard_map.439.refs_3_.refs_7_.refs_9_), channel_id=1, source_target_pairs={{0,4},{1,5},{2,6},{3,7},{4,0},{5,1},{6,2},{7,3},{8,12},{9,13},{10,... | collective-permute-start | bytes 1966088 | tf_op jit(solution)/shard_map/ppermute | solution.py:722
  50.8 18.4 %collective-permute-start.14 = (bf16[2,128,512]{2,1,0:T(8,128)(2,1)S(1)}, bf16[2,128,512]{2,1,0:T(8,128)(2,1)}, u32[]{:S(2)}, u32[]{:S(2)}) collective-permute-start(bf16[2,128,512]{2,1,0:T(8,128)(2,1)S(1)} %get-tuple-element.64.refs_1_), channel_id=1, source_target_pairs={{0,2},{1,3},{2,0},{3,1},{4,6},{5,7},{6,4},{7,5},{8,10},{9,11},{10,... | collective-permute-start | bytes 786440 | tf_op jit(solution)/shard_map/ppermute | solution.py:719
  58.6 13.2 %collective-permute-start.15 = (bf16[2,128,512]{2,1,0:T(8,128)(2,1)S(1)}, bf16[2,128,512]{2,1,0:T(8,128)(2,1)}, u32[]{:S(2)}, u32[]{:S(2)}) collective-permute-start(bf16[2,128,512]{2,1,0:T(8,128)(2,1)S(1)} %get-tuple-element.70), channel_id=1, source_target_pairs={{0,1},{1,0},{2,3},{3,2},{4,5},{5,4},{6,7},{7,6},{8,9},{9,8},{10,11... | collective-permute-start | bytes 786440 | tf_op jit(solution)/shard_map/ppermute | solution.py:719
  61.6 19.1 %collective-permute-start.17 = (bf16[4,64,1024]{2,1,0:T(8,128)(2,1)S(1)}, bf16[4,64,1024]{2,1,0:T(8,128)(2,1)S(1)}, u32[]{:S(2)}, u32[]{:S(2)}) collective-permute-start(bf16[4,64,1024]{2,1,0:T(8,128)(2,1)S(1)} %get-tuple-element.67.refs_8_.refs_0_), channel_id=1, source_target_pairs={{0,16},{1,17},{2,18},{3,19},{4,12},{5,13},{6,14},{7,15},{8,24},{9,... | collective-permute-start | bytes 1572872 | tf_op jit(solution)/shard_map/ppermute | solution.py:728
  61.7 19.6 %collective-permute-start.19 = (bf16[4,64,1024]{2,1,0:T(8,128)(2,1)S(1)}, bf16[4,64,1024]{2,1,0:T(8,128)(2,1)S(1)}, u32[]{:S(2)}, u32[]{:S(2)}) collective-permute-start(bf16[4,64,1024]{2,1,0:T(8,128)(2,1)S(1)} %get-tuple-element.67.refs_8_.refs_0_), channel_id=1, source_target_pairs={{0,4},{1,5},{2,6},{3,7},{4,0},{5,1},{6,2},{7,3},{8,12},{9,13},{10,... | collective-permute-start | bytes 1572872 | tf_op jit(solution)/shard_map/ppermute | solution.py:722
  61.8 17.9 %collective-permute-start.18 = (bf16[4,64,1024]{2,1,0:T(8,128)(2,1)}, bf16[4,64,1024]{2,1,0:T(8,128)(2,1)S(1)}, u32[]{:S(2)}, u32[]{:S(2)}) collective-permute-start(bf16[4,64,1024]{2,1,0:T(8,128)(2,1)} %collective-permute-done.16.refs_1_), channel_id=1, source_target_pairs={{0,16},{1,17},{2,18},{3,19},{4,12},{5,13},{6,14},{7,15},{8,24},{9,... | collective-permute-start | bytes 1572872 | tf_op jit(solution)/shard_map/ppermute | solution.py:728
  69.2 12.0 %collective-permute-start.20 = (bf16[4,64,1024]{2,1,0:T(8,128)(2,1)}, bf16[4,64,1024]{2,1,0:T(8,128)(2,1)S(1)}, u32[]{:S(2)}, u32[]{:S(2)}) collective-permute-start(bf16[4,64,1024]{2,1,0:T(8,128)(2,1)} %collective-permute-done.16.refs_1_), channel_id=1, source_target_pairs={{0,4},{1,5},{2,6},{3,7},{4,0},{5,1},{6,2},{7,3},{8,12},{9,13},{10,... | collective-permute-start | bytes 1572872 | tf_op jit(solution)/shard_map/ppermute | solution.py:722
  105.1 17.7 %collective-permute-start.24 = (bf16[2,128,512]{2,1,0:T(8,128)(2,1)S(1)}, bf16[2,128,512]{2,1,0:T(8,128)(2,1)S(1)}, u32[]{:S(2)}, u32[]{:S(2)}) collective-permute-start(bf16[2,128,512]{2,1,0:T(8,128)(2,1)S(1)} %shard_map.445.refs_0_), channel_id=1, source_target_pairs={{0,2},{1,3},{2,0},{3,1},{4,6},{5,7},{6,4},{7,5},{8,10},{9,11},{10,... | collective-permute-start | bytes 786440 | tf_op jit(solution)/shard_map/ppermute | solution.py:719
  105.2 17.7 %collective-permute-start.26 = (bf16[2,128,512]{2,1,0:T(8,128)(2,1)S(1)}, bf16[2,128,512]{2,1,0:T(8,128)(2,1)S(1)}, u32[]{:S(2)}, u32[]{:S(2)}) collective-permute-start(bf16[2,128,512]{2,1,0:T(8,128)(2,1)S(1)} %shard_map.445.refs_0_), channel_id=1, source_target_pairs={{0,1},{1,0},{2,3},{3,2},{4,5},{5,4},{6,7},{7,6},{8,9},{9,8},{10,11... | collective-permute-start | bytes 786440 | tf_op jit(solution)/shard_map/ppermute | solution.py:719
  107.4 16.0 %collective-permute-start.25 = (bf16[2,4,64,1024]{3,2,1,0:T(8,128)(2,1)S(1)}, bf16[2,4,64,1024]{3,2,1,0:T(8,128)(2,1)S(1)}, u32[]{:S(2)}, u32[]{:S(2)}) collective-permute-start(bf16[2,4,64,1024]{3,2,1,0:T(8,128)(2,1)S(1)} %get-tuple-element.127.refs_1_.refs_14_), channel_id=1, source_target_pairs={{0,16},{1,17},{2,18},{3,19},{4,12},{5,13},{6,14},{7,15},{8,24},{9,... | collective-permute-start | bytes 3145736 | tf_op jit(solution)/shard_map/ppermute | solution.py:728
  114.3 16.4 %collective-permute-start.28 = (bf16[2,128,512]{2,1,0:T(8,128)(2,1)S(1)}, bf16[2,128,512]{2,1,0:T(8,128)(2,1)S(1)}, u32[]{:S(2)}, u32[]{:S(2)}) collective-permute-start(bf16[2,128,512]{2,1,0:T(8,128)(2,1)S(1)} %bitcast.81), channel_id=1, source_target_pairs={{0,2},{1,3},{2,0},{3,1},{4,6},{5,7},{6,4},{7,5},{8,10},{9,11},{10,... | collective-permute-start | bytes 786440 | tf_op jit(solution)/shard_map/ppermute | solution.py:719
  115.8 16.0 %collective-permute-start.31 = (bf16[2,128,512]{2,1,0:T(8,128)(2,1)S(1)}, bf16[2,128,512]{2,1,0:T(8,128)(2,1)S(1)}, u32[]{:S(2)}, u32[]{:S(2)}) collective-permute-start(bf16[2,128,512]{2,1,0:T(8,128)(2,1)S(1)} %bitcast.82), channel_id=1, source_target_pairs={{0,1},{1,0},{2,3},{3,2},{4,5},{5,4},{6,7},{7,6},{8,9},{9,8},{10,11... | collective-permute-start | bytes 786440 | tf_op jit(solution)/shard_map/ppermute | solution.py:719
  125.9 17.0 %collective-permute-start.27 = (bf16[2,128,512]{2,1,0:T(8,128)(2,1)S(1)}, bf16[2,128,512]{2,1,0:T(8,128)(2,1)S(1)}, u32[]{:S(2)}, u32[]{:S(2)}) collective-permute-start(bf16[2,128,512]{2,1,0:T(8,128)(2,1)S(1)} %shard_map.450.refs_1_), channel_id=1, source_target_pairs={{0,1},{1,0},{2,3},{3,2},{4,5},{5,4},{6,7},{7,6},{8,9},{9,8},{10,11... | collective-permute-start | bytes 786440 | tf_op jit(solution)/shard_map/ppermute | solution.py:719
  130.7 10.6 %collective-permute-start.34 = (bf16[2,4,80,512]{3,2,1,0:T(8,128)(2,1)S(1)}, bf16[2,4,80,512]{3,2,1,0:T(8,128)(2,1)S(1)}, u32[]{:S(2)}, u32[]{:S(2)}) collective-permute-start(bf16[2,4,80,512]{3,2,1,0:T(8,128)(2,1)S(1)} %get-tuple-element.129.refs_1_), channel_id=1, source_target_pairs={{0,16},{1,17},{2,18},{3,19},{4,12},{5,13},{6,14},{7,15},{8,24},{9,... | collective-permute-start | bytes 1966088 | tf_op jit(solution)/shard_map/ppermute | solution.py:728
  132.1 18.3 %collective-permute-start.33 = (bf16[2,4,64,512]{3,2,1,0:T(8,128)(2,1)S(1)}, bf16[2,4,64,512]{3,2,1,0:T(8,128)(2,1)S(1)}, u32[]{:S(2)}, u32[]{:S(2)}) collective-permute-start(bf16[2,4,64,512]{3,2,1,0:T(8,128)(2,1)S(1)} %get-tuple-element.101.refs_1_), channel_id=1, source_target_pairs={{0,16},{1,17},{2,18},{3,19},{4,12},{5,13},{6,14},{7,15},{8,24},{9,... | collective-permute-start | bytes 1572872 | tf_op jit(solution)/shard_map/ppermute | solution.py:728
  133.0 24.2 %collective-permute-start.32 = (bf16[2,128,512]{2,1,0:T(8,128)(2,1)S(1)}, bf16[2,128,512]{2,1,0:T(8,128)(2,1)S(1)}, u32[]{:S(2)}, u32[]{:S(2)}) collective-permute-start(bf16[2,128,512]{2,1,0:T(8,128)(2,1)S(1)} %shard_map.454.refs_5_), channel_id=1, source_target_pairs={{0,1},{1,0},{2,3},{3,2},{4,5},{5,4},{6,7},{7,6},{8,9},{9,8},{10,11... | collective-permute-start | bytes 786440 | tf_op jit(solution)/shard_map/ppermute | solution.py:719
  133.2 18.9 %collective-permute-start.37 = (bf16[2,64,1024]{2,1,0:T(8,128)(2,1)S(1)}, bf16[2,64,1024]{2,1,0:T(8,128)(2,1)S(1)}, u32[]{:S(2)}, u32[]{:S(2)}) collective-permute-start(bf16[2,64,1024]{2,1,0:T(8,128)(2,1)S(1)} %get-tuple-element.137.refs_1_), channel_id=1, source_target_pairs={{0,1},{1,0},{2,3},{3,2},{4,5},{5,4},{6,7},{7,6},{8,9},{9,8},{10,11... | collective-permute-start | bytes 786440 | tf_op jit(solution)/shard_map/ppermute | solution.py:719
  152.3 12.1 %collective-permute-start.41 = (bf16[64,1024]{1,0:T(8,128)(2,1)S(1)}, bf16[64,1024]{1,0:T(8,128)(2,1)S(1)}, u32[]{:S(2)}, u32[]{:S(2)}) collective-permute-start(bf16[64,1024]{1,0:T(8,128)(2,1)S(1)} %get-tuple-element.141.refs_1_), channel_id=1, source_target_pairs={{0,2},{1,3},{2,0},{3,1},{4,6},{5,7},{6,4},{7,5},{8,10},{9,11},{10,... | collective-permute-start | bytes 393224 | tf_op jit(solution)/shard_map/ppermute | solution.py:719
  (97 other events, 576.8 us)
